TPU v7x, 32 devices: a whole 2x2x4 slice. The times are simulated.
32 devices in a mesh: rep: 2 (over y), wide: 8 (over z, x), tensor: 2 (over core).
Axes of the slice: x: 2, y: 2, z: 4, core: 2. Of those that a mesh axis runs over, the one named last changes fastest.
Arguments:
- tokens: bfloat16 [128, 8192], P(('rep', 'wide')), parts along dimension 0, may hold values from -6 to 6
- query_quant_codes: int32 [8192, 8192], P(None, ('tensor', 'wide')), may hold values from 0 to 15
- query_absmax_scale: float32 [128, 8192], P(None, ('tensor', 'wide')), may hold values from 0.012153398 to 0.039774757
- output_quant_codes: int32 [8192, 8192], P('tensor', 'wide'), may hold values from 0 to 15
- output_absmax_scale: float32 [128, 8192], P('tensor', 'wide'), may hold values from 0.03314563 to 0.13258252
- adapter_down_maps: bfloat16 [8192, 48, 32], P(None, 'wide'), may hold values from -0.0625 to 0.0625
- adapter_up_maps: bfloat16 [48, 32, 8192], P('wide', None, 'tensor'), may hold values from -1 to 1
- row_adapter_index: int32 [128], P('rep'), parts along dimension 0, may hold values from 0 to 47
- adapter_storage_slot: int32 [48], replicated, may hold values from 0 to 47, each once
- row_cache_length: int32 [128], P(('rep', 'wide')), parts along dimension 0, may hold values from 2 to 64
- stored_key_cache: bfloat16 [128, 64, 1024], P(('rep', 'wide'), None, 'tensor'), parts along dimension 0, may hold values from -201 to 201
- stored_value_cache: bfloat16 [128, 64, 1024], P(('rep', 'wide'), None, 'tensor'), parts along dimension 0, may hold values from -6 to 6
- fresh_token_key: bfloat16 [128, 1024], P(('rep', 'wide'), 'tensor'), parts along dimension 0, may hold values from -6 to 6
- fresh_token_value: bfloat16 [128, 1024], P(('rep', 'wide'), 'tensor'), parts along dimension 0, may hold values from -6 to 6
Outputs:
- attention_out: bfloat16 [128, 8192], P(('rep', 'wide')), parts along dimension 0
There are 2 independent parts, one for each index of `rep`. A program takes and returns all parts, laid end to end along the dimension named above; an argument that names none is the same for every part. Nothing has to cross between parts.
Inputs may be any that keep to these rules, and one draw needn't show every extreme that they name: `row_adapter_index`: adapter of each row; a few adapters serve many rows. `adapter_storage_slot`: each adapter's storage slot, each slot used once; slot s lies on index s // 6 of wide.
All inputs are finite; a program needn't handle non-finite values.
Results may differ from a plain program's by a relative error of at most 0.012.
The roundings to bfloat16 on the way count: a program that leaves them out, or rounds other values in their place, can miss the bound.
Values may be sent and summed in bfloat16 or wider, within the bound.
No kernel may reach another device: no remote copies, remote signals or barrier semaphores. Data moves between devices by JAX's collectives and lax.ppermute only.
A program may use at most 128 MiB of HBM per device.

v0:
```python
import math

import jax
import jax.numpy as jnp
from jax import lax
from jax.sharding import PartitionSpec as P

HEAD_SIZE = 128
QBLOCK = 64


NF4_LEVELS = (
    -1.0,
    -0.6961928009986877,
    -0.5250730514526367,
    -0.39491748809814453,
    -0.28444138169288635,
    -0.18477343022823334,
    -0.09105003625154495,
    0.0,
    0.07958029955625534,
    0.16093020141124725,
    0.24611230194568634,
    0.33791524171829224,
    0.44070982933044434,
    0.5626170039176941,
    0.7229568362236023,
    1.0,
)
ADAPTER_SCALE = 0.5
NEG_LARGE = -1e30


def dequantize(codes, scales):
    levels = jnp.zeros(codes.shape, jnp.float32)
    for number, level in enumerate(NF4_LEVELS):
        levels = jnp.where(codes == number, level, levels)
    height, breadth = codes.shape
    blocks = levels.reshape(height // QBLOCK, QBLOCK, breadth) * scales[:, None, :]
    return blocks.reshape(height, breadth).astype(jnp.bfloat16)


def on_device(
    tokens,
    query_quant_codes,
    query_absmax_scale,
    output_quant_codes,
    output_absmax_scale,
    adapter_down_maps,
    adapter_up_maps,
    row_adapter_index,
    adapter_storage_slot,
    row_cache_length,
    stored_key_cache,
    stored_value_cache,
    fresh_token_key,
    fresh_token_value,
):
    rows_dev = tokens.shape[0]
    query_weight = dequantize(query_quant_codes, query_absmax_scale)
    query_width = query_weight.shape[1]
    owned_portion = adapter_down_maps.shape[1]
    adapter_rank_size = adapter_down_maps.shape[2]
    down_matrix_flat = adapter_down_maps.reshape(
        adapter_down_maps.shape[0], owned_portion * adapter_rank_size
    )
    joined = jnp.concatenate([query_weight, down_matrix_flat], axis=1)
    projected = jnp.dot(
        lax.all_gather(tokens, "wide", axis=0, tiled=True),
        joined,
        preferred_element_type=jnp.float32,
    )
    query_base = projected[:, :query_width].astype(jnp.bfloat16)
    down_all = projected[:, query_width:]
    matches = row_adapter_index[:, None] == jnp.arange(adapter_storage_slot.shape[0])[None, :]
    slots = jnp.sum(jnp.where(matches, adapter_storage_slot[None, :], 0), axis=1)
    local_slot = slots - lax.axis_index("wide") * owned_portion
    query_transferred = lax.all_to_all(query_base, "wide", split_axis=0, concat_axis=1, tiled=True)
    column_owner = jnp.arange(owned_portion * adapter_rank_size) // adapter_rank_size
    keep = column_owner[None, :] == local_slot[:, None]
    rank_terms = jnp.where(keep, down_all, 0.0).astype(jnp.bfloat16)
    up_matrix_flat = adapter_up_maps.reshape(
        owned_portion * adapter_rank_size, adapter_up_maps.shape[2]
    )
    rounded = jnp.dot(rank_terms, up_matrix_flat, preferred_element_type=jnp.float32).astype(
        jnp.bfloat16
    )
    adapter_update = lax.psum_scatter(
        lax.optimization_barrier(rounded).astype(jnp.float32),
        "wide",
        scatter_dimension=0,
        tiled=True,
    )
    query_vector = (query_transferred.astype(jnp.float32) + ADAPTER_SCALE * adapter_update).astype(
        jnp.bfloat16
    )
    kv_local = stored_key_cache.shape[2] // HEAD_SIZE
    length = stored_key_cache.shape[1]
    grouped = query_vector.reshape(rows_dev, kv_local, -1, HEAD_SIZE)
    keys = stored_key_cache.reshape(rows_dev, length, kv_local, HEAD_SIZE)
    values = stored_value_cache.reshape(rows_dev, length, kv_local, HEAD_SIZE)
    scores = jnp.einsum(
        "rgkd,rtgd->rgkt", grouped, keys, preferred_element_type=jnp.float32
    ) / math.sqrt(HEAD_SIZE)
    valid = jnp.arange(length)[None, :] < row_cache_length[:, None]
    scores = jnp.where(valid[:, None, None, :], scores, NEG_LARGE)
    fresh = jnp.einsum(
        "rgkd,rgd->rgk",
        grouped,
        fresh_token_key.reshape(rows_dev, kv_local, HEAD_SIZE),
        preferred_element_type=jnp.float32,
    ) / math.sqrt(HEAD_SIZE)
    highest = jnp.maximum(jnp.max(scores, axis=-1), fresh)
    weights = jnp.exp(scores - highest[..., None])
    fresh_weight = jnp.exp(fresh - highest)
    total = jnp.sum(weights, axis=-1) + fresh_weight
    probs = (weights / total[..., None]).astype(jnp.bfloat16)
    fresh_prob = (fresh_weight / total).astype(jnp.bfloat16)
    context = jnp.einsum("rgkt,rtgd->rgkd", probs, values, preferred_element_type=jnp.float32)
    context = context + fresh_prob.astype(jnp.float32)[..., None] * fresh_token_value.reshape(
        rows_dev, kv_local, 1, HEAD_SIZE
    ).astype(jnp.float32)
    context = context.astype(jnp.bfloat16).reshape(
        rows_dev, kv_local * grouped.shape[2] * HEAD_SIZE
    )
    output_weight = dequantize(output_quant_codes, output_absmax_scale)
    partial_out = jnp.dot(
        lax.all_gather(context, "wide", axis=0, tiled=True),
        output_weight,
        preferred_element_type=jnp.float32,
    )
    summed = lax.psum(partial_out, "tensor")
    routed = lax.all_to_all(
        summed.astype(jnp.bfloat16), "wide", split_axis=0, concat_axis=1, tiled=True
    ).astype(summed.dtype)
    return routed.astype(jnp.bfloat16)


def solution(mesh):
    in_specs = (
        P(("rep", "wide"), None),
        P(None, ("tensor", "wide")),
        P(None, ("tensor", "wide")),
        P("tensor", "wide"),
        P("tensor", "wide"),
        P(None, "wide", None),
        P("wide", None, "tensor"),
        P("rep"),
        P(),
        P(("rep", "wide")),
        P(("rep", "wide"), None, "tensor"),
        P(("rep", "wide"), None, "tensor"),
        P(("rep", "wide"), "tensor"),
        P(("rep", "wide"), "tensor"),
    )
    out_specs = P(("rep", "wide"), None)
    return jax.shard_map(
        on_device, mesh=mesh, in_specs=in_specs, out_specs=out_specs, check_vma=False
    )
```

profile of v0, /device:TPU:0, one launch (start us, length us, event | category | flops | bytes accessed | tf_op | source)
XLA Modules:
  0.0 183.9 jit_solution(8497196278328149524)
XLA Ops:
  6.5 0.0 copy-start
  6.5 0.0 copy-start.7
  6.5 0.0 copy-start.6
  6.5 0.0 all-gather.2.cloned.1.call-start
  6.5 0.7 all-gather.2.cloned.1.call-update
  7.3 0.0 reduce-scatter.2.cloned.1.call-start
  7.3 5.9 %copy.20 = bf16[8192,192]{1,0:T(8,128)(2,1)} copy(bf16[8192,192]{0,1:T(8,128)(2,1)} %bitcast.59) | data formatting | bytes 6291456 | tf_op jit(solution)/shard_map/reshape | solution.py:64
  13.2 22.0 %fusion.1 = bf16[8192,512]{1,0:T(8,128)(2,1)} fusion(s32[8192,512]{1,0:T(8,128)} %param.15, f32[128,512]{1,0:T(8,128)} %param.16), kind=kLoop, calls=%fused_computation.3 | loop fusion | flops 142606336 | bytes 25427968 | tf_op jit(solution)/shard_map/convert_element_type | solution.py:40
  35.3 0.0 copy-start.3
  35.3 0.0 copy-start.2
  35.3 0.0 copy-done.7
  35.3 0.0 copy-done.6
  35.3 0.1 select_reduce_fusion
  35.4 17.0 %all-gather.2.cloned.1.call-done = bf16[64,8192]{1,0:T(8,128)(2,1)} async-done(((bf16[8,8192]{1,0:T(8,128)(2,1)}), bf16[64,8192]{1,0:T(8,128)(2,1)}) %all-gather.2.cloned.1.call-update) | async-done | bytes 1048592 | tf_op jit(solution)/shard_map/all_gather | solution.py:69
  52.4 6.2 %fusion.6 = bf16[64,704]{1,0:T(8,128)(2,1)S(1)} fusion(bf16[64,8192]{1,0:T(8,128)(2,1)} %all-gather.2.cloned.1.call-done, bf16[8192,192]{1,0:T(8,128)(2,1)} %copy.20, bf16[8192,512]{1,0:T(8,128)(2,1)} %fusion.1), kind=kOutput, calls=%fused_computation.9 | convolution fusion | flops 761266176 | bytes 12673024 | tf_op jit(solution)/shard_map/dot_general | solution.py:68
  58.5 0.0 copy-done
  58.6 0.0 copy-start.8
  58.6 0.0 copy-start.5
  58.6 0.0 copy-start.1
  58.6 0.0 copy-start.4
  58.6 0.5 convolution_convert_fusion
  59.1 1.1 convert_element_type.62
  60.2 0.0 reduce-scatter.2.cloned.1.call-update
  60.2 0.0 copy-done.3
  60.2 0.0 copy-done.2
  60.2 21.9 %fusion = bf16[4096,1024]{1,0:T(8,128)(2,1)} fusion(s32[4096,1024]{1,0:T(8,128)} %param.17, f32[64,1024]{1,0:T(8,128)S(1)} %copy-done.2), kind=kLoop, calls=%fused_computation.1 | loop fusion | flops 142606336 | bytes 25427968 | tf_op jit(solution)/shard_map/convert_element_type | solution.py:40
  82.1 0.6 fusion.17
  82.8 3.4 %all-to-all-start = ((bf16[8,8,512]{2,1,0:T(8,128)(2,1)}), bf16[8,8,512]{2,1,0:T(8,128)(2,1)S(1)}, u32[]{:S(2)}, u32[]{:S(2)}) async-start(bf16[8,8,512]{2,1,0:T(8,128)(2,1)} %fusion.17), calls=%async_computation | async-start | bytes 131072 | tf_op jit(solution)/shard_map/all_to_all | solution.py:78
  86.2 0.0 copy-done.8
  86.2 0.1 iota_compare_fusion.1
  86.2 6.8 %all-to-all-done = bf16[8,8,512]{2,1,0:T(8,128)(2,1)S(1)} async-done(((bf16[8,8,512]{2,1,0:T(8,128)(2,1)}), bf16[8,8,512]{2,1,0:T(8,128)(2,1)S(1)}, u32[]{:S(2)}, u32[]{:S(2)}) %all-to-all-start) | async-done | bytes 65568 | tf_op jit(solution)/shard_map/all_to_all | solution.py:78
  93.1 29.6 %reduce-scatter.2.cloned.1.call-done = f32[8,4096]{1,0:T(8,128)} async-done(((f32[64,4096]{1,0:T(8,128)}), f32[8,4096]{1,0:T(8,128)}) %reduce-scatter.2.cloned.1.call-update) | async-done | bytes 131088 | tf_op jit(solution)/shard_map/reduce_scatter | solution.py:88
  122.7 0.9 add_convert_fusion
  123.6 0.0 copy-done.5
  123.6 0.2 fusion.21
  123.8 0.0 copy-done.1
  123.8 0.5 fusion.33
  124.3 0.2 fusion.16
  124.6 0.0 copy-done.4
  124.6 0.3 fusion.11
  124.9 31.5 %all_gather.7 = bf16[64,4096]{1,0:T(8,128)(2,1)S(1)} all-gather(bf16[8,4096]{1,0:T(8,128)(2,1)S(1)} %bitcast.65), channel_id=1, replica_groups=mesh['rep'=2,'wide'=8,'tensor'=2] {'wide'}, dimensions={0}, use_global_device_ids=true | all-gather | bytes 589824 | tf_op jit(solution)/shard_map/all_gather | solution.py:128
  156.5 5.0 %fusion.34 = f32[64,1024]{1,0:T(8,128)S(1)} fusion(bf16[64,4096]{1,0:T(8,128)(2,1)S(1)} %all_gather.7, bf16[4096,1024]{1,0:T(8,128)(2,1)} %fusion), kind=kOutput, calls=%fused_computation.55 | convolution fusion | flops 536870912 | bytes 9175040 | tf_op jit(solution)/shard_map/dot_general | solution.py:127
  161.4 4.2 %all-reduce.1 = bf16[64,1024]{1,0:T(8,128)(2,1)S(1)} all-reduce(f32[64,1024]{1,0:T(8,128)S(1)} %fusion.34), channel_id=1, replica_groups=mesh['rep'=2,'wide'=8,'tensor'=2] {'tensor'}, use_global_device_ids=true, to_apply=%region_4.5 | all-reduce | flops 65536 | bytes 393216 | tf_op jit(solution)/shard_map/psum | solution.py:132
  165.6 10.8 %all_to_all.32 = bf16[8,8,1024]{2,1,0:T(8,128)(2,1)S(1)} all-to-all(bf16[8,8,1024]{2,1,0:T(8,128)(2,1)S(1)} %bitcast.60), channel_id=1, replica_groups=mesh['rep'=2,'wide'=8,'tensor'=2] {'wide'}, dimensions={0} | all-to-all | bytes 262144 | tf_op jit(solution)/shard_map/all_to_all | solution.py:133
  176.4 0.7 copy.53
  (8 shorter events, 0.1 us)
Async XLA Ops:
  6.5 52.0 %copy-start = (bf16[6,32,4096]{2,1,0:T(8,128)(2,1)S(1)}, bf16[6,32,4096]{2,1,0:T(8,128)(2,1)}, u32[]{:S(2)}) copy-start(bf16[6,32,4096]{2,1,0:T(8,128)(2,1)} %param.20) | copy-start | bytes 4718596
  6.5 28.7 %copy-start.7 = (s32[64]{0:T(128)S(1)}, s32[64]{0:T(128)}, u32[]{:S(2)}) copy-start(s32[64]{0:T(128)} %param.21) | copy-start | bytes 772
  6.5 28.7 %copy-start.6 = (s32[48]{0:T(128)S(1)}, s32[48]{0:T(128)}, u32[]{:S(2)}) copy-start(s32[48]{0:T(128)} %param.22) | copy-start | bytes 580
  6.5 45.8 %all-gather.2.cloned.1.call-start = ((), (), s32[]{:S(2)}) async-start(), calls=%async_computation.3 | async-start | bytes 1179648 | tf_op jit(solution)/shard_map/all_gather | solution.py:69
  7.3 115.5 %reduce-scatter.2.cloned.1.call-start = ((), (), s32[]{:S(2)}) async-start(), calls=%async_computation.4 | async-start | bytes 1179648 | tf_op jit(solution)/shard_map/reduce_scatter | solution.py:88
  35.3 25.0 %copy-start.3 = (bf16[8,512]{1,0:T(8,128)(2,1)S(1)}, bf16[8,512]{1,0:T(8,128)(2,1)}, u32[]{:S(2)}) copy-start(bf16[8,512]{1,0:T(8,128)(2,1)} %param.27) | copy-start | bytes 24580
  35.3 25.0 %copy-start.2 = (f32[64,1024]{1,0:T(8,128)S(1)}, f32[64,1024]{1,0:T(8,128)}, u32[]{:S(2)}) copy-start(f32[64,1024]{1,0:T(8,128)} %param.18) | copy-start | bytes 786436
  58.6 27.6 %copy-start.8 = (s32[8]{0:T(128)S(1)}, s32[8]{0:T(128)}, u32[]{:S(2)}) copy-start(s32[8]{0:T(128)} %param.23) | copy-start | bytes 100
  58.6 65.1 %copy-start.5 = (bf16[8,512]{1,0:T(8,128)(2,1)S(1)}, bf16[8,512]{1,0:T(8,128)(2,1)}, u32[]{:S(2)}) copy-start(bf16[8,512]{1,0:T(8,128)(2,1)} %param.26) | copy-start | bytes 24580
  58.6 65.2 %copy-start.1 = (bf16[8,64,512]{2,1,0:T(8,128)(2,1)S(1)}, bf16[8,64,512]{2,1,0:T(8,128)(2,1)}, u32[]{:S(2)}) copy-start(bf16[8,64,512]{2,1,0:T(8,128)(2,1)} %param.24) | copy-start | bytes 1572868
  58.6 66.0 %copy-start.4 = (bf16[8,64,512]{2,1,0:T(8,128)(2,1)S(1)}, bf16[8,64,512]{2,1,0:T(8,128)(2,1)}, u32[]{:S(2)}) copy-start(bf16[8,64,512]{2,1,0:T(8,128)(2,1)} %param.25) | copy-start | bytes 1572868
  82.8 10.3 %all-to-all-start = ((bf16[8,8,512]{2,1,0:T(8,128)(2,1)}), bf16[8,8,512]{2,1,0:T(8,128)(2,1)S(1)}, u32[]{:S(2)}, u32[]{:S(2)}) async-start(bf16[8,8,512]{2,1,0:T(8,128)(2,1)} %fusion.17), calls=%async_computation | async-start | bytes 131072 | tf_op jit(solution)/shard_map/all_to_all | solution.py:78
Sparse Core Ops, SparseCore 0:
  9.5 42.8 all-gather.1
  60.3 62.3 reduce-scatter.1
where the time goes:
time: 184 us
  waiting for transfers between devices  54.2 us (29%)
  blocking collectives  46.5 us (25%)
  other arithmetic  46.4 us (25%)
  between operations  13.6 us (7%)
  matrix products  12.5 us (7%)
  local copies, waits for them, and re-layouts  7.27 us (4%)
  starting transfers between devices  3.45 us (2%)
    convert_element_type x2, other arithmetic, dequantize(): return blocks.reshape(height, breadth).astype(jnp.bfloat16)  43.9 us
    all_gather x1, blocking collectives, on_device(): lax.all_gather(context, 'wide', axis=0, tiled=True)  31.5 us
    reduce_scatter x1, waiting for transfers between devices, on_device(): lax.psum_scatter(lax.optimization_barrier(rounded).astype(jnp.float32), '...  29.6 us
    all_gather x1, waiting for transfers between devices, on_device(): lax.all_gather(tokens, 'wide', axis=0, tiled=True)  17 us
    all_to_all x1, blocking collectives, on_device(): lax.all_to_all(summed.astype(jnp.bfloat16), 'wide', split_axis=0, concat_...  10.8 us
    all_to_all x1, waiting for transfers between devices, on_device(): lax.all_to_all(query_base, 'wide', split_axis=0, concat_axis=1, tiled=True)  6.83 us
    dot_general x1, matrix products, on_device(): jnp.dot(lax.all_gather(tokens, 'wide', axis=0, tiled=True), joined, prefe...  6.16 us
    reshape x1, local copies, waits for them, and re-layouts, on_device(): adapter_down_maps.reshape(adapter_down_maps.shape[0], owned_portion * ada...  5.91 us
  transfers between devices with their start and end apart: 3, of which 3 were waited for; matrix products, arithmetic and copies ran while one was open for 28% of the time, Pallas kernels for 0%

commit v1 on v0

v1 whole, which is shorter than its diff:
```python
import math

import jax
import jax.numpy as jnp
import numpy as np
from jax import lax
from jax.experimental import pallas as pl
from jax.experimental.pallas import tpu as pltpu
from jax.sharding import PartitionSpec as P

HEAD_SIZE = 128
QBLOCK = 64
LANES = 128


NF4_LEVELS = (
    -1.0,
    -0.6961928009986877,
    -0.5250730514526367,
    -0.39491748809814453,
    -0.28444138169288635,
    -0.18477343022823334,
    -0.09105003625154495,
    0.0,
    0.07958029955625534,
    0.16093020141124725,
    0.24611230194568634,
    0.33791524171829224,
    0.44070982933044434,
    0.5626170039176941,
    0.7229568362236023,
    1.0,
)
ADAPTER_SCALE = 0.5
NEG_LARGE = -1e30
MIB = 1 << 20
VMEM = pl.BlockSpec(memory_space=pltpu.VMEM)
SMEM = pl.BlockSpec(memory_space=pltpu.SMEM)
ANY = pl.BlockSpec(memory_space=pl.ANY)
LOOKUP = lax.GatherDimensionNumbers(
    offset_dims=(),
    collapsed_slice_dims=(0,),
    start_index_map=(0,),
    operand_batching_dims=(1,),
    start_indices_batching_dims=(1,),
)


def dequantize(codes, scales):
    levels = jnp.zeros(codes.shape, jnp.float32)
    for number, level in enumerate(NF4_LEVELS):
        levels = jnp.where(codes == number, level, levels)
    height, breadth = codes.shape
    blocks = levels.reshape(height // QBLOCK, QBLOCK, breadth) * scales[:, None, :]
    return blocks.reshape(height, breadth).astype(jnp.bfloat16)


def dequantize_part(codes, scales, row, column, height, breadth, after=()):
    chunk = 512
    steps = height // chunk
    blocks = chunk // QBLOCK
    levels = np.repeat(np.array(NF4_LEVELS, np.float32)[:, None], LANES, axis=1)

    def kernel(start, codes_ref, scales_ref, levels_ref, *rest):
        out_ref, held, arrived = rest[-3:]

        def fetch(step):
            return pltpu.make_async_copy(
                codes_ref.at[
                    pl.ds(pl.multiple_of(start[0] + step * chunk, chunk), chunk),
                    pl.ds(pl.multiple_of(start[1], LANES), breadth),
                ],
                held.at[pl.ds(pl.multiple_of(step * chunk, chunk), chunk)],
                arrived.at[step],
            )

        for step in range(steps):
            fetch(step).start()
        table = levels_ref[...]

        def work(step, carry):
            fetch(step).wait()
            first = pl.multiple_of(start[0] // QBLOCK + step * blocks, blocks)
            for lane in range(0, breadth, LANES):
                group = scales_ref[
                    pl.ds(first, blocks), pl.ds(pl.multiple_of(start[1] + lane, LANES), LANES)
                ]
                for block in range(blocks):
                    products = (table * group[block : block + 1]).astype(jnp.bfloat16)
                    at = pl.multiple_of(step * chunk + block * QBLOCK, QBLOCK)
                    numbers = held[pl.ds(at, QBLOCK), lane : lane + LANES].astype(jnp.int16)
                    for piece in range(0, QBLOCK, 16):
                        out_ref[pl.ds(at + piece, 16), lane : lane + LANES] = lax.gather(
                            products,
                            numbers[piece : piece + 16][..., None],
                            LOOKUP,
                            (1, 1),
                            mode=lax.GatherScatterMode.PROMISE_IN_BOUNDS,
                        )
            return carry

        lax.fori_loop(0, steps, work, 0)

    start = jnp.stack([row, column]).astype(jnp.int32)
    return pl.pallas_call(
        kernel,
        in_specs=[SMEM, ANY, VMEM, VMEM] + [ANY] * len(after),
        out_specs=VMEM,
        out_shape=pltpu.VMEM((height, breadth), jnp.bfloat16),
        scratch_shapes=[
            pltpu.VMEM((height, breadth), jnp.int32),
            pltpu.SemaphoreType.DMA((steps,)),
        ],
        compiler_params=pltpu.CompilerParams(vmem_limit_bytes=20 * MIB),
        cost_estimate=pl.CostEstimate(
            flops=2 * height * breadth, bytes_accessed=6 * height * breadth, transcendentals=0
        ),
        name="dequantize",
    )(start, codes, scales, jnp.asarray(levels), *after)


def project_rows(
    place, other_order, own, other, weight_own, weight_other, down, keep_rank, up
):
    count = own[0].shape[0] * 2
    half = own[0].shape[1]
    query_width = weight_own.shape[1]
    ranks, width = up.shape
    block = 8
    chunk = 512

    def kernel(
        place_ref,
        order_ref,
        own_low,
        own_high,
        other_low,
        other_high,
        weight_own_ref,
        weight_other_ref,
        down_ref,
        keep_ref,
        up_ref,
        stay_ref,
        leave_ref,
        query_part,
        down_part,
    ):
        core = place_ref[1]
        mine = jnp.concatenate([own_low[...], own_high[...]], axis=0)
        theirs = jnp.concatenate([other_low[...], other_high[...]], axis=0)
        last = (((1,), (1,)), ((), ()))
        down_part[...] = lax.dot_general(
            theirs,
            down_ref[:, pl.ds(pl.multiple_of((1 - core) * half, half), half)],
            last,
            preferred_element_type=jnp.float32,
        )
        query_part[...] = jnp.dot(
            theirs, weight_other_ref[...], preferred_element_type=jnp.float32
        )
        down_mine = lax.dot_general(
            mine,
            down_ref[:, pl.ds(pl.multiple_of(core * half, half), half)],
            last,
            preferred_element_type=jnp.float32,
        )
        query_mine = jnp.dot(mine, weight_own_ref[...], preferred_element_type=jnp.float32)
        down_rows, query_rows = [], []
        for at in range(0, count, block):
            there = pl.ds(pl.multiple_of(order_ref[at // block] * block, block), block)
            down_rows.append(down_mine[at : at + block] + down_part[there, :])
            query_rows.append(query_mine[at : at + block] + query_part[there, :])
        down_all = jnp.concatenate(down_rows, axis=0)
        query_base = jnp.concatenate(query_rows, axis=0).astype(jnp.bfloat16)
        terms = jnp.where(keep_ref[...] != 0, down_all, 0.0).astype(jnp.bfloat16)
        for lane in range(0, width, chunk):
            delta = jnp.dot(
                terms, up_ref[:, lane : lane + chunk], preferred_element_type=jnp.float32
            ).astype(jnp.bfloat16)
            scaled = (ADAPTER_SCALE * delta.astype(jnp.float32)).astype(jnp.bfloat16)
            stay_ref[:, lane : lane + chunk] = scaled[: count // 2]
            leave_ref[:, lane : lane + chunk] = scaled[count // 2 :]
        here = pl.ds(pl.multiple_of(place_ref[0] * query_width, query_width), query_width)
        base = query_base.astype(jnp.float32)
        stay_ref[:, here] = (base[: count // 2] + stay_ref[:, here].astype(jnp.float32)).astype(
            jnp.bfloat16
        )
        leave_ref[:, here] = (base[count // 2 :] + leave_ref[:, here].astype(jnp.float32)).astype(
            jnp.bfloat16
        )

    shape = jax.ShapeDtypeStruct((count // 2, width), jnp.bfloat16)
    return pl.pallas_call(
        kernel,
        in_specs=[SMEM, SMEM] + [VMEM] * 9,
        out_specs=[VMEM, VMEM],
        out_shape=[shape, shape],
        scratch_shapes=[
            pltpu.VMEM((count, query_width), jnp.float32),
            pltpu.VMEM((count, ranks), jnp.float32),
        ],
        compiler_params=pltpu.CompilerParams(vmem_limit_bytes=24 * MIB),
        cost_estimate=pl.CostEstimate(
            flops=2 * count * (2 * half * (query_width + ranks) + ranks * width),
            bytes_accessed=14 * MIB,
            transcendentals=0,
        ),
        name="project_rows",
    )(place, other_order, *own, *other, weight_own, weight_other, down, keep_rank, up)


def project_out(low, high, weight):
    count = low.shape[0] * 2

    def kernel(low_ref, high_ref, weight_ref, out_ref):
        rows = jnp.concatenate([low_ref[...], high_ref[...]], axis=0)
        out_ref[...] = jnp.dot(rows, weight_ref[...], preferred_element_type=jnp.float32)

    return pl.pallas_call(
        kernel,
        in_specs=[VMEM] * 3,
        out_specs=VMEM,
        out_shape=jax.ShapeDtypeStruct((count, weight.shape[1]), jnp.float32),
        compiler_params=pltpu.CompilerParams(vmem_limit_bytes=12 * MIB),
        cost_estimate=pl.CostEstimate(
            flops=2 * count * weight.shape[0] * weight.shape[1],
            bytes_accessed=6 * MIB,
            transcendentals=0,
        ),
        name="project_out",
    )(low, high, weight)


def sum_halves(targets, other_order, mine, theirs):
    block = 8
    count, width = mine.shape

    def kernel(targets_ref, order_ref, mine_ref, theirs_ref, out_ref):
        for at in range(0, count, block):
            there = pl.ds(pl.multiple_of(order_ref[at // block] * block, block), block)
            out_ref[targets_ref[at // block]] = (
                mine_ref[at : at + block] + theirs_ref[there, :]
            ).astype(jnp.bfloat16)

    return pl.pallas_call(
        kernel,
        in_specs=[SMEM, SMEM, VMEM, VMEM],
        out_specs=VMEM,
        out_shape=jax.ShapeDtypeStruct((count // block, block, width), jnp.bfloat16),
        name="sum_halves",
    )(targets, other_order, mine, theirs)


def join_columns(place, mine, theirs):
    sources, rows, width = mine.shape

    def kernel(place_ref, mine_ref, theirs_ref, out_ref):
        core = place_ref[1]
        for source in range(sources):
            first = source * 2 * width
            out_ref[:, pl.ds(pl.multiple_of(first + core * width, width), width)] = mine_ref[source]
            out_ref[:, pl.ds(pl.multiple_of(first + (1 - core) * width, width), width)] = (
                theirs_ref[source]
            )

    return pl.pallas_call(
        kernel,
        in_specs=[SMEM, VMEM, VMEM],
        out_specs=VMEM,
        out_shape=jax.ShapeDtypeStruct((rows, sources * 2 * width), mine.dtype),
        name="join_columns",
    )(place, mine, theirs)


def attend(
    query_vector,
    row_cache_length,
    stored_key_cache,
    stored_value_cache,
    fresh_token_key,
    fresh_token_value,
):
    rows_dev = query_vector.shape[0]
    kv_local = stored_key_cache.shape[2] // HEAD_SIZE
    length = stored_key_cache.shape[1]
    grouped = query_vector.reshape(rows_dev, kv_local, -1, HEAD_SIZE)
    keys = stored_key_cache.reshape(rows_dev, length, kv_local, HEAD_SIZE)
    values = stored_value_cache.reshape(rows_dev, length, kv_local, HEAD_SIZE)
    scores = jnp.einsum(
        "rgkd,rtgd->rgkt", grouped, keys, preferred_element_type=jnp.float32
    ) / math.sqrt(HEAD_SIZE)
    valid = jnp.arange(length)[None, :] < row_cache_length[:, None]
    scores = jnp.where(valid[:, None, None, :], scores, NEG_LARGE)
    fresh = jnp.einsum(
        "rgkd,rgd->rgk",
        grouped,
        fresh_token_key.reshape(rows_dev, kv_local, HEAD_SIZE),
        preferred_element_type=jnp.float32,
    ) / math.sqrt(HEAD_SIZE)
    highest = jnp.maximum(jnp.max(scores, axis=-1), fresh)
    weights = jnp.exp(scores - highest[..., None])
    fresh_weight = jnp.exp(fresh - highest)
    total = jnp.sum(weights, axis=-1) + fresh_weight
    probs = (weights / total[..., None]).astype(jnp.bfloat16)
    fresh_prob = (fresh_weight / total).astype(jnp.bfloat16)
    context = jnp.einsum("rgkt,rtgd->rgkd", probs, values, preferred_element_type=jnp.float32)
    context = context + fresh_prob.astype(jnp.float32)[..., None] * fresh_token_value.reshape(
        rows_dev, kv_local, 1, HEAD_SIZE
    ).astype(jnp.float32)
    return context.astype(jnp.bfloat16).reshape(
        rows_dev, kv_local * grouped.shape[2] * HEAD_SIZE
    )


def plain(
    tokens,
    query_quant_codes,
    query_absmax_scale,
    output_quant_codes,
    output_absmax_scale,
    adapter_down_maps,
    adapter_up_maps,
    row_adapter_index,
    adapter_storage_slot,
    row_cache_length,
    stored_key_cache,
    stored_value_cache,
    fresh_token_key,
    fresh_token_value,
):
    query_weight = dequantize(query_quant_codes, query_absmax_scale)
    query_width = query_weight.shape[1]
    owned_portion = adapter_down_maps.shape[1]
    adapter_rank_size = adapter_down_maps.shape[2]
    down_matrix_flat = adapter_down_maps.reshape(
        adapter_down_maps.shape[0], owned_portion * adapter_rank_size
    )
    joined = jnp.concatenate([query_weight, down_matrix_flat], axis=1)
    projected = jnp.dot(
        lax.all_gather(tokens, "wide", axis=0, tiled=True),
        joined,
        preferred_element_type=jnp.float32,
    )
    query_base = projected[:, :query_width].astype(jnp.bfloat16)
    down_all = projected[:, query_width:]
    matches = row_adapter_index[:, None] == jnp.arange(adapter_storage_slot.shape[0])[None, :]
    slots = jnp.sum(jnp.where(matches, adapter_storage_slot[None, :], 0), axis=1)
    local_slot = slots - lax.axis_index("wide") * owned_portion
    query_transferred = lax.all_to_all(query_base, "wide", split_axis=0, concat_axis=1, tiled=True)
    column_owner = jnp.arange(owned_portion * adapter_rank_size) // adapter_rank_size
    keep = column_owner[None, :] == local_slot[:, None]
    rank_terms = jnp.where(keep, down_all, 0.0).astype(jnp.bfloat16)
    up_matrix_flat = adapter_up_maps.reshape(
        owned_portion * adapter_rank_size, adapter_up_maps.shape[2]
    )
    rounded = jnp.dot(rank_terms, up_matrix_flat, preferred_element_type=jnp.float32).astype(
        jnp.bfloat16
    )
    adapter_update = lax.psum_scatter(
        lax.optimization_barrier(rounded).astype(jnp.float32),
        "wide",
        scatter_dimension=0,
        tiled=True,
    )
    query_vector = (query_transferred.astype(jnp.float32) + ADAPTER_SCALE * adapter_update).astype(
        jnp.bfloat16
    )
    context = attend(
        query_vector,
        row_cache_length,
        stored_key_cache,
        stored_value_cache,
        fresh_token_key,
        fresh_token_value,
    )
    output_weight = dequantize(output_quant_codes, output_absmax_scale)
    partial_out = jnp.dot(
        lax.all_gather(context, "wide", axis=0, tiled=True),
        output_weight,
        preferred_element_type=jnp.float32,
    )
    summed = lax.psum(partial_out, "tensor")
    routed = lax.all_to_all(
        summed.astype(jnp.bfloat16), "wide", split_axis=0, concat_axis=1, tiled=True
    )
    return routed


def fast(
    wide,
    tokens,
    query_quant_codes,
    query_absmax_scale,
    output_quant_codes,
    output_absmax_scale,
    adapter_down_maps,
    adapter_up_maps,
    row_adapter_index,
    adapter_storage_slot,
    row_cache_length,
    stored_key_cache,
    stored_value_cache,
    fresh_token_key,
    fresh_token_value,
):
    rows_dev, model_width = tokens.shape
    half = model_width // 2
    rounds = wide.bit_length() - 1
    flips = [list(range(rounds))[::-1], [0] + list(range(1, rounds))[::-1]]
    offsets = np.zeros((2, wide), np.int32)
    for core in range(2):
        for number in range(rounds):
            for at in range(wide):
                offsets[core, at] |= ((at >> number) & 1) << flips[core][number]
    positions = np.argsort(offsets, axis=1)
    orders = np.stack([positions[1 - core][offsets[core]] for core in range(2)]).astype(np.int32)

    me = lax.axis_index("wide").astype(jnp.int32)
    core = lax.axis_index("tensor").astype(jnp.int32)
    place = jnp.stack([me, core])
    first_core = core == 0
    other_order = jnp.where(first_core, orders[0], orders[1])
    targets = me ^ jnp.where(first_core, offsets[0], offsets[1])

    def swap(array, number):
        pairs = [
            (peer * 2 + side, (peer ^ (1 << flips[side][number])) * 2 + side)
            for peer in range(wide)
            for side in range(2)
        ]
        return lax.ppermute(array, ("wide", "tensor"), pairs)

    def cross(array):
        return lax.ppermute(array, "tensor", [(0, 1), (1, 0)])

    def gather_rows(array):
        for number in range(rounds - 1):
            array = jnp.concatenate([array, swap(array, number)], axis=0)
        return array, swap(array, rounds - 1)

    own = gather_rows(lax.dynamic_slice(tokens, (0, core * half), (rows_dev, half)))
    other = [cross(part) for part in own]

    weight_own = dequantize_part(
        query_quant_codes,
        query_absmax_scale,
        core * half,
        jnp.int32(0),
        half,
        query_quant_codes.shape[1],
    )
    weight_other = dequantize_part(
        query_quant_codes,
        query_absmax_scale,
        (1 - core) * half,
        jnp.int32(0),
        half,
        query_quant_codes.shape[1],
    )
    out_height, out_width = output_quant_codes.shape
    out_half = out_width // 2
    out_leave = dequantize_part(
        output_quant_codes,
        output_absmax_scale,
        jnp.int32(0),
        (1 - core) * out_half,
        out_height,
        out_half,
    )
    out_stay = dequantize_part(
        output_quant_codes,
        output_absmax_scale,
        jnp.int32(0),
        core * out_half,
        out_height,
        out_half,
    )

    owned, rank = adapter_down_maps.shape[1:]
    all_rows = (targets[:, None] * rows_dev + jnp.arange(rows_dev)[None, :]).reshape(-1)
    picked = all_rows[:, None] == jnp.arange(all_rows.shape[0])[None, :]
    adapters = jnp.sum(jnp.where(picked, row_adapter_index[None, :], 0), axis=1)
    matches = adapters[:, None] == jnp.arange(adapter_storage_slot.shape[0])[None, :]
    slots = jnp.sum(jnp.where(matches, adapter_storage_slot[None, :], 0), axis=1)
    rank_owner = jnp.arange(owned * rank) // rank + me * owned
    keep_rank = (rank_owner[None, :] == slots[:, None]).astype(jnp.int32)

    down = adapter_down_maps.transpose(1, 2, 0).reshape(owned * rank, model_width)
    up = adapter_up_maps.reshape(owned * rank, adapter_up_maps.shape[2])
    stay, leave = project_rows(
        place, other_order, own, other, weight_own, weight_other, down, keep_rank, up
    )

    for number in range(rounds)[::-1]:
        total = stay + swap(leave, number)
        keep = total.shape[0] // 2
        stay, leave = total[:keep], total[keep:]
    query_vector = total

    context = attend(
        query_vector,
        row_cache_length,
        stored_key_cache,
        stored_value_cache,
        fresh_token_key,
        fresh_token_value,
    )
    low, high = gather_rows(context)
    theirs = cross(project_out(low, high, out_leave))
    mine = project_out(low, high, out_stay)
    routed = lax.all_to_all(sum_halves(targets, other_order, mine, theirs), "wide", 0, 0)
    return join_columns(place, routed, cross(routed))


def solution(mesh):
    in_specs = (
        P(("rep", "wide"), None),
        P(None, ("tensor", "wide")),
        P(None, ("tensor", "wide")),
        P("tensor", "wide"),
        P("tensor", "wide"),
        P(None, "wide", None),
        P("wide", None, "tensor"),
        P("rep"),
        P(),
        P(("rep", "wide")),
        P(("rep", "wide"), None, "tensor"),
        P(("rep", "wide"), None, "tensor"),
        P(("rep", "wide"), "tensor"),
        P(("rep", "wide"), "tensor"),
    )
    out_specs = P(("rep", "wide"), None)
    wide = mesh.shape["wide"]

    def on_device(*args):
        query_width, out_width = args[1].shape[1], args[3].shape[1]
        whole_tiles = query_width % LANES == 0 and out_width % (2 * LANES) == 0
        return fast(wide, *args) if whole_tiles else plain(*args)

    return jax.shard_map(
        on_device, mesh=mesh, in_specs=in_specs, out_specs=out_specs, check_vma=False
    )
```

time: 184 us -> 112 us (0.61)
  other arithmetic: 46.4 us -> 4.25 us
  blocking collectives: 46.5 us -> 11.3 us
  waiting for transfers between devices: 54.2 us -> 31.5 us
  Pallas kernels: 0 us -> 19.9 us
  local copies, waits for them, and re-layouts: 7.27 us -> 25.1 us
  starting transfers between devices: 3.45 us -> 18.1 us
  between operations: 13.6 us -> 0.32 us
  matrix products: 12.5 us -> 0.94 us
    convert_element_type x6 -> x2, other arithmetic: 45.9 us -> 0.08 us  [the longest x1 0.07 us: fast(): keep_rank = (rank_owner[None, :] == slots[:, None]).astype(jnp.int32)]
    all_gather x1 -> x0, blocking collectives: 31.5 us -> none  [on_device(): lax.all_gather(context, 'wide', axis=0, tiled=True)]
    ppermute x0 -> x13, waiting for transfers between devices: none -> 31.5 us  [the longest x9 30.2 us: swap(): return lax.ppermute(array, ('wide', 'tensor'), pairs)]
    reduce_scatter x1 -> x0, waiting for transfers between devices: 29.6 us -> none  [on_device(): lax.psum_scatter(lax.optimization_barrier(rounded).astype(jnp.float32), '...]
    unnamed x20 -> x47, local copies, waits for them, and re-layouts: 0.73 us -> 24.1 us
    pallas_call x0 -> x9, Pallas kernels: none -> 19.9 us  [the longest x4 11.8 us: dequantize_part(): pl.pallas_call(kernel, in_specs=[SMEM, ANY, VMEM, VMEM] + [ANY] * len(aft...]
    ppermute x0 -> x13, starting transfers between devices: none -> 18.1 us  [the longest x9 18.1 us: swap(): return lax.ppermute(array, ('wide', 'tensor'), pairs)]
    all_gather x1 -> x0, waiting for transfers between devices: 17 us -> none  [on_device(): lax.all_gather(tokens, 'wide', axis=0, tiled=True)]
  transfers between devices with their start and end apart: 3 -> 13, of which waited for: 3 -> 9; matrix products, arithmetic and copies ran while one was open for 28% -> 4% of each run, Pallas kernels for 0% -> 11%
where the time goes in v1:
time: 112 us; the launch traced here: 111 us
  waiting for transfers between devices  31.5 us (28%)
  local copies, waits for them, and re-layouts  25.1 us (22%)
  Pallas kernels  19.9 us (18%)
  starting transfers between devices  18.1 us (16%)
  blocking collectives  11.3 us (10%)
  other arithmetic  4.25 us (4%)
    ppermute x9, waiting for transfers between devices, swap(): return lax.ppermute(array, ('wide', 'tensor'), pairs)  30.2 us
    unnamed x47, local copies, waits for them, and re-layouts  24.1 us
    ppermute x9, starting transfers between devices, swap(): return lax.ppermute(array, ('wide', 'tensor'), pairs)  18.1 us
    pallas_call x4, Pallas kernels, dequantize_part(): pl.pallas_call(kernel, in_specs=[SMEM, ANY, VMEM, VMEM] + [ANY] * len(aft...  11.8 us
    all_to_all x1, blocking collectives, fast(): lax.all_to_all(sum_halves(targets, other_order, mine, theirs), 'wide', 0, 0)  11.3 us
    pallas_call x1, Pallas kernels, project_rows(): pl.pallas_call(kernel, in_specs=[SMEM, SMEM] + [VMEM] * 9, out_specs=[VME...  3.19 us
  transfers between devices with their start and end apart: 13, of which 9 were waited for; matrix products, arithmetic and copies ran while one was open for 4% of the time, Pallas kernels for 11%

profile of v1, /device:TPU:0, one launch (start us, length us, event | category | flops | bytes accessed | tf_op | source)
XLA Modules:
  0.0 111.5 jit_solution(15661912454547280639)
XLA Ops:
  0.0 0.9 constant_dynamic-slice_fusion
  0.9 4.0 %collective-permute-start = (bf16[8,4096]{1,0:T(8,128)(2,1)S(1)}, bf16[8,4096]{1,0:T(8,128)(2,1)S(1)}, u32[]{:S(2)}, u32[]{:S(2)}) collective-permute-start(bf16[8,4096]{1,0:T(8,128)(2,1)S(1)} %constant_dynamic-slice_fusion), channel_id=1, source_target_pairs={{0,8},{1,3},{2,10},{3,1},{4,12},{5,7},{6,14},{7,5},{8,0},{9,11},{1... | collective-permute-start | bytes 196616 | tf_op jit(solution)/shard_map/ppermute | solution.py:432
  4.9 1.2 %broadcast_multiply_fusion = (s32[8]{0:T(128)S(1)}, s32[8]{0:T(128)}) fusion(s32[8]{0:T(128)} %constant.63.clone, s32[8]{0:T(128)} %constant.64.clone, pred[]{:T(512)S(6)} %eq.20, s32[]{:T(128)} %axis_index.23), kind=kLoop, calls=%fused_computation.53 | loop fusion | flops 24 | bytes 133 | tf_op jit(solution)/shard_map/mul | solution.py:481
  6.1 0.1 iota_add_fusion
  6.2 0.1 add.59
  6.3 0.8 select_reduce_fusion
  7.1 0.1 collective-permute-done
  7.2 2.0 %collective-permute-start.1 = (bf16[16,4096]{1,0:T(8,128)(2,1)S(1)}, bf16[16,4096]{1,0:T(8,128)(2,1)S(1)}, u32[]{:S(2)}, u32[]{:S(2)}) collective-permute-start(bf16[16,4096]{1,0:T(8,128)(2,1)S(1)} %pad_maximum_fusion.1), channel_id=1, source_target_pairs={{0,4},{1,9},{2,6},{3,11},{4,0},{5,13},{6,2},{7,15},{8,12},{9,1},{1... | collective-permute-start | bytes 393224 | tf_op jit(solution)/shard_map/ppermute | solution.py:432
  9.2 0.7 select_reduce_fusion.1
  9.9 2.6 %collective-permute-done.1 = bf16[16,4096]{1,0:T(8,128)(2,1)S(1)} collective-permute-done((bf16[16,4096]{1,0:T(8,128)(2,1)S(1)}, bf16[16,4096]{1,0:T(8,128)(2,1)S(1)}, u32[]{:S(2)}, u32[]{:S(2)}) %collective-permute-start.1) | collective-permute-done | bytes 131104 | tf_op jit(solution)/shard_map/ppermute | solution.py:432
  12.5 1.9 %collective-permute-start.2 = (bf16[32,4096]{1,0:T(8,128)(2,1)S(1)}, bf16[32,4096]{1,0:T(8,128)(2,1)S(1)}, u32[]{:S(2)}, u32[]{:S(2)}) collective-permute-start(bf16[32,4096]{1,0:T(8,128)(2,1)S(1)} %pad_maximum_fusion.own_low), channel_id=1, source_target_pairs={{0,2},{1,5},{2,0},{3,7},{4,6},{5,1},{6,4},{7,3},{8,10},{9,13},{10,... | collective-permute-start | bytes 786440 | tf_op jit(solution)/shard_map/ppermute | solution.py:432
  14.4 0.1 pad_add_fusion
  14.5 0.7 broadcast_select_fusion.order_ref
  15.2 0.0 collective-permute-start.3
  15.2 3.8 %collective-permute-done.2.own_high = bf16[32,4096]{1,0:T(8,128)(2,1)S(1)} collective-permute-done((bf16[32,4096]{1,0:T(8,128)(2,1)S(1)}, bf16[32,4096]{1,0:T(8,128)(2,1)S(1)}, u32[]{:S(2)}, u32[]{:S(2)}) %collective-permute-start.2) | collective-permute-done | bytes 262176 | tf_op jit(solution)/shard_map/ppermute | solution.py:432
  19.0 0.1 pad_add_fusion.4.place_ref
  19.1 5.8 %copy-done.1 = s32[8192,512]{1,0:T(8,128)S(1)} copy-done((s32[8192,512]{1,0:T(8,128)S(1)}, s32[8192,512]{1,0:T(8,128)}, u32[]{:S(2)}) %copy-start.1) | copy-done | bytes 16777240
  24.8 0.9 copy-done.7
  25.8 0.7 copy-done.11
  26.5 2.7 %dequantize.4.weight_own_ref = bf16[4096,512]{1,0:T(8,128)(2,1)S(1)} custom-call(s32[2]{0:T(128)S(1)} %get-tuple-element.16.start, s32[8192,512]{1,0:T(8,128)S(1)} %copy-done.1, f32[128,512]{1,0:T(8,128)S(1)} %copy-done.7, f32[16,128]{1,0:T(8,128)S(1)} %copy-done.11), custom_call_target="tpu_custom_call" | custom-call | flops 4194304 | bytes 12582912 | tf_op jit(solution)/shard_map/dequantize/pallas_call | solution.py:105
  29.2 3.1 %copy-done.2 = s32[8192,512]{1,0:T(8,128)S(1)} copy-done((s32[8192,512]{1,0:T(8,128)S(1)}, s32[8192,512]{1,0:T(8,128)}, u32[]{:S(2)}) %copy-start.2) | copy-done | bytes 16777240
  32.3 2.7 %dequantize.5.weight_other_ref = bf16[4096,512]{1,0:T(8,128)(2,1)S(1)} custom-call(s32[2]{0:T(128)S(1)} %get-tuple-element.15.start, s32[8192,512]{1,0:T(8,128)S(1)} %copy-done.2, f32[128,512]{1,0:T(8,128)S(1)} %copy-done.8, f32[16,128]{1,0:T(8,128)S(1)} %copy-done.12), custom_call_target="tpu_custom_call" | custom-call | flops 4194304 | bytes 12582912 | tf_op jit(solution)/shard_map/dequantize/pallas_call | solution.py:105
  35.0 0.1 compare_convert_fusion.keep_ref
  35.0 0.0 collective-permute-done.3.other_low
  35.1 0.0 copy-start.19
  35.1 0.0 copy-start.21
  35.1 0.0 copy-start.20
  35.1 0.0 copy-start.15
  35.1 3.2 %project_rows.1 = (bf16[32,4096]{1,0:T(8,128)(2,1)S(1)}, bf16[32,4096]{1,0:T(8,128)(2,1)S(1)}) custom-call(s32[2]{0:T(128)S(1)} %pad_add_fusion.4.place_ref, s32[8]{0:T(128)S(1)} %broadcast_select_fusion.order_ref, bf16[32,4096]{1,0:T(8,128)(2,1)S(1)} %pad_maximum_fusion.own_low, bf16[32,4096]{1,0:T(8,128)(2,1)S(1)} %collective-permute-done.2.own_high, ...), custom_call_target="tpu_custom_call" | custom-call | flops 838860800 | bytes 14680064 | tf_op jit(solution)/shard_map/project_rows/pallas_call | solution.py:194
  38.3 0.0 copy-start.9
  38.3 1.9 %collective-permute-start.5 = (bf16[32,4096]{1,0:T(8,128)(2,1)S(1)}, bf16[32,4096]{1,0:T(8,128)(2,1)S(1)}, u32[]{:S(2)}, u32[]{:S(2)}) collective-permute-start(bf16[32,4096]{1,0:T(8,128)(2,1)S(1)} %get-tuple-element.8), channel_id=1, source_target_pairs={{0,2},{1,5},{2,0},{3,7},{4,6},{5,1},{6,4},{7,3},{8,10},{9,13},{10,... | collective-permute-start | bytes 786440 | tf_op jit(solution)/shard_map/ppermute | solution.py:432
  40.2 4.5 %collective-permute-done.5 = bf16[32,4096]{1,0:T(8,128)(2,1)S(1)} collective-permute-done((bf16[32,4096]{1,0:T(8,128)(2,1)S(1)}, bf16[32,4096]{1,0:T(8,128)(2,1)S(1)}, u32[]{:S(2)}, u32[]{:S(2)}) %collective-permute-start.5) | collective-permute-done | bytes 262176 | tf_op jit(solution)/shard_map/ppermute | solution.py:432
  44.8 0.1 add.60
  44.9 1.7 %collective-permute-start.6 = (bf16[16,4096]{1,0:T(8,128)(2,1)S(1)}, bf16[16,4096]{1,0:T(8,128)(2,1)S(1)}, u32[]{:S(2)}, u32[]{:S(2)}) collective-permute-start(bf16[16,4096]{1,0:T(8,128)(2,1)S(1)} %slice.17), channel_id=1, source_target_pairs={{0,4},{1,9},{2,6},{3,11},{4,0},{5,13},{6,2},{7,15},{8,12},{9,1},{1... | collective-permute-start | bytes 393224 | tf_op jit(solution)/shard_map/ppermute | solution.py:432
  46.6 4.7 %collective-permute-done.6 = bf16[16,4096]{1,0:T(8,128)(2,1)S(1)} collective-permute-done((bf16[16,4096]{1,0:T(8,128)(2,1)S(1)}, bf16[16,4096]{1,0:T(8,128)(2,1)S(1)}, u32[]{:S(2)}, u32[]{:S(2)}) %collective-permute-start.6) | collective-permute-done | bytes 131104 | tf_op jit(solution)/shard_map/ppermute | solution.py:432
  51.3 2.3 %collective-permute-start.7 = (bf16[8,4096]{1,0:T(8,128)(2,1)S(1)}, bf16[8,4096]{1,0:T(8,128)(2,1)S(1)}, u32[]{:S(2)}, u32[]{:S(2)}) collective-permute-start(bf16[8,4096]{1,0:T(8,128)(2,1)S(1)} %slice.19), channel_id=1, source_target_pairs={{0,8},{1,3},{2,10},{3,1},{4,12},{5,7},{6,14},{7,5},{8,0},{9,11},{1... | collective-permute-start | bytes 196616 | tf_op jit(solution)/shard_map/ppermute | solution.py:432
  53.7 0.1 iota_compare_fusion.2
  53.7 2.8 %collective-permute-done.7 = bf16[8,4096]{1,0:T(8,128)(2,1)S(1)} collective-permute-done((bf16[8,4096]{1,0:T(8,128)(2,1)S(1)}, bf16[8,4096]{1,0:T(8,128)(2,1)S(1)}, u32[]{:S(2)}, u32[]{:S(2)}) %collective-permute-start.7) | collective-permute-done | bytes 65568 | tf_op jit(solution)/shard_map/ppermute | solution.py:432
  56.6 0.2 fusion.10
  56.8 0.5 fusion.19
  57.3 0.2 fusion.7
  57.5 0.3 fusion.2
  57.9 2.3 %collective-permute-start.8 = (bf16[8,4096]{1,0:T(8,128)(2,1)S(1)}, bf16[8,4096]{1,0:T(8,128)(2,1)S(1)}, u32[]{:S(2)}, u32[]{:S(2)}) collective-permute-start(bf16[8,4096]{1,0:T(8,128)(2,1)S(1)} %bitcast.47), channel_id=1, source_target_pairs={{0,8},{1,3},{2,10},{3,1},{4,12},{5,7},{6,14},{7,5},{8,0},{9,11},{1... | collective-permute-start | bytes 196616 | tf_op jit(solution)/shard_map/ppermute | solution.py:432
  60.2 5.7 %collective-permute-done.8 = bf16[8,4096]{1,0:T(8,128)(2,1)S(1)} collective-permute-done((bf16[8,4096]{1,0:T(8,128)(2,1)S(1)}, bf16[8,4096]{1,0:T(8,128)(2,1)S(1)}, u32[]{:S(2)}, u32[]{:S(2)}) %collective-permute-start.8) | collective-permute-done | bytes 65568 | tf_op jit(solution)/shard_map/ppermute | solution.py:432
  65.9 0.4 collective-permute-start.9
  66.3 5.9 %collective-permute-done.9 = bf16[16,4096]{1,0:T(8,128)(2,1)S(1)} collective-permute-done((bf16[16,4096]{1,0:T(8,128)(2,1)S(1)}, bf16[16,4096]{1,0:T(8,128)(2,1)S(1)}, u32[]{:S(2)}, u32[]{:S(2)}) %collective-permute-start.9) | collective-permute-done | bytes 131104 | tf_op jit(solution)/shard_map/ppermute | solution.py:432
  72.3 1.6 %collective-permute-start.10 = (bf16[32,4096]{1,0:T(8,128)(2,1)S(1)}, bf16[32,4096]{1,0:T(8,128)(2,1)S(1)}, u32[]{:S(2)}, u32[]{:S(2)}) collective-permute-start(bf16[32,4096]{1,0:T(8,128)(2,1)S(1)} %constant_dynamic-update-slice_fusion.low_ref), channel_id=1, source_target_pairs={{0,2},{1,5},{2,0},{3,7},{4,6},{5,1},{6,4},{7,3},{8,10},{9,13},{10,... | collective-permute-start | bytes 786440 | tf_op jit(solution)/shard_map/ppermute | solution.py:432
  73.9 0.1 pad_add_fusion.2
  73.9 5.8 %copy-done.3 = s32[4096,1024]{1,0:T(8,128)S(1)} copy-done((s32[4096,1024]{1,0:T(8,128)S(1)}, s32[4096,1024]{1,0:T(8,128)}, u32[]{:S(2)}) %copy-start.3) | copy-done | bytes 16777240
  79.7 3.2 %dequantize.7.weight_ref = bf16[4096,512]{1,0:T(8,128)(2,1)S(1)} custom-call(s32[2]{0:T(128)S(1)} %get-tuple-element.17.start, s32[4096,1024]{1,0:T(8,128)S(1)} %copy-done.3, f32[64,1024]{1,0:T(8,128)S(1)} %copy-done.9, f32[16,128]{1,0:T(8,128)S(1)} %copy-done.12), custom_call_target="tpu_custom_call" | custom-call | flops 4194304 | bytes 12582912 | tf_op jit(solution)/shard_map/dequantize/pallas_call | solution.py:105
  83.0 0.8 project_out.3
  83.8 0.1 collective-permute-start.11
  83.9 0.0 copy-start.4
  83.9 5.8 %copy-done.4 = s32[4096,1024]{1,0:T(8,128)S(1)} copy-done((s32[4096,1024]{1,0:T(8,128)S(1)}, s32[4096,1024]{1,0:T(8,128)}, u32[]{:S(2)}) %copy-start.4) | copy-done | bytes 16777240
  89.7 3.2 %dequantize.6.weight_ref = bf16[4096,512]{1,0:T(8,128)(2,1)S(1)} custom-call(s32[2]{0:T(128)S(1)} %get-tuple-element.18.start, s32[4096,1024]{1,0:T(8,128)S(1)} %copy-done.4, f32[64,1024]{1,0:T(8,128)S(1)} %copy-done.9, f32[16,128]{1,0:T(8,128)S(1)} %copy-done.12), custom_call_target="tpu_custom_call" | custom-call | flops 4194304 | bytes 12582912 | tf_op jit(solution)/shard_map/dequantize/pallas_call | solution.py:105
  92.9 0.8 project_out.2.mine_ref
  93.8 0.0 copy-start.10
  93.8 0.6 copy-done.10
  94.4 0.6 copy-done.17
  95.1 1.6 %sum_halves.1 = bf16[8,8,512]{2,1,0:T(8,128)(2,1)} custom-call(s32[8]{0:T(128)} %get-tuple-element.10.targets_ref, s32[8]{0:T(128)} %copy-done.13, f32[64,512]{1,0:T(8,128)} %copy-done.10, f32[64,512]{1,0:T(8,128)} %copy-done.17), custom_call_target="tpu_custom_call" | custom-call | tf_op jit(solution)/shard_map/sum_halves/pallas_call | solution.py:246
  96.7 11.3 %all_to_all.5.mine_ref = bf16[8,8,512]{2,1,0:T(8,128)(2,1)S(1)} all-to-all(bf16[8,8,512]{2,1,0:T(8,128)(2,1)} %sum_halves.1), channel_id=1, replica_groups=mesh['rep'=2,'wide'=8,'tensor'=2] {'wide'}, dimensions={0} | all-to-all | bytes 131072 | tf_op jit(solution)/shard_map/all_to_all | solution.py:512
  108.0 1.3 %collective-permute-done.12.theirs_ref = bf16[8,8,512]{2,1,0:T(8,128)(2,1)S(1)} collective-permute-done((bf16[8,8,512]{2,1,0:T(8,128)(2,1)S(1)}, bf16[8,8,512]{2,1,0:T(8,128)(2,1)S(1)}, u32[]{:S(2)}, u32[]{:S(2)}) %collective-permute-start.12) | collective-permute-done | bytes 65568 | tf_op jit(solution)/shard_map/ppermute | solution.py:435
  109.3 0.6 copy-done.18
  109.9 1.6 %join_columns.1 = bf16[8,8192]{1,0:T(8,128)(2,1)} custom-call(s32[2]{0:T(128)} %copy-done.14, bf16[8,8,512]{2,1,0:T(8,128)(2,1)} %copy-done.16, bf16[8,8,512]{2,1,0:T(8,128)(2,1)} %copy-done.18), custom_call_target="tpu_custom_call" | custom-call | tf_op jit(solution)/shard_map/join_columns/pallas_call | solution.py:267
  (49 shorter events, 0.3 us)
Async XLA Ops:
  0.0 57.5 %copy-start = (bf16[8,64,512]{2,1,0:T(8,128)(2,1)S(1)}, bf16[8,64,512]{2,1,0:T(8,128)(2,1)}, u32[]{:S(2)}) copy-start(bf16[8,64,512]{2,1,0:T(8,128)(2,1)} %param.33) | copy-start | bytes 1572868
  0.9 6.3 %collective-permute-start = (bf16[8,4096]{1,0:T(8,128)(2,1)S(1)}, bf16[8,4096]{1,0:T(8,128)(2,1)S(1)}, u32[]{:S(2)}, u32[]{:S(2)}) collective-permute-start(bf16[8,4096]{1,0:T(8,128)(2,1)S(1)} %constant_dynamic-slice_fusion), channel_id=1, source_target_pairs={{0,8},{1,3},{2,10},{3,1},{4,12},{5,7},{6,14},{7,5},{8,0},{9,11},{1... | collective-permute-start | bytes 196616 | tf_op jit(solution)/shard_map/ppermute | solution.py:432
  7.2 5.3 %collective-permute-start.1 = (bf16[16,4096]{1,0:T(8,128)(2,1)S(1)}, bf16[16,4096]{1,0:T(8,128)(2,1)S(1)}, u32[]{:S(2)}, u32[]{:S(2)}) collective-permute-start(bf16[16,4096]{1,0:T(8,128)(2,1)S(1)} %pad_maximum_fusion.1), channel_id=1, source_target_pairs={{0,4},{1,9},{2,6},{3,11},{4,0},{5,13},{6,2},{7,15},{8,12},{9,1},{1... | collective-permute-start | bytes 393224 | tf_op jit(solution)/shard_map/ppermute | solution.py:432
  12.5 6.4 %collective-permute-start.2 = (bf16[32,4096]{1,0:T(8,128)(2,1)S(1)}, bf16[32,4096]{1,0:T(8,128)(2,1)S(1)}, u32[]{:S(2)}, u32[]{:S(2)}) collective-permute-start(bf16[32,4096]{1,0:T(8,128)(2,1)S(1)} %pad_maximum_fusion.own_low), channel_id=1, source_target_pairs={{0,2},{1,5},{2,0},{3,7},{4,6},{5,1},{6,4},{7,3},{8,10},{9,13},{10,... | collective-permute-start | bytes 786440 | tf_op jit(solution)/shard_map/ppermute | solution.py:432
  15.2 19.9 %copy-start.13 = (s32[8]{0:T(128)}, s32[8]{0:T(128)S(1)}, u32[]{:S(2)}) copy-start(s32[8]{0:T(128)S(1)} %broadcast_select_fusion.order_ref) | copy-start | bytes 100
  15.2 19.9 %collective-permute-start.3 = (bf16[32,4096]{1,0:T(8,128)(2,1)S(1)}, bf16[32,4096]{1,0:T(8,128)(2,1)S(1)}, u32[]{:S(2)}, u32[]{:S(2)}) collective-permute-start(bf16[32,4096]{1,0:T(8,128)(2,1)S(1)} %pad_maximum_fusion.own_low), channel_id=1, source_target_pairs={{0,1},{1,0},{2,3},{3,2},{4,5},{5,4},{6,7},{7,6},{8,9},{9,8},{10,11... | collective-permute-start | bytes 786440 | tf_op jit(solution)/shard_map/ppermute | solution.py:435
  19.0 16.1 %collective-permute-start.4 = (bf16[32,4096]{1,0:T(8,128)(2,1)S(1)}, bf16[32,4096]{1,0:T(8,128)(2,1)S(1)}, u32[]{:S(2)}, u32[]{:S(2)}) collective-permute-start(bf16[32,4096]{1,0:T(8,128)(2,1)S(1)} %collective-permute-done.2.own_high), channel_id=1, source_target_pairs={{0,1},{1,0},{2,3},{3,2},{4,5},{5,4},{6,7},{7,6},{8,9},{9,8},{10,11... | collective-permute-start | bytes 786440 | tf_op jit(solution)/shard_map/ppermute | solution.py:435
  19.1 16.0 %copy-start.14 = (s32[2]{0:T(128)}, s32[2]{0:T(128)S(1)}, u32[]{:S(2)}) copy-start(s32[2]{0:T(128)S(1)} %pad_add_fusion.4.place_ref) | copy-start | bytes 28
  19.1 5.8 %copy-start.1 = (s32[8192,512]{1,0:T(8,128)S(1)}, s32[8192,512]{1,0:T(8,128)}, u32[]{:S(2)}) copy-start(s32[8192,512]{1,0:T(8,128)} %codes_ref.5) | copy-start | bytes 50331652
  24.8 0.9 copy-start.7
  25.8 0.7 copy-start.11
  26.5 5.8 %copy-start.2 = (s32[8192,512]{1,0:T(8,128)S(1)}, s32[8192,512]{1,0:T(8,128)}, u32[]{:S(2)}) copy-start(s32[8192,512]{1,0:T(8,128)} %codes_ref.5) | copy-start | bytes 50331652
  26.5 5.8 %copy-start.8 = (f32[128,512]{1,0:T(8,128)S(1)}, f32[128,512]{1,0:T(8,128)}, u32[]{:S(2)}) copy-start(f32[128,512]{1,0:T(8,128)} %scales_ref.5) | copy-start | bytes 786436
  26.5 5.8 %copy-start.12 = (f32[16,128]{1,0:T(8,128)S(1)}, f32[16,128]{1,0:T(8,128)}, u32[]{:S(2)}) copy-start(f32[16,128]{1,0:T(8,128)} %constant.65.clone.levels_ref) | copy-start | bytes 24580
  32.3 2.8 %copy-start.5 = (bf16[8192,6,32]{0,2,1:T(8,128)(2,1)S(1)}, bf16[8192,6,32]{0,2,1:T(8,128)(2,1)}, u32[]{:S(2)}) copy-start(bf16[8192,6,32]{0,2,1:T(8,128)(2,1)} %param.27) | copy-start | bytes 9437188
  32.3 2.8 %copy-start.6 = (bf16[6,32,4096]{2,1,0:T(8,128)(2,1)S(1)}, bf16[6,32,4096]{2,1,0:T(8,128)(2,1)}, u32[]{:S(2)}) copy-start(bf16[6,32,4096]{2,1,0:T(8,128)(2,1)} %param.28) | copy-start | bytes 4718596
  35.1 11.5 %copy-start.19 = (bf16[8,512]{1,0:T(8,128)(2,1)S(1)}, bf16[8,512]{1,0:T(8,128)(2,1)}, u32[]{:S(2)}) copy-start(bf16[8,512]{1,0:T(8,128)(2,1)} %param.35) | copy-start | bytes 24580
  35.1 18.6 %copy-start.21 = (s32[8]{0:T(128)S(1)}, s32[8]{0:T(128)}, u32[]{:S(2)}) copy-start(s32[8]{0:T(128)} %param.31) | copy-start | bytes 100
  35.1 21.5 %copy-start.20 = (bf16[8,512]{1,0:T(8,128)(2,1)S(1)}, bf16[8,512]{1,0:T(8,128)(2,1)}, u32[]{:S(2)}) copy-start(bf16[8,512]{1,0:T(8,128)(2,1)} %param.34) | copy-start | bytes 24580
  35.1 21.6 %copy-start.15 = (bf16[8,64,512]{2,1,0:T(8,128)(2,1)S(1)}, bf16[8,64,512]{2,1,0:T(8,128)(2,1)}, u32[]{:S(2)}) copy-start(bf16[8,64,512]{2,1,0:T(8,128)(2,1)} %param.32) | copy-start | bytes 1572868
  38.3 35.6 %copy-start.9 = (f32[64,1024]{1,0:T(8,128)S(1)}, f32[64,1024]{1,0:T(8,128)}, u32[]{:S(2)}) copy-start(f32[64,1024]{1,0:T(8,128)} %scales_ref.7) | copy-start | bytes 786436
  38.3 6.4 %collective-permute-start.5 = (bf16[32,4096]{1,0:T(8,128)(2,1)S(1)}, bf16[32,4096]{1,0:T(8,128)(2,1)S(1)}, u32[]{:S(2)}, u32[]{:S(2)}) collective-permute-start(bf16[32,4096]{1,0:T(8,128)(2,1)S(1)} %get-tuple-element.8), channel_id=1, source_target_pairs={{0,2},{1,5},{2,0},{3,7},{4,6},{5,1},{6,4},{7,3},{8,10},{9,13},{10,... | collective-permute-start | bytes 786440 | tf_op jit(solution)/shard_map/ppermute | solution.py:432
  44.9 6.4 %collective-permute-start.6 = (bf16[16,4096]{1,0:T(8,128)(2,1)S(1)}, bf16[16,4096]{1,0:T(8,128)(2,1)S(1)}, u32[]{:S(2)}, u32[]{:S(2)}) collective-permute-start(bf16[16,4096]{1,0:T(8,128)(2,1)S(1)} %slice.17), channel_id=1, source_target_pairs={{0,4},{1,9},{2,6},{3,11},{4,0},{5,13},{6,2},{7,15},{8,12},{9,1},{1... | collective-permute-start | bytes 393224 | tf_op jit(solution)/shard_map/ppermute | solution.py:432
  51.3 5.2 %collective-permute-start.7 = (bf16[8,4096]{1,0:T(8,128)(2,1)S(1)}, bf16[8,4096]{1,0:T(8,128)(2,1)S(1)}, u32[]{:S(2)}, u32[]{:S(2)}) collective-permute-start(bf16[8,4096]{1,0:T(8,128)(2,1)S(1)} %slice.19), channel_id=1, source_target_pairs={{0,8},{1,3},{2,10},{3,1},{4,12},{5,7},{6,14},{7,5},{8,0},{9,11},{1... | collective-permute-start | bytes 196616 | tf_op jit(solution)/shard_map/ppermute | solution.py:432
  57.9 8.0 %collective-permute-start.8 = (bf16[8,4096]{1,0:T(8,128)(2,1)S(1)}, bf16[8,4096]{1,0:T(8,128)(2,1)S(1)}, u32[]{:S(2)}, u32[]{:S(2)}) collective-permute-start(bf16[8,4096]{1,0:T(8,128)(2,1)S(1)} %bitcast.47), channel_id=1, source_target_pairs={{0,8},{1,3},{2,10},{3,1},{4,12},{5,7},{6,14},{7,5},{8,0},{9,11},{1... | collective-permute-start | bytes 196616 | tf_op jit(solution)/shard_map/ppermute | solution.py:432
  65.9 6.4 %collective-permute-start.9 = (bf16[16,4096]{1,0:T(8,128)(2,1)S(1)}, bf16[16,4096]{1,0:T(8,128)(2,1)S(1)}, u32[]{:S(2)}, u32[]{:S(2)}) collective-permute-start(bf16[16,4096]{1,0:T(8,128)(2,1)S(1)} %pad_maximum_fusion.2), channel_id=1, source_target_pairs={{0,4},{1,9},{2,6},{3,11},{4,0},{5,13},{6,2},{7,15},{8,12},{9,1},{1... | collective-permute-start | bytes 393224 | tf_op jit(solution)/shard_map/ppermute | solution.py:432
  72.3 10.7 %collective-permute-start.10 = (bf16[32,4096]{1,0:T(8,128)(2,1)S(1)}, bf16[32,4096]{1,0:T(8,128)(2,1)S(1)}, u32[]{:S(2)}, u32[]{:S(2)}) collective-permute-start(bf16[32,4096]{1,0:T(8,128)(2,1)S(1)} %constant_dynamic-update-slice_fusion.low_ref), channel_id=1, source_target_pairs={{0,2},{1,5},{2,0},{3,7},{4,6},{5,1},{6,4},{7,3},{8,10},{9,13},{10,... | collective-permute-start | bytes 786440 | tf_op jit(solution)/shard_map/ppermute | solution.py:432
  73.9 5.8 %copy-start.3 = (s32[4096,1024]{1,0:T(8,128)S(1)}, s32[4096,1024]{1,0:T(8,128)}, u32[]{:S(2)}) copy-start(s32[4096,1024]{1,0:T(8,128)} %codes_ref.7) | copy-start | bytes 50331652
  83.8 10.6 %collective-permute-start.11 = (f32[64,512]{1,0:T(8,128)S(1)}, f32[64,512]{1,0:T(8,128)S(1)}, u32[]{:S(2)}, u32[]{:S(2)}) collective-permute-start(f32[64,512]{1,0:T(8,128)S(1)} %project_out.3), channel_id=1, source_target_pairs={{0,1},{1,0},{2,3},{3,2},{4,5},{5,4},{6,7},{7,6},{8,9},{9,8},{10,11... | collective-permute-start | bytes 393224 | tf_op jit(solution)/shard_map/ppermute | solution.py:435
  83.9 5.8 %copy-start.4 = (s32[4096,1024]{1,0:T(8,128)S(1)}, s32[4096,1024]{1,0:T(8,128)}, u32[]{:S(2)}) copy-start(s32[4096,1024]{1,0:T(8,128)} %codes_ref.7) | copy-start | bytes 50331652
  93.8 0.7 copy-start.10
  94.4 0.7 copy-start.17
  108.0 1.3 %copy-start.16 = (bf16[8,8,512]{2,1,0:T(8,128)(2,1)}, bf16[8,8,512]{2,1,0:T(8,128)(2,1)S(1)}, u32[]{:S(2)}) copy-start(bf16[8,8,512]{2,1,0:T(8,128)(2,1)S(1)} %all_to_all.5.mine_ref) | copy-start | bytes 196612
  108.0 1.3 %collective-permute-start.12 = (bf16[8,8,512]{2,1,0:T(8,128)(2,1)S(1)}, bf16[8,8,512]{2,1,0:T(8,128)(2,1)S(1)}, u32[]{:S(2)}, u32[]{:S(2)}) collective-permute-start(bf16[8,8,512]{2,1,0:T(8,128)(2,1)S(1)} %all_to_all.5.mine_ref), channel_id=1, source_target_pairs={{0,1},{1,0},{2,3},{3,2},{4,5},{5,4},{6,7},{7,6},{8,9},{9,8},{10,11... | collective-permute-start | bytes 196616 | tf_op jit(solution)/shard_map/ppermute | solution.py:435
  109.3 0.6 copy-start.18

commit v2 on v1

--- a/solution.py
+++ b/solution.py
@@ -55,35 +55,46 @@
     return blocks.reshape(height, breadth).astype(jnp.bfloat16)
 
 
-def dequantize_part(codes, scales, row, column, height, breadth, after=()):
+def dequantize_part(codes, scales, segments, column, breadth, room, sent):
     chunk = 512
+    height = sum(rows for _, rows in segments)
     steps = height // chunk
     blocks = chunk // QBLOCK
-    levels = np.repeat(np.array(NF4_LEVELS, np.float32)[:, None], LANES, axis=1)
-
-    def kernel(start, codes_ref, scales_ref, levels_ref, *rest):
-        out_ref, held, arrived = rest[-3:]
+    starts = [first + at for first, rows in segments for at in range(0, rows, chunk)]
+    starts, _ = lax.optimization_barrier((jnp.stack([column] + starts).astype(jnp.int32), sent))
+
+    def kernel(starts_ref, codes_ref, scales_ref, out_ref, held, factors, arrived, factors_arrived):
+        columns = pl.ds(pl.multiple_of(starts_ref[0], LANES), breadth)
 
         def fetch(step):
             return pltpu.make_async_copy(
-                codes_ref.at[
-                    pl.ds(pl.multiple_of(start[0] + step * chunk, chunk), chunk),
-                    pl.ds(pl.multiple_of(start[1], LANES), breadth),
-                ],
+                codes_ref.at[pl.ds(pl.multiple_of(starts_ref[step + 1], chunk), chunk), columns],
                 held.at[pl.ds(pl.multiple_of(step * chunk, chunk), chunk)],
                 arrived.at[step],
             )
 
+        def fetch_factors(step):
+            first = pl.multiple_of(starts_ref[step + 1] // QBLOCK, blocks)
+            return pltpu.make_async_copy(
+                scales_ref.at[pl.ds(first, blocks), columns],
+                factors.at[pl.ds(pl.multiple_of(step * blocks, blocks), blocks)],
+                factors_arrived.at[step],
+            )
+
         for step in range(steps):
+            fetch_factors(step).start()
             fetch(step).start()
-        table = levels_ref[...]
+        number = lax.broadcasted_iota(jnp.int32, (16, LANES), 0)
+        table = jnp.zeros((16, LANES), jnp.float32)
+        for code, level in enumerate(NF4_LEVELS):
+            table = jnp.where(number == code, level, table)
 
         def work(step, carry):
+            fetch_factors(step).wait()
             fetch(step).wait()
-            first = pl.multiple_of(start[0] // QBLOCK + step * blocks, blocks)
             for lane in range(0, breadth, LANES):
-                group = scales_ref[
-                    pl.ds(first, blocks), pl.ds(pl.multiple_of(start[1] + lane, LANES), LANES)
+                group = factors[
+                    pl.ds(pl.multiple_of(step * blocks, blocks), blocks), lane : lane + LANES
                 ]
                 for block in range(blocks):
                     products = (table * group[block : block + 1]).astype(jnp.bfloat16)
@@ -101,79 +112,91 @@
 
         lax.fori_loop(0, steps, work, 0)
 
-    start = jnp.stack([row, column]).astype(jnp.int32)
     return pl.pallas_call(
         kernel,
-        in_specs=[SMEM, ANY, VMEM, VMEM] + [ANY] * len(after),
+        in_specs=[SMEM, ANY, ANY],
         out_specs=VMEM,
         out_shape=pltpu.VMEM((height, breadth), jnp.bfloat16),
         scratch_shapes=[
             pltpu.VMEM((height, breadth), jnp.int32),
+            pltpu.VMEM((height // QBLOCK, breadth), jnp.float32),
+            pltpu.SemaphoreType.DMA((steps,)),
             pltpu.SemaphoreType.DMA((steps,)),
         ],
-        compiler_params=pltpu.CompilerParams(vmem_limit_bytes=20 * MIB),
+        compiler_params=pltpu.CompilerParams(vmem_limit_bytes=room * MIB),
         cost_estimate=pl.CostEstimate(
             flops=2 * height * breadth, bytes_accessed=6 * height * breadth, transcendentals=0
         ),
         name="dequantize",
-    )(start, codes, scales, jnp.asarray(levels), *after)
-
-
-def project_rows(
-    place, other_order, own, other, weight_own, weight_other, down, keep_rank, up
-):
+    )(starts, codes, scales)
+
+
+LAST = (((1,), (1,)), ((), ()))
+
+
+def project_own(place, own, first_weight, rest_weight, down):
     count = own[0].shape[0] * 2
     half = own[0].shape[1]
-    query_width = weight_own.shape[1]
-    ranks, width = up.shape
-    block = 8
+    cut, query_width = first_weight.shape
+
+    def kernel(place_ref, low, high, first_ref, rest_ref, down_ref, query_ref, rank_ref):
+        rows = jnp.concatenate([low[...], high[...]], axis=0)
+        here = pl.ds(pl.multiple_of(place_ref[1] * half, half), half)
+        rank_ref[...] = lax.dot_general(
+            rows, down_ref[:, here], LAST, preferred_element_type=jnp.float32
+        )
+        query_ref[...] = jnp.dot(
+            rows[:, :cut], first_ref[...], preferred_element_type=jnp.float32
+        ) + jnp.dot(rows[:, cut:], rest_ref[: half - cut], preferred_element_type=jnp.float32)
+
+    return pl.pallas_call(
+        kernel,
+        in_specs=[SMEM] + [VMEM] * 5,
+        out_specs=[VMEM, VMEM],
+        out_shape=[
+            jax.ShapeDtypeStruct((count, query_width), jnp.float32),
+            jax.ShapeDtypeStruct((count, down.shape[0]), jnp.float32),
+        ],
+        compiler_params=pltpu.CompilerParams(vmem_limit_bytes=24 * MIB),
+        cost_estimate=pl.CostEstimate(
+            flops=2 * count * half * (query_width + down.shape[0]),
+            bytes_accessed=7 * MIB,
+            transcendentals=0,
+        ),
+        name="project_own",
+    )(place, *own, first_weight, rest_weight, down)
+
+
+def project_other(place, other, rest_weight, down, query_mine, rank_mine, keep_rank, up):
+    count = other[0].shape[0] * 2
+    half = other[0].shape[1]
+    query_width = rest_weight.shape[1]
+    width = up.shape[1]
     chunk = 512
 
     def kernel(
         place_ref,
-        order_ref,
-        own_low,
-        own_high,
-        other_low,
-        other_high,
-        weight_own_ref,
-        weight_other_ref,
+        low,
+        high,
+        rest_ref,
         down_ref,
+        query_ref,
+        rank_ref,
         keep_ref,
         up_ref,
         stay_ref,
         leave_ref,
-        query_part,
-        down_part,
     ):
-        core = place_ref[1]
-        mine = jnp.concatenate([own_low[...], own_high[...]], axis=0)
-        theirs = jnp.concatenate([other_low[...], other_high[...]], axis=0)
-        last = (((1,), (1,)), ((), ()))
-        down_part[...] = lax.dot_general(
-            theirs,
-            down_ref[:, pl.ds(pl.multiple_of((1 - core) * half, half), half)],
-            last,
-            preferred_element_type=jnp.float32,
-        )
-        query_part[...] = jnp.dot(
-            theirs, weight_other_ref[...], preferred_element_type=jnp.float32
-        )
-        down_mine = lax.dot_general(
-            mine,
-            down_ref[:, pl.ds(pl.multiple_of(core * half, half), half)],
-            last,
-            preferred_element_type=jnp.float32,
-        )
-        query_mine = jnp.dot(mine, weight_own_ref[...], preferred_element_type=jnp.float32)
-        down_rows, query_rows = [], []
-        for at in range(0, count, block):
-            there = pl.ds(pl.multiple_of(order_ref[at // block] * block, block), block)
-            down_rows.append(down_mine[at : at + block] + down_part[there, :])
-            query_rows.append(query_mine[at : at + block] + query_part[there, :])
-        down_all = jnp.concatenate(down_rows, axis=0)
-        query_base = jnp.concatenate(query_rows, axis=0).astype(jnp.bfloat16)
-        terms = jnp.where(keep_ref[...] != 0, down_all, 0.0).astype(jnp.bfloat16)
+        rows = jnp.concatenate([low[...], high[...]], axis=0)
+        there = pl.ds(pl.multiple_of((1 - place_ref[1]) * half, half), half)
+        ranks = rank_ref[...] + lax.dot_general(
+            rows, down_ref[:, there], LAST, preferred_element_type=jnp.float32
+        )
+        terms = jnp.where(keep_ref[...] != 0, ranks, 0.0).astype(jnp.bfloat16)
+        query = query_ref[...] + jnp.dot(
+            rows, rest_ref[rest_ref.shape[0] - half :], preferred_element_type=jnp.float32
+        )
+        base = query.astype(jnp.bfloat16).astype(jnp.float32)
         for lane in range(0, width, chunk):
             delta = jnp.dot(
                 terms, up_ref[:, lane : lane + chunk], preferred_element_type=jnp.float32
@@ -182,7 +205,6 @@
             stay_ref[:, lane : lane + chunk] = scaled[: count // 2]
             leave_ref[:, lane : lane + chunk] = scaled[count // 2 :]
         here = pl.ds(pl.multiple_of(place_ref[0] * query_width, query_width), query_width)
-        base = query_base.astype(jnp.float32)
         stay_ref[:, here] = (base[: count // 2] + stay_ref[:, here].astype(jnp.float32)).astype(
             jnp.bfloat16
         )
@@ -193,21 +215,17 @@
     shape = jax.ShapeDtypeStruct((count // 2, width), jnp.bfloat16)
     return pl.pallas_call(
         kernel,
-        in_specs=[SMEM, SMEM] + [VMEM] * 9,
+        in_specs=[SMEM] + [VMEM] * 8,
         out_specs=[VMEM, VMEM],
         out_shape=[shape, shape],
-        scratch_shapes=[
-            pltpu.VMEM((count, query_width), jnp.float32),
-            pltpu.VMEM((count, ranks), jnp.float32),
-        ],
         compiler_params=pltpu.CompilerParams(vmem_limit_bytes=24 * MIB),
         cost_estimate=pl.CostEstimate(
-            flops=2 * count * (2 * half * (query_width + ranks) + ranks * width),
-            bytes_accessed=14 * MIB,
+            flops=2 * count * (half * (query_width + up.shape[0]) + up.shape[0] * width),
+            bytes_accessed=8 * MIB,
             transcendentals=0,
         ),
-        name="project_rows",
-    )(place, other_order, *own, *other, weight_own, weight_other, down, keep_rank, up)
+        name="project_other",
+    )(place, *other, rest_weight, down, query_mine, rank_mine, keep_rank, up)
 
 
 def project_out(low, high, weight):
@@ -232,45 +250,41 @@
     )(low, high, weight)
 
 
-def sum_halves(targets, other_order, mine, theirs):
+def sum_halves(targets, mine, theirs):
     block = 8
     count, width = mine.shape
 
-    def kernel(targets_ref, order_ref, mine_ref, theirs_ref, out_ref):
+    def kernel(targets_ref, mine_ref, theirs_ref, out_ref):
         for at in range(0, count, block):
-            there = pl.ds(pl.multiple_of(order_ref[at // block] * block, block), block)
-            out_ref[targets_ref[at // block]] = (
-                mine_ref[at : at + block] + theirs_ref[there, :]
-            ).astype(jnp.bfloat16)
-
-    return pl.pallas_call(
-        kernel,
-        in_specs=[SMEM, SMEM, VMEM, VMEM],
-        out_specs=VMEM,
-        out_shape=jax.ShapeDtypeStruct((count // block, block, width), jnp.bfloat16),
-        name="sum_halves",
-    )(targets, other_order, mine, theirs)
-
-
-def join_columns(place, mine, theirs):
-    sources, rows, width = mine.shape
-
-    def kernel(place_ref, mine_ref, theirs_ref, out_ref):
-        core = place_ref[1]
-        for source in range(sources):
-            first = source * 2 * width
-            out_ref[:, pl.ds(pl.multiple_of(first + core * width, width), width)] = mine_ref[source]
-            out_ref[:, pl.ds(pl.multiple_of(first + (1 - core) * width, width), width)] = (
-                theirs_ref[source]
-            )
+            rows = (mine_ref[at : at + block] + theirs_ref[at : at + block]).astype(jnp.bfloat16)
+            for side in range(2):
+                out_ref[targets_ref[at // block] * 2 + side] = rows
 
     return pl.pallas_call(
         kernel,
         in_specs=[SMEM, VMEM, VMEM],
         out_specs=VMEM,
-        out_shape=jax.ShapeDtypeStruct((rows, sources * 2 * width), mine.dtype),
+        out_shape=jax.ShapeDtypeStruct((count // block * 2, block, width), jnp.bfloat16),
+        compiler_params=pltpu.CompilerParams(vmem_limit_bytes=4 * MIB),
+        name="sum_halves",
+    )(targets, mine, theirs)
+
+
+def join_columns(pieces):
+    sources, rows, width = pieces.shape
+
+    def kernel(pieces_ref, out_ref):
+        for source in range(sources):
+            out_ref[:, source * width : (source + 1) * width] = pieces_ref[source]
+
+    return pl.pallas_call(
+        kernel,
+        in_specs=[VMEM],
+        out_specs=VMEM,
+        out_shape=jax.ShapeDtypeStruct((rows, sources * width), pieces.dtype),
+        compiler_params=pltpu.CompilerParams(vmem_limit_bytes=4 * MIB),
         name="join_columns",
-    )(place, mine, theirs)
+    )(pieces)
 
 
 def attend(
@@ -407,75 +421,84 @@
     rows_dev, model_width = tokens.shape
     half = model_width // 2
     rounds = wide.bit_length() - 1
-    flips = [list(range(rounds))[::-1], [0] + list(range(1, rounds))[::-1]]
-    offsets = np.zeros((2, wide), np.int32)
-    for core in range(2):
-        for number in range(rounds):
-            for at in range(wide):
-                offsets[core, at] |= ((at >> number) & 1) << flips[core][number]
-    positions = np.argsort(offsets, axis=1)
-    orders = np.stack([positions[1 - core][offsets[core]] for core in range(2)]).astype(np.int32)
+    offsets = np.zeros(wide, np.int32)
+    for number in range(rounds):
+        for at in range(wide):
+            offsets[at] |= ((at >> number) & 1) << (rounds - 1 - number)
 
     me = lax.axis_index("wide").astype(jnp.int32)
     core = lax.axis_index("tensor").astype(jnp.int32)
+    zero = jnp.int32(0)
     place = jnp.stack([me, core])
-    first_core = core == 0
-    other_order = jnp.where(first_core, orders[0], orders[1])
-    targets = me ^ jnp.where(first_core, offsets[0], offsets[1])
+    targets = me ^ offsets
 
     def swap(array, number):
-        pairs = [
-            (peer * 2 + side, (peer ^ (1 << flips[side][number])) * 2 + side)
-            for peer in range(wide)
-            for side in range(2)
-        ]
-        return lax.ppermute(array, ("wide", "tensor"), pairs)
+        bit = 1 << (rounds - 1 - number)
+        return lax.ppermute(array, "wide", [(peer, peer ^ bit) for peer in range(wide)])
 
     def cross(array):
         return lax.ppermute(array, "tensor", [(0, 1), (1, 0)])
 
-    def gather_rows(array):
-        for number in range(rounds - 1):
-            array = jnp.concatenate([array, swap(array, number)], axis=0)
-        return array, swap(array, rounds - 1)
-
-    own = gather_rows(lax.dynamic_slice(tokens, (0, core * half), (rows_dev, half)))
-    other = [cross(part) for part in own]
-
-    weight_own = dequantize_part(
-        query_quant_codes,
-        query_absmax_scale,
-        core * half,
-        jnp.int32(0),
-        half,
-        query_quant_codes.shape[1],
-    )
-    weight_other = dequantize_part(
-        query_quant_codes,
-        query_absmax_scale,
-        (1 - core) * half,
-        jnp.int32(0),
-        half,
-        query_quant_codes.shape[1],
-    )
+    def beside(work, sent, received):
+        if work is None:
+            return received, None
+        return lax.optimization_barrier((received, work(sent)))
+
+    def gather_rows(array, works):
+        made = []
+        for number in range(rounds):
+            work = works.get(rounds - 1 - number)
+            received, result = beside(work, array, swap(array, number))
+            made.append(result)
+            if number < rounds - 1:
+                array = jnp.concatenate([array, received], axis=0)
+        return (array, received), made[::-1]
+
+    query_width = query_quant_codes.shape[1]
     out_height, out_width = output_quant_codes.shape
     out_half = out_width // 2
-    out_leave = dequantize_part(
-        output_quant_codes,
-        output_absmax_scale,
-        jnp.int32(0),
-        (1 - core) * out_half,
-        out_height,
-        out_half,
-    )
-    out_stay = dequantize_part(
-        output_quant_codes,
-        output_absmax_scale,
-        jnp.int32(0),
-        core * out_half,
-        out_height,
-        out_half,
-    )
+    cut = half // 2
+    own_row, other_row = core * half, (1 - core) * half
+
+    def query_first(sent):
+        return dequantize_part(
+            query_quant_codes,
+            query_absmax_scale,
+            [(own_row, cut)],
+            zero,
+            query_width,
+            50,
+            sent,
+        )
+
+    def query_rest(sent):
+        return dequantize_part(
+            query_quant_codes,
+            query_absmax_scale,
+            [(own_row + cut, half - cut), (other_row, half)],
+            zero,
+            query_width,
+            46,
+            sent,
+        )
+
+    def out_part(column):
+        return lambda sent: dequantize_part(
+            output_quant_codes,
+            output_absmax_scale,
+            [(zero, out_height)],
+            column,
+            out_half,
+            47,
+            sent,
+        )
+
+    own, made = gather_rows(
+        lax.dynamic_slice(tokens, (0, core * half), (rows_dev, half)),
+        {1: query_first, 0: query_rest},
+    )
+    rest_weight, first_weight = made[:2]
+    other = [cross(part) for part in own]
 
     owned, rank = adapter_down_maps.shape[1:]
     all_rows = (targets[:, None] * rows_dev + jnp.arange(rows_dev)[None, :]).reshape(-1)
@@ -488,29 +511,34 @@
 
     down = adapter_down_maps.transpose(1, 2, 0).reshape(owned * rank, model_width)
     up = adapter_up_maps.reshape(owned * rank, adapter_up_maps.shape[2])
-    stay, leave = project_rows(
-        place, other_order, own, other, weight_own, weight_other, down, keep_rank, up
-    )
-
+    query_mine, rank_mine = project_own(place, own, first_weight, rest_weight, down)
+    stay, leave = project_other(
+        place, other, rest_weight, down, query_mine, rank_mine, keep_rank, up
+    )
+
+    out_leave = None
     for number in range(rounds)[::-1]:
-        total = stay + swap(leave, number)
+        work = out_part((1 - core) * out_half) if number == rounds - 1 else None
+        received, result = beside(work, leave, swap(leave, number))
+        out_leave = out_leave if result is None else result
+        total = stay + received
         keep = total.shape[0] // 2
         stay, leave = total[:keep], total[keep:]
-    query_vector = total
 
     context = attend(
-        query_vector,
+        total,
         row_cache_length,
         stored_key_cache,
         stored_value_cache,
         fresh_token_key,
         fresh_token_value,
     )
-    low, high = gather_rows(context)
+    (low, high), made = gather_rows(context, {0: out_part(core * out_half)})
+    out_stay = made[0]
     theirs = cross(project_out(low, high, out_leave))
     mine = project_out(low, high, out_stay)
-    routed = lax.all_to_all(sum_halves(targets, other_order, mine, theirs), "wide", 0, 0)
-    return join_columns(place, routed, cross(routed))
+    routed = lax.all_to_all(sum_halves(targets, mine, theirs), ("wide", "tensor"), 0, 0)
+    return join_columns(routed)
 
 
 def solution(mesh):

time: 112 us -> 80.7 us (0.72)
  local copies, waits for them, and re-layouts: 25.1 us -> 4.37 us
  waiting for transfers between devices: 31.5 us -> 22.1 us
  Pallas kernels: 19.9 us -> 24.6 us
  starting transfers between devices: 18.1 us -> 14.3 us
  other arithmetic: 4.25 us -> 1.6 us
    unnamed x47 -> x31, local copies, waits for them, and re-layouts: 24.1 us -> 3.01 us
    ppermute x9, waiting for transfers between devices: 30.2 us -> 21.7 us  [swap(): lax.ppermute(array, 'wide', [(peer, peer ^ bit) for peer in range(wide)])]
    pallas_call x7 -> x8, Pallas kernels: 18.2 us -> 22.9 us  [the longest x4 17.8 us: dequantize_part(): pl.pallas_call(kernel, in_specs=[SMEM, ANY, ANY], out_specs=VMEM, out_sha...]
    ppermute x9, starting transfers between devices: 18.1 us -> 13.8 us  [swap(): lax.ppermute(array, 'wide', [(peer, peer ^ bit) for peer in range(wide)])]
  transfers between devices with their start and end apart: 13 -> 12, of which waited for: 9 -> 9; matrix products, arithmetic and copies ran while one was open for 4% -> 2% of each run, Pallas kernels for 11% -> 25%
where the time goes in v2:
time: 80.7 us; the launch traced here: 80.5 us
  Pallas kernels  24.6 us (30%)
  waiting for transfers between devices  22.1 us (27%)
  starting transfers between devices  14.3 us (18%)
  blocking collectives  12.3 us (15%)
  local copies, waits for them, and re-layouts  4.37 us (5%)
  other arithmetic  1.6 us (2%)
  matrix products  0.94 us (1%)
    ppermute x9, waiting for transfers between devices, swap(): lax.ppermute(array, 'wide', [(peer, peer ^ bit) for peer in range(wide)])  21.7 us
    pallas_call x4, Pallas kernels, dequantize_part(): pl.pallas_call(kernel, in_specs=[SMEM, ANY, ANY], out_specs=VMEM, out_sha...  17.8 us
    ppermute x9, starting transfers between devices, swap(): lax.ppermute(array, 'wide', [(peer, peer ^ bit) for peer in range(wide)])  13.8 us
    all_to_all x1, blocking collectives, fast(): lax.all_to_all(sum_halves(targets, mine, theirs), ('wide', 'tensor'), 0, 0)  12.3 us
    unnamed x31, local copies, waits for them, and re-layouts  3.01 us
    pallas_call x1, Pallas kernels, project_other(): pl.pallas_call(kernel, in_specs=[SMEM] + [VMEM] * 8, out_specs=[VMEM, VME...  2.11 us
    pallas_call x1, Pallas kernels, project_own(): pl.pallas_call(kernel, in_specs=[SMEM] + [VMEM] * 5, out_specs=[VMEM, VME...  1.78 us
    pallas_call x2, Pallas kernels, project_out(): pl.pallas_call(kernel, in_specs=[VMEM] * 3, out_specs=VMEM, out_shape=jax...  1.69 us
  transfers between devices with their start and end apart: 12, of which 9 were waited for; matrix products, arithmetic and copies ran while one was open for 2% of the time, Pallas kernels for 25%

profile of v2, /device:TPU:0, one launch (start us, length us, event | category | flops | bytes accessed | tf_op | source)
XLA Modules:
  0.0 80.5 jit_solution(17136908880000648547)
XLA Ops:
  0.0 0.9 %constant_dynamic-slice_fusion = bf16[8,4096]{1,0:T(8,128)(2,1)S(1)} fusion(bf16[8,8192]{1,0:T(8,128)(2,1)} %param.15, s32[]{:T(128)S(6)} %select_n.24), kind=kLoop, calls=%fused_computation.47 | loop fusion | bytes 131076 | tf_op jit(solution)/shard_map/dynamic_slice | solution.py:497
  0.9 4.0 %collective-permute-start = (bf16[8,4096]{1,0:T(8,128)(2,1)S(1)}, bf16[8,4096]{1,0:T(8,128)(2,1)S(1)}, u32[]{:S(2)}, u32[]{:S(2)}) collective-permute-start(bf16[8,4096]{1,0:T(8,128)(2,1)S(1)} %constant_dynamic-slice_fusion), channel_id=1, source_target_pairs={{0,8},{2,10},{4,12},{6,14},{8,0},{10,2},{12,4},{14,6},{1,9},{3,11}... | collective-permute-start | bytes 196616 | tf_op jit(solution)/shard_map/ppermute | solution.py:437
  4.9 0.7 broadcast_multiply_fusion
  5.6 0.1 stack.82.starts_ref
  5.7 2.9 %collective-permute-done = bf16[8,4096]{1,0:T(8,128)(2,1)S(1)} collective-permute-done((bf16[8,4096]{1,0:T(8,128)(2,1)S(1)}, bf16[8,4096]{1,0:T(8,128)(2,1)S(1)}, u32[]{:S(2)}, u32[]{:S(2)}) %collective-permute-start) | collective-permute-done | bytes 65568 | tf_op jit(solution)/shard_map/ppermute | solution.py:437
  8.6 0.6 collective-permute-start.1
  9.2 0.1 iota_add_fusion
  9.3 0.9 %copy-done.5 = f32[128,512]{1,0:T(8,128)S(1)} copy-done((f32[128,512]{1,0:T(8,128)S(1)}, f32[128,512]{1,0:T(8,128)}, u32[]{:S(2)}) %copy-start.5) | copy-done | bytes 262168
  10.3 3.0 %dequantize.4.first_ref = bf16[2048,512]{1,0:T(8,128)(2,1)S(1)} custom-call(s32[5]{0:T(128)S(1)} %stack.82.starts_ref, s32[8192,512]{1,0:T(8,128)} %codes_ref.5, f32[128,512]{1,0:T(8,128)S(1)} %copy-done.5), custom_call_target="tpu_custom_call" | custom-call | flops 2097152 | bytes 6291456 | tf_op jit(solution)/shard_map/dequantize/pallas_call | solution.py:115
  13.3 0.4 collective-permute-done.1
  13.7 1.8 %collective-permute-start.3 = (bf16[32,4096]{1,0:T(8,128)(2,1)S(1)}, bf16[32,4096]{1,0:T(8,128)(2,1)S(1)}, u32[]{:S(2)}, u32[]{:S(2)}) collective-permute-start(bf16[32,4096]{1,0:T(8,128)(2,1)S(1)} %pad_maximum_fusion.low), channel_id=1, source_target_pairs={{0,2},{2,0},{4,6},{6,4},{8,10},{10,8},{12,14},{14,12},{1,3},{3,1},... | collective-permute-start | bytes 786440 | tf_op jit(solution)/shard_map/ppermute | solution.py:437
  15.4 0.1 add.121
  15.5 0.1 stack.95.starts_ref
  15.6 0.2 select_reduce_fusion
  15.8 0.1 select_reduce_fusion.1
  15.9 0.1 collective-permute-start.2
  16.0 5.8 %dequantize.5.rest_ref = bf16[6144,512]{1,0:T(8,128)(2,1)S(1)} custom-call(s32[13]{0:T(128)S(1)} %stack.95.starts_ref, s32[8192,512]{1,0:T(8,128)} %codes_ref.5, f32[128,512]{1,0:T(8,128)S(1)} %copy-done.6), custom_call_target="tpu_custom_call" | custom-call | flops 6291456 | bytes 18874368 | tf_op jit(solution)/shard_map/dequantize/pallas_call | solution.py:115
  21.8 0.0 collective-permute-done.3.high
  21.8 0.3 collective-permute-start.4
  22.2 0.1 pad_add_fusion.place_ref
  22.3 0.1 compare_convert_fusion.keep_ref
  22.4 0.0 copy-start.4
  22.4 1.8 %project_own.1 = (f32[64,512]{1,0:T(8,128)S(1)}, f32[64,192]{1,0:T(8,128)S(1)}) custom-call(s32[2]{0:T(128)S(1)} %pad_add_fusion.place_ref, bf16[32,4096]{1,0:T(8,128)(2,1)S(1)} %pad_maximum_fusion.low, bf16[32,4096]{1,0:T(8,128)(2,1)S(1)} %collective-permute-done.3.high, bf16[2048,512]{1,0:T(8,128)(2,1)S(1)} %dequantize.4.first_ref, ...), custom_call_target="tpu_custom_call" | custom-call | flops 369098752 | bytes 7340032 | tf_op jit(solution)/shard_map/project_own/pallas_call | solution.py:152
  24.1 0.0 collective-permute-done.2.low
  24.2 0.0 collective-permute-done.4.high
  24.2 0.0 copy-start.7
  24.2 2.1 %project_other.1 = (bf16[32,4096]{1,0:T(8,128)(2,1)S(1)}, bf16[32,4096]{1,0:T(8,128)(2,1)S(1)}) custom-call(s32[2]{0:T(128)S(1)} %pad_add_fusion.place_ref, bf16[32,4096]{1,0:T(8,128)(2,1)S(1)} %collective-permute-done.2.low, bf16[32,4096]{1,0:T(8,128)(2,1)S(1)} %collective-permute-done.4.high, bf16[6144,512]{1,0:T(8,128)(2,1)S(1)} %dequantize.5.rest_ref, ...), custom_call_target="tpu_custom_call" | custom-call | flops 469762048 | bytes 8388608 | tf_op jit(solution)/shard_map/project_other/pallas_call | solution.py:216
  26.3 0.4 collective-permute-start.5
  26.7 0.1 stack.97.starts_ref
  26.8 0.0 copy-start.9
  26.8 0.0 copy-start.13
  26.8 0.0 copy-start.10
  26.8 0.0 copy-start.8
  26.8 4.3 %dequantize.6.weight_ref = bf16[4096,512]{1,0:T(8,128)(2,1)S(1)} custom-call(s32[9]{0:T(128)S(1)} %stack.97.starts_ref, s32[4096,1024]{1,0:T(8,128)} %codes_ref.7, f32[64,1024]{1,0:T(8,128)S(1)} %copy-done.7), custom_call_target="tpu_custom_call" | custom-call | flops 4194304 | bytes 12582912 | tf_op jit(solution)/shard_map/dequantize/pallas_call | solution.py:115
  31.2 1.9 %copy-done.1 = bf16[4096,512]{1,0:T(8,128)(2,1)} copy-done((bf16[4096,512]{1,0:T(8,128)(2,1)}, bf16[4096,512]{1,0:T(8,128)(2,1)S(1)}, u32[]{:S(2)}) %copy-start.1) | copy-done | bytes 4194328
  33.1 1.7 %collective-permute-done.5 = bf16[32,4096]{1,0:T(8,128)(2,1)S(1)} collective-permute-done((bf16[32,4096]{1,0:T(8,128)(2,1)S(1)}, bf16[32,4096]{1,0:T(8,128)(2,1)S(1)}, u32[]{:S(2)}, u32[]{:S(2)}) %collective-permute-start.5) | collective-permute-done | bytes 262176 | tf_op jit(solution)/shard_map/ppermute | solution.py:437
  34.8 0.1 add.122
  34.9 1.2 %collective-permute-start.6 = (bf16[16,4096]{1,0:T(8,128)(2,1)S(1)}, bf16[16,4096]{1,0:T(8,128)(2,1)S(1)}, u32[]{:S(2)}, u32[]{:S(2)}) collective-permute-start(bf16[16,4096]{1,0:T(8,128)(2,1)S(1)} %slice.17), channel_id=1, source_target_pairs={{0,4},{2,6},{4,0},{6,2},{8,12},{10,14},{12,8},{14,10},{1,5},{3,7},... | collective-permute-start | bytes 393224 | tf_op jit(solution)/shard_map/ppermute | solution.py:437
  36.1 0.0 copy-done.9
  36.1 3.8 %collective-permute-done.6 = bf16[16,4096]{1,0:T(8,128)(2,1)S(1)} collective-permute-done((bf16[16,4096]{1,0:T(8,128)(2,1)S(1)}, bf16[16,4096]{1,0:T(8,128)(2,1)S(1)}, u32[]{:S(2)}, u32[]{:S(2)}) %collective-permute-start.6) | collective-permute-done | bytes 131104 | tf_op jit(solution)/shard_map/ppermute | solution.py:437
  40.0 2.9 %collective-permute-start.7 = (bf16[8,4096]{1,0:T(8,128)(2,1)S(1)}, bf16[8,4096]{1,0:T(8,128)(2,1)S(1)}, u32[]{:S(2)}, u32[]{:S(2)}) collective-permute-start(bf16[8,4096]{1,0:T(8,128)(2,1)S(1)} %slice.19), channel_id=1, source_target_pairs={{0,8},{2,10},{4,12},{6,14},{8,0},{10,2},{12,4},{14,6},{1,9},{3,11}... | collective-permute-start | bytes 196616 | tf_op jit(solution)/shard_map/ppermute | solution.py:437
  42.9 0.1 iota_compare_fusion.2
  42.9 3.0 %collective-permute-done.7 = bf16[8,4096]{1,0:T(8,128)(2,1)S(1)} collective-permute-done((bf16[8,4096]{1,0:T(8,128)(2,1)S(1)}, bf16[8,4096]{1,0:T(8,128)(2,1)S(1)}, u32[]{:S(2)}, u32[]{:S(2)}) %collective-permute-start.7) | collective-permute-done | bytes 65568 | tf_op jit(solution)/shard_map/ppermute | solution.py:437
  45.9 0.0 copy-done.10
  45.9 0.2 fusion.10
  46.1 0.5 fusion.17
  46.6 0.2 fusion.7
  46.8 0.0 copy-done
  46.8 0.3 fusion.2
  47.2 2.3 %collective-permute-start.8 = (bf16[8,4096]{1,0:T(8,128)(2,1)S(1)}, bf16[8,4096]{1,0:T(8,128)(2,1)S(1)}, u32[]{:S(2)}, u32[]{:S(2)}) collective-permute-start(bf16[8,4096]{1,0:T(8,128)(2,1)S(1)} %bitcast.62), channel_id=1, source_target_pairs={{0,8},{2,10},{4,12},{6,14},{8,0},{10,2},{12,4},{14,6},{1,9},{3,11}... | collective-permute-start | bytes 196616 | tf_op jit(solution)/shard_map/ppermute | solution.py:437
  49.5 3.7 %collective-permute-done.8 = bf16[8,4096]{1,0:T(8,128)(2,1)S(1)} collective-permute-done((bf16[8,4096]{1,0:T(8,128)(2,1)S(1)}, bf16[8,4096]{1,0:T(8,128)(2,1)S(1)}, u32[]{:S(2)}, u32[]{:S(2)}) %collective-permute-start.8) | collective-permute-done | bytes 65568 | tf_op jit(solution)/shard_map/ppermute | solution.py:437
  53.2 0.3 collective-permute-start.9
  53.5 4.7 %collective-permute-done.9 = bf16[16,4096]{1,0:T(8,128)(2,1)S(1)} collective-permute-done((bf16[16,4096]{1,0:T(8,128)(2,1)S(1)}, bf16[16,4096]{1,0:T(8,128)(2,1)S(1)}, u32[]{:S(2)}, u32[]{:S(2)}) %collective-permute-start.9) | collective-permute-done | bytes 131104 | tf_op jit(solution)/shard_map/ppermute | solution.py:437
  58.3 0.3 collective-permute-start.10
  58.6 0.1 stack.99.starts_ref
  58.7 4.6 %dequantize.7.weight_ref = bf16[4096,512]{1,0:T(8,128)(2,1)S(1)} custom-call(s32[9]{0:T(128)S(1)} %stack.99.starts_ref, s32[4096,1024]{1,0:T(8,128)} %codes_ref.7, f32[64,1024]{1,0:T(8,128)S(1)} %copy-done.7), custom_call_target="tpu_custom_call" | custom-call | flops 4194304 | bytes 12582912 | tf_op jit(solution)/shard_map/dequantize/pallas_call | solution.py:115
  63.3 1.4 %collective-permute-done.10.high_ref = bf16[32,4096]{1,0:T(8,128)(2,1)S(1)} collective-permute-done((bf16[32,4096]{1,0:T(8,128)(2,1)S(1)}, bf16[32,4096]{1,0:T(8,128)(2,1)S(1)}, u32[]{:S(2)}, u32[]{:S(2)}) %collective-permute-start.10) | collective-permute-done | bytes 262176 | tf_op jit(solution)/shard_map/ppermute | solution.py:437
  64.7 0.8 %project_out.3 = f32[64,512]{1,0:T(8,128)S(1)} custom-call(bf16[32,4096]{1,0:T(8,128)(2,1)S(1)} %constant_dynamic-update-slice_fusion.low_ref, bf16[32,4096]{1,0:T(8,128)(2,1)S(1)} %collective-permute-done.10.high_ref, bf16[4096,512]{1,0:T(8,128)(2,1)S(1)} %copy-done.2), custom_call_target="tpu_custom_call" | custom-call | flops 268435456 | bytes 6291456 | tf_op jit(solution)/shard_map/project_out/pallas_call | solution.py:238
  65.6 0.1 collective-permute-start.11
  65.7 0.8 %project_out.2.mine_ref = f32[64,512]{1,0:T(8,128)S(1)} custom-call(bf16[32,4096]{1,0:T(8,128)(2,1)S(1)} %constant_dynamic-update-slice_fusion.low_ref, bf16[32,4096]{1,0:T(8,128)(2,1)S(1)} %collective-permute-done.10.high_ref, bf16[4096,512]{1,0:T(8,128)(2,1)S(1)} %dequantize.7.weight_ref), custom_call_target="tpu_custom_call" | custom-call | flops 268435456 | bytes 6291456 | tf_op jit(solution)/shard_map/project_out/pallas_call | solution.py:238
  66.5 0.5 collective-permute-done.11.theirs_ref
  67.0 0.6 sum_halves.1
  67.6 12.3 %all_to_all.5.pieces_ref = bf16[16,8,512]{2,1,0:T(8,128)(2,1)S(1)} all-to-all(bf16[16,8,512]{2,1,0:T(8,128)(2,1)S(1)} %sum_halves.1), channel_id=1, replica_groups=mesh['rep'=2,'wide'=8,'tensor'=2] {'wide','tensor'}, dimensions={0} | all-to-all | bytes 262144 | tf_op jit(solution)/shard_map/all_to_all | solution.py:540
  79.9 0.7 join_columns.1
  (33 shorter events, 0.2 us)
Async XLA Ops:
  0.0 46.8 %copy-start = (bf16[8,64,512]{2,1,0:T(8,128)(2,1)S(1)}, bf16[8,64,512]{2,1,0:T(8,128)(2,1)}, u32[]{:S(2)}) copy-start(bf16[8,64,512]{2,1,0:T(8,128)(2,1)} %param.26) | copy-start | bytes 1572868
  0.9 7.7 %collective-permute-start = (bf16[8,4096]{1,0:T(8,128)(2,1)S(1)}, bf16[8,4096]{1,0:T(8,128)(2,1)S(1)}, u32[]{:S(2)}, u32[]{:S(2)}) collective-permute-start(bf16[8,4096]{1,0:T(8,128)(2,1)S(1)} %constant_dynamic-slice_fusion), channel_id=1, source_target_pairs={{0,8},{2,10},{4,12},{6,14},{8,0},{10,2},{12,4},{14,6},{1,9},{3,11}... | collective-permute-start | bytes 196616 | tf_op jit(solution)/shard_map/ppermute | solution.py:437
  8.6 5.0 %collective-permute-start.1 = (bf16[16,4096]{1,0:T(8,128)(2,1)S(1)}, bf16[16,4096]{1,0:T(8,128)(2,1)S(1)}, u32[]{:S(2)}, u32[]{:S(2)}) collective-permute-start(bf16[16,4096]{1,0:T(8,128)(2,1)S(1)} %pad_maximum_fusion.1), channel_id=1, source_target_pairs={{0,4},{2,6},{4,0},{6,2},{8,12},{10,14},{12,8},{14,10},{1,5},{3,7},... | collective-permute-start | bytes 393224 | tf_op jit(solution)/shard_map/ppermute | solution.py:437
  9.3 0.9 %copy-start.5 = (f32[128,512]{1,0:T(8,128)S(1)}, f32[128,512]{1,0:T(8,128)}, u32[]{:S(2)}) copy-start(f32[128,512]{1,0:T(8,128)} %scales_ref.5) | copy-start | bytes 786436
  10.3 5.3 %copy-start.11 = (s32[64]{0:T(128)S(1)}, s32[64]{0:T(128)}, u32[]{:S(2)}) copy-start(s32[64]{0:T(128)} %param.22) | copy-start | bytes 772
  10.3 5.5 %copy-start.12 = (s32[48]{0:T(128)S(1)}, s32[48]{0:T(128)}, u32[]{:S(2)}) copy-start(s32[48]{0:T(128)} %param.23) | copy-start | bytes 580
  10.3 5.7 %copy-start.6 = (f32[128,512]{1,0:T(8,128)S(1)}, f32[128,512]{1,0:T(8,128)}, u32[]{:S(2)}) copy-start(f32[128,512]{1,0:T(8,128)} %scales_ref.5) | copy-start | bytes 786436
  13.7 8.2 %collective-permute-start.3 = (bf16[32,4096]{1,0:T(8,128)(2,1)S(1)}, bf16[32,4096]{1,0:T(8,128)(2,1)S(1)}, u32[]{:S(2)}, u32[]{:S(2)}) collective-permute-start(bf16[32,4096]{1,0:T(8,128)(2,1)S(1)} %pad_maximum_fusion.low), channel_id=1, source_target_pairs={{0,2},{2,0},{4,6},{6,4},{8,10},{10,8},{12,14},{14,12},{1,3},{3,1},... | collective-permute-start | bytes 786440 | tf_op jit(solution)/shard_map/ppermute | solution.py:437
  15.9 6.5 %copy-start.3 = (bf16[8192,6,32]{0,2,1:T(8,128)(2,1)S(1)}, bf16[8192,6,32]{0,2,1:T(8,128)(2,1)}, u32[]{:S(2)}) copy-start(bf16[8192,6,32]{0,2,1:T(8,128)(2,1)} %param.20) | copy-start | bytes 9437188
  15.9 8.2 %collective-permute-start.2 = (bf16[32,4096]{1,0:T(8,128)(2,1)S(1)}, bf16[32,4096]{1,0:T(8,128)(2,1)S(1)}, u32[]{:S(2)}, u32[]{:S(2)}) collective-permute-start(bf16[32,4096]{1,0:T(8,128)(2,1)S(1)} %pad_maximum_fusion.low), channel_id=1, source_target_pairs={{0,1},{1,0},{2,3},{3,2},{4,5},{5,4},{6,7},{7,6},{8,9},{9,8},{10,11... | collective-permute-start | bytes 786440 | tf_op jit(solution)/shard_map/ppermute | solution.py:440
  21.8 2.3 %collective-permute-start.4 = (bf16[32,4096]{1,0:T(8,128)(2,1)S(1)}, bf16[32,4096]{1,0:T(8,128)(2,1)S(1)}, u32[]{:S(2)}, u32[]{:S(2)}) collective-permute-start(bf16[32,4096]{1,0:T(8,128)(2,1)S(1)} %collective-permute-done.3.high), channel_id=1, source_target_pairs={{0,1},{1,0},{2,3},{3,2},{4,5},{5,4},{6,7},{7,6},{8,9},{9,8},{10,11... | collective-permute-start | bytes 786440 | tf_op jit(solution)/shard_map/ppermute | solution.py:440
  22.4 1.8 %copy-start.4 = (bf16[6,32,4096]{2,1,0:T(8,128)(2,1)S(1)}, bf16[6,32,4096]{2,1,0:T(8,128)(2,1)}, u32[]{:S(2)}) copy-start(bf16[6,32,4096]{2,1,0:T(8,128)(2,1)} %param.21) | copy-start | bytes 4718596
  24.2 2.6 %copy-start.7 = (f32[64,1024]{1,0:T(8,128)S(1)}, f32[64,1024]{1,0:T(8,128)}, u32[]{:S(2)}) copy-start(f32[64,1024]{1,0:T(8,128)} %scales_ref.7) | copy-start | bytes 786436
  26.3 8.5 %collective-permute-start.5 = (bf16[32,4096]{1,0:T(8,128)(2,1)S(1)}, bf16[32,4096]{1,0:T(8,128)(2,1)S(1)}, u32[]{:S(2)}, u32[]{:S(2)}) collective-permute-start(bf16[32,4096]{1,0:T(8,128)(2,1)S(1)} %get-tuple-element.30), channel_id=1, source_target_pairs={{0,2},{2,0},{4,6},{6,4},{8,10},{10,8},{12,14},{14,12},{1,3},{3,1},... | collective-permute-start | bytes 786440 | tf_op jit(solution)/shard_map/ppermute | solution.py:437
  26.8 9.3 %copy-start.9 = (bf16[8,512]{1,0:T(8,128)(2,1)S(1)}, bf16[8,512]{1,0:T(8,128)(2,1)}, u32[]{:S(2)}) copy-start(bf16[8,512]{1,0:T(8,128)(2,1)} %param.28) | copy-start | bytes 24580
  26.8 16.1 %copy-start.13 = (s32[8]{0:T(128)S(1)}, s32[8]{0:T(128)}, u32[]{:S(2)}) copy-start(s32[8]{0:T(128)} %param.24) | copy-start | bytes 100
  26.8 19.1 %copy-start.10 = (bf16[8,512]{1,0:T(8,128)(2,1)S(1)}, bf16[8,512]{1,0:T(8,128)(2,1)}, u32[]{:S(2)}) copy-start(bf16[8,512]{1,0:T(8,128)(2,1)} %param.27) | copy-start | bytes 24580
  26.8 19.3 %copy-start.8 = (bf16[8,64,512]{2,1,0:T(8,128)(2,1)S(1)}, bf16[8,64,512]{2,1,0:T(8,128)(2,1)}, u32[]{:S(2)}) copy-start(bf16[8,64,512]{2,1,0:T(8,128)(2,1)} %param.25) | copy-start | bytes 1572868
  31.2 2.0 %copy-start.1 = (bf16[4096,512]{1,0:T(8,128)(2,1)}, bf16[4096,512]{1,0:T(8,128)(2,1)S(1)}, u32[]{:S(2)}) copy-start(bf16[4096,512]{1,0:T(8,128)(2,1)S(1)} %dequantize.6.weight_ref) | copy-start | bytes 12582916
  34.9 5.0 %collective-permute-start.6 = (bf16[16,4096]{1,0:T(8,128)(2,1)S(1)}, bf16[16,4096]{1,0:T(8,128)(2,1)S(1)}, u32[]{:S(2)}, u32[]{:S(2)}) collective-permute-start(bf16[16,4096]{1,0:T(8,128)(2,1)S(1)} %slice.17), channel_id=1, source_target_pairs={{0,4},{2,6},{4,0},{6,2},{8,12},{10,14},{12,8},{14,10},{1,5},{3,7},... | collective-permute-start | bytes 393224 | tf_op jit(solution)/shard_map/ppermute | solution.py:437
  40.0 5.9 %collective-permute-start.7 = (bf16[8,4096]{1,0:T(8,128)(2,1)S(1)}, bf16[8,4096]{1,0:T(8,128)(2,1)S(1)}, u32[]{:S(2)}, u32[]{:S(2)}) collective-permute-start(bf16[8,4096]{1,0:T(8,128)(2,1)S(1)} %slice.19), channel_id=1, source_target_pairs={{0,8},{2,10},{4,12},{6,14},{8,0},{10,2},{12,4},{14,6},{1,9},{3,11}... | collective-permute-start | bytes 196616 | tf_op jit(solution)/shard_map/ppermute | solution.py:437
  47.2 6.0 %collective-permute-start.8 = (bf16[8,4096]{1,0:T(8,128)(2,1)S(1)}, bf16[8,4096]{1,0:T(8,128)(2,1)S(1)}, u32[]{:S(2)}, u32[]{:S(2)}) collective-permute-start(bf16[8,4096]{1,0:T(8,128)(2,1)S(1)} %bitcast.62), channel_id=1, source_target_pairs={{0,8},{2,10},{4,12},{6,14},{8,0},{10,2},{12,4},{14,6},{1,9},{3,11}... | collective-permute-start | bytes 196616 | tf_op jit(solution)/shard_map/ppermute | solution.py:437
  53.2 5.0 %collective-permute-start.9 = (bf16[16,4096]{1,0:T(8,128)(2,1)S(1)}, bf16[16,4096]{1,0:T(8,128)(2,1)S(1)}, u32[]{:S(2)}, u32[]{:S(2)}) collective-permute-start(bf16[16,4096]{1,0:T(8,128)(2,1)S(1)} %pad_maximum_fusion.2), channel_id=1, source_target_pairs={{0,4},{2,6},{4,0},{6,2},{8,12},{10,14},{12,8},{14,10},{1,5},{3,7},... | collective-permute-start | bytes 393224 | tf_op jit(solution)/shard_map/ppermute | solution.py:437
  58.3 6.4 %collective-permute-start.10 = (bf16[32,4096]{1,0:T(8,128)(2,1)S(1)}, bf16[32,4096]{1,0:T(8,128)(2,1)S(1)}, u32[]{:S(2)}, u32[]{:S(2)}) collective-permute-start(bf16[32,4096]{1,0:T(8,128)(2,1)S(1)} %constant_dynamic-update-slice_fusion.low_ref), channel_id=1, source_target_pairs={{0,2},{2,0},{4,6},{6,4},{8,10},{10,8},{12,14},{14,12},{1,3},{3,1},... | collective-permute-start | bytes 786440 | tf_op jit(solution)/shard_map/ppermute | solution.py:437
  58.7 6.0 %copy-start.2 = (bf16[4096,512]{1,0:T(8,128)(2,1)S(1)}, bf16[4096,512]{1,0:T(8,128)(2,1)}, u32[]{:S(2)}) copy-start(bf16[4096,512]{1,0:T(8,128)(2,1)} %copy-done.1) | copy-start | bytes 12582916
  65.6 1.4 %collective-permute-start.11 = (f32[64,512]{1,0:T(8,128)S(1)}, f32[64,512]{1,0:T(8,128)S(1)}, u32[]{:S(2)}, u32[]{:S(2)}) collective-permute-start(f32[64,512]{1,0:T(8,128)S(1)} %project_out.3), channel_id=1, source_target_pairs={{0,1},{1,0},{2,3},{3,2},{4,5},{5,4},{6,7},{7,6},{8,9},{9,8},{10,11... | collective-permute-start | bytes 393224 | tf_op jit(solution)/shard_map/ppermute | solution.py:440

commit v3 on v2

--- a/solution.py
+++ b/solution.py
@@ -134,28 +134,26 @@
 LAST = (((1,), (1,)), ((), ()))
 
 
-def project_own(place, own, first_weight, rest_weight, down):
+def project_own(place, own, weight, down):
     count = own[0].shape[0] * 2
     half = own[0].shape[1]
-    cut, query_width = first_weight.shape
-
-    def kernel(place_ref, low, high, first_ref, rest_ref, down_ref, query_ref, rank_ref):
+    query_width = weight.shape[1]
+
+    def kernel(place_ref, low, high, weight_ref, down_ref, query_ref, rank_ref):
         rows = jnp.concatenate([low[...], high[...]], axis=0)
         here = pl.ds(pl.multiple_of(place_ref[1] * half, half), half)
         rank_ref[...] = lax.dot_general(
-            rows, down_ref[:, here], LAST, preferred_element_type=jnp.float32
-        )
-        query_ref[...] = jnp.dot(
-            rows[:, :cut], first_ref[...], preferred_element_type=jnp.float32
-        ) + jnp.dot(rows[:, cut:], rest_ref[: half - cut], preferred_element_type=jnp.float32)
+            down_ref[:, here], rows, LAST, preferred_element_type=jnp.float32
+        )
+        query_ref[...] = jnp.dot(rows, weight_ref[...], preferred_element_type=jnp.float32)
 
     return pl.pallas_call(
         kernel,
-        in_specs=[SMEM] + [VMEM] * 5,
+        in_specs=[SMEM] + [VMEM] * 4,
         out_specs=[VMEM, VMEM],
         out_shape=[
             jax.ShapeDtypeStruct((count, query_width), jnp.float32),
-            jax.ShapeDtypeStruct((count, down.shape[0]), jnp.float32),
+            jax.ShapeDtypeStruct((down.shape[0], count), jnp.float32),
         ],
         compiler_params=pltpu.CompilerParams(vmem_limit_bytes=24 * MIB),
         cost_estimate=pl.CostEstimate(
@@ -164,13 +162,13 @@
             transcendentals=0,
         ),
         name="project_own",
-    )(place, *own, first_weight, rest_weight, down)
-
-
-def project_other(place, other, rest_weight, down, query_mine, rank_mine, keep_rank, up):
+    )(place, *own, weight, down)
+
+
+def project_other(place, other, weight, down, query_mine, rank_mine, keep_rank, up):
     count = other[0].shape[0] * 2
     half = other[0].shape[1]
-    query_width = rest_weight.shape[1]
+    query_width = weight.shape[1]
     width = up.shape[1]
     chunk = 512
 
@@ -178,7 +176,7 @@
         place_ref,
         low,
         high,
-        rest_ref,
+        weight_ref,
         down_ref,
         query_ref,
         rank_ref,
@@ -190,11 +188,11 @@
         rows = jnp.concatenate([low[...], high[...]], axis=0)
         there = pl.ds(pl.multiple_of((1 - place_ref[1]) * half, half), half)
         ranks = rank_ref[...] + lax.dot_general(
-            rows, down_ref[:, there], LAST, preferred_element_type=jnp.float32
-        )
-        terms = jnp.where(keep_ref[...] != 0, ranks, 0.0).astype(jnp.bfloat16)
+            down_ref[:, there], rows, LAST, preferred_element_type=jnp.float32
+        )
+        terms = jnp.where(keep_ref[...] != 0, ranks.T, 0.0).astype(jnp.bfloat16)
         query = query_ref[...] + jnp.dot(
-            rows, rest_ref[rest_ref.shape[0] - half :], preferred_element_type=jnp.float32
+            rows, weight_ref[...], preferred_element_type=jnp.float32
         )
         base = query.astype(jnp.bfloat16).astype(jnp.float32)
         for lane in range(0, width, chunk):
@@ -225,7 +223,7 @@
             transcendentals=0,
         ),
         name="project_other",
-    )(place, *other, rest_weight, down, query_mine, rank_mine, keep_rank, up)
+    )(place, *other, weight, down, query_mine, rank_mine, keep_rank, up)
 
 
 def project_out(low, high, weight):
@@ -420,11 +418,7 @@
 ):
     rows_dev, model_width = tokens.shape
     half = model_width // 2
-    rounds = wide.bit_length() - 1
-    offsets = np.zeros(wide, np.int32)
-    for number in range(rounds):
-        for at in range(wide):
-            offsets[at] |= ((at >> number) & 1) << (rounds - 1 - number)
+    offsets = np.array([far * 2 + near for near in range(2) for far in range(wide // 2)], np.int32)
 
     me = lax.axis_index("wide").astype(jnp.int32)
     core = lax.axis_index("tensor").astype(jnp.int32)
@@ -432,72 +426,44 @@
     place = jnp.stack([me, core])
     targets = me ^ offsets
 
-    def swap(array, number):
-        bit = 1 << (rounds - 1 - number)
-        return lax.ppermute(array, "wide", [(peer, peer ^ bit) for peer in range(wide)])
+    def swap(array, offset):
+        return lax.ppermute(array, "wide", [(peer, peer ^ offset) for peer in range(wide)])
 
     def cross(array):
         return lax.ppermute(array, "tensor", [(0, 1), (1, 0)])
 
     def beside(work, sent, received):
-        if work is None:
-            return received, None
         return lax.optimization_barrier((received, work(sent)))
 
-    def gather_rows(array, works):
-        made = []
-        for number in range(rounds):
-            work = works.get(rounds - 1 - number)
-            received, result = beside(work, array, swap(array, number))
-            made.append(result)
-            if number < rounds - 1:
-                array = jnp.concatenate([array, received], axis=0)
-        return (array, received), made[::-1]
+    far_offsets = range(2, wide, 2)
 
     query_width = query_quant_codes.shape[1]
     out_height, out_width = output_quant_codes.shape
     out_half = out_width // 2
-    cut = half // 2
-    own_row, other_row = core * half, (1 - core) * half
-
-    def query_first(sent):
-        return dequantize_part(
-            query_quant_codes,
-            query_absmax_scale,
-            [(own_row, cut)],
-            zero,
-            query_width,
-            50,
-            sent,
-        )
-
-    def query_rest(sent):
-        return dequantize_part(
-            query_quant_codes,
-            query_absmax_scale,
-            [(own_row + cut, half - cut), (other_row, half)],
-            zero,
-            query_width,
-            46,
-            sent,
-        )
-
-    def out_part(column):
+
+    def query_part(row, room):
+        return lambda sent: dequantize_part(
+            query_quant_codes, query_absmax_scale, [(row, half)], zero, query_width, room, sent
+        )
+
+    def out_part(column, room):
         return lambda sent: dequantize_part(
             output_quant_codes,
             output_absmax_scale,
             [(zero, out_height)],
             column,
             out_half,
-            47,
+            room,
             sent,
         )
 
-    own, made = gather_rows(
-        lax.dynamic_slice(tokens, (0, core * half), (rows_dev, half)),
-        {1: query_first, 0: query_rest},
-    )
-    rest_weight, first_weight = made[:2]
+    block = lax.dynamic_slice(tokens, (0, core * half), (rows_dev, half))
+    arrived, weight_own = beside(
+        query_part(core * half, 50), block, [swap(block, offset) for offset in far_offsets]
+    )
+    low = jnp.concatenate([block] + arrived, axis=0)
+    high, weight_other = beside(query_part((1 - core) * half, 48), low, swap(low, 1))
+    own = (low, high)
     other = [cross(part) for part in own]
 
     owned, rank = adapter_down_maps.shape[1:]
@@ -511,30 +477,32 @@
 
     down = adapter_down_maps.transpose(1, 2, 0).reshape(owned * rank, model_width)
     up = adapter_up_maps.reshape(owned * rank, adapter_up_maps.shape[2])
-    query_mine, rank_mine = project_own(place, own, first_weight, rest_weight, down)
+    query_mine, rank_mine = project_own(place, own, weight_own, down)
     stay, leave = project_other(
-        place, other, rest_weight, down, query_mine, rank_mine, keep_rank, up
-    )
-
-    out_leave = None
-    for number in range(rounds)[::-1]:
-        work = out_part((1 - core) * out_half) if number == rounds - 1 else None
-        received, result = beside(work, leave, swap(leave, number))
-        out_leave = out_leave if result is None else result
-        total = stay + received
-        keep = total.shape[0] // 2
-        stay, leave = total[:keep], total[keep:]
+        place, other, weight_other, down, query_mine, rank_mine, keep_rank, up
+    )
+
+    received, out_leave = beside(out_part((1 - core) * out_half, 46), leave, swap(leave, 1))
+    stay = stay + received
+    blocks = [stay[at : at + rows_dev] for at in range(0, stay.shape[0], rows_dev)]
+    arrived, out_stay = beside(
+        out_part(core * out_half, 44),
+        stay,
+        [swap(part, offset) for part, offset in zip(blocks[1:], far_offsets)],
+    )
+    query_vector = sum(arrived, blocks[0])
 
     context = attend(
-        total,
+        query_vector,
         row_cache_length,
         stored_key_cache,
         stored_value_cache,
         fresh_token_key,
         fresh_token_value,
     )
-    (low, high), made = gather_rows(context, {0: out_part(core * out_half)})
-    out_stay = made[0]
+    arrived = [context] + [swap(context, offset) for offset in far_offsets]
+    low = jnp.concatenate(arrived, axis=0)
+    high = jnp.concatenate([swap(part, 1) for part in arrived], axis=0)
     theirs = cross(project_out(low, high, out_leave))
     mine = project_out(low, high, out_stay)
     routed = lax.all_to_all(sum_halves(targets, mine, theirs), ("wide", "tensor"), 0, 0)

time: 80.7 us -> 75.7 us (0.938)
  waiting for transfers between devices: 22.1 us -> 9.34 us
  starting transfers between devices: 14.3 us -> 21.8 us
  blocking collectives: 12.3 us -> 10.6 us
  local copies, waits for them, and re-layouts: 4.37 us -> 6.05 us
    ppermute x9 -> x15, waiting for transfers between devices: 21.7 us -> 8.85 us  [swap(): lax.ppermute(array, 'wide', [(peer, peer ^ offset) for peer in range(wide)])]
    ppermute x9 -> x15, starting transfers between devices: 13.8 us -> 21.7 us  [swap(): lax.ppermute(array, 'wide', [(peer, peer ^ offset) for peer in range(wide)])]
    all_to_all x1, blocking collectives: 12.3 us -> 10.6 us  [fast(): lax.all_to_all(sum_halves(targets, mine, theirs), ('wide', 'tensor'), 0, 0)]
    unnamed x31 -> x37, local copies, waits for them, and re-layouts: 3.01 us -> 4.19 us
  transfers between devices with their start and end apart: 12 -> 18, of which waited for: 9 -> 8; matrix products, arithmetic and copies ran while one was open for 2% -> 3% of each run, Pallas kernels for 25% -> 27%
where the time goes in v3:
time: 75.7 us; the launch traced here: 75.5 us
  Pallas kernels  24.7 us (33%)
  starting transfers between devices  21.8 us (29%)
  blocking collectives  10.6 us (14%)
  waiting for transfers between devices  9.34 us (12%)
  local copies, waits for them, and re-layouts  6.05 us (8%)
  other arithmetic  1.59 us (2%)
  matrix products  0.95 us (1%)
    ppermute x15, starting transfers between devices, swap(): lax.ppermute(array, 'wide', [(peer, peer ^ offset) for peer in range(wide)])  21.7 us
    pallas_call x4, Pallas kernels, dequantize_part(): pl.pallas_call(kernel, in_specs=[SMEM, ANY, ANY], out_specs=VMEM, out_sha...  17.9 us
    all_to_all x1, blocking collectives, fast(): lax.all_to_all(sum_halves(targets, mine, theirs), ('wide', 'tensor'), 0, 0)  10.6 us
    ppermute x15, waiting for transfers between devices, swap(): lax.ppermute(array, 'wide', [(peer, peer ^ offset) for peer in range(wide)])  8.85 us
    unnamed x37, local copies, waits for them, and re-layouts  4.19 us
    pallas_call x1, Pallas kernels, project_other(): pl.pallas_call(kernel, in_specs=[SMEM] + [VMEM] * 8, out_specs=[VMEM, VME...  2.11 us
    pallas_call x1, Pallas kernels, project_own(): pl.pallas_call(kernel, in_specs=[SMEM] + [VMEM] * 4, out_specs=[VMEM, VME...  1.77 us
    pallas_call x2, Pallas kernels, project_out(): pl.pallas_call(kernel, in_specs=[VMEM] * 3, out_specs=VMEM, out_shape=jax...  1.68 us
  transfers between devices with their start and end apart: 18, of which 8 were waited for; matrix products, arithmetic and copies ran while one was open for 3% of the time, Pallas kernels for 27%

profile of v3, /device:TPU:0, one launch (start us, length us, event | category | flops | bytes accessed | tf_op | source)
XLA Modules:
  0.0 75.5 jit_solution(7398406386966538252)
XLA Ops:
  0.0 0.9 %constant_dynamic-slice_fusion = bf16[8,4096]{1,0:T(8,128)(2,1)S(1)} fusion(bf16[8,8192]{1,0:T(8,128)(2,1)} %param.15, s32[]{:T(128)S(6)} %select_n.24), kind=kLoop, calls=%fused_computation.51 | loop fusion | bytes 131076 | tf_op jit(solution)/shard_map/dynamic_slice | solution.py:460
  0.9 3.0 %collective-permute-start = (bf16[8,4096]{1,0:T(8,128)(2,1)S(1)}, bf16[8,4096]{1,0:T(8,128)(2,1)S(1)}, u32[]{:S(2)}, u32[]{:S(2)}) collective-permute-start(bf16[8,4096]{1,0:T(8,128)(2,1)S(1)} %constant_dynamic-slice_fusion), channel_id=1, source_target_pairs={{0,4},{2,6},{4,0},{6,2},{8,12},{10,14},{12,8},{14,10},{1,5},{3,7},... | collective-permute-start | bytes 196616 | tf_op jit(solution)/shard_map/ppermute | solution.py:430
  3.9 2.6 %collective-permute-start.1 = (bf16[8,4096]{1,0:T(8,128)(2,1)S(1)}, bf16[8,4096]{1,0:T(8,128)(2,1)S(1)}, u32[]{:S(2)}, u32[]{:S(2)}) collective-permute-start(bf16[8,4096]{1,0:T(8,128)(2,1)S(1)} %constant_dynamic-slice_fusion), channel_id=1, source_target_pairs={{0,8},{2,10},{4,12},{6,14},{8,0},{10,2},{12,4},{14,6},{1,9},{3,11}... | collective-permute-start | bytes 196616 | tf_op jit(solution)/shard_map/ppermute | solution.py:430
  6.5 0.0 collective-permute-start.2
  6.5 0.7 broadcast_multiply_fusion
  7.2 0.1 iota_add_fusion
  7.3 0.6 stack.86.starts_ref
  7.9 4.6 %dequantize.4.weight_ref = bf16[4096,512]{1,0:T(8,128)(2,1)S(1)} custom-call(s32[9]{0:T(128)} %stack.86.starts_ref, s32[8192,512]{1,0:T(8,128)} %codes_ref.5, f32[128,512]{1,0:T(8,128)} %scales_ref.5), custom_call_target="tpu_custom_call" | custom-call | flops 4194304 | bytes 12582912 | tf_op jit(solution)/shard_map/dequantize/pallas_call | solution.py:115
  12.5 1.9 %copy-done.3 = bf16[4096,512]{1,0:T(8,128)(2,1)} copy-done((bf16[4096,512]{1,0:T(8,128)(2,1)}, bf16[4096,512]{1,0:T(8,128)(2,1)S(1)}, u32[]{:S(2)}) %copy-start.3) | copy-done | bytes 4194328
  14.5 1.8 %collective-permute-start.4 = (bf16[32,4096]{1,0:T(8,128)(2,1)S(1)}, bf16[32,4096]{1,0:T(8,128)(2,1)S(1)}, u32[]{:S(2)}, u32[]{:S(2)}) collective-permute-start(bf16[32,4096]{1,0:T(8,128)(2,1)S(1)} %pad_maximum_fusion.low), channel_id=1, source_target_pairs={{0,2},{2,0},{4,6},{6,4},{8,10},{10,8},{12,14},{14,12},{1,3},{3,1},... | collective-permute-start | bytes 786440 | tf_op jit(solution)/shard_map/ppermute | solution.py:430
  16.2 0.1 add.118
  16.3 0.1 stack.95.starts_ref
  16.4 0.2 select_reduce_fusion
  16.6 0.1 select_reduce_fusion.1
  16.7 0.0 copy-start.5
  16.7 0.1 collective-permute-start.3
  16.8 4.6 %dequantize.5.weight_ref = bf16[4096,512]{1,0:T(8,128)(2,1)S(1)} custom-call(s32[9]{0:T(128)S(1)} %stack.95.starts_ref, s32[8192,512]{1,0:T(8,128)} %codes_ref.5, f32[128,512]{1,0:T(8,128)S(1)} %copy-done.7), custom_call_target="tpu_custom_call" | custom-call | flops 4194304 | bytes 12582912 | tf_op jit(solution)/shard_map/dequantize/pallas_call | solution.py:115
  21.4 0.0 copy-start.6
  21.4 0.6 collective-permute-done.4.high
  22.0 0.1 pad_add_fusion.place_ref
  22.1 0.1 compare_convert_fusion.keep_ref
  22.2 0.0 copy-done.4
  22.2 0.2 copy-done.5
  22.3 1.8 %project_own.1 = (f32[64,512]{1,0:T(8,128)S(1)}, f32[192,64]{1,0:T(8,128)S(1)}) custom-call(s32[2]{0:T(128)S(1)} %pad_add_fusion.place_ref, bf16[32,4096]{1,0:T(8,128)(2,1)S(1)} %pad_maximum_fusion.low, bf16[32,4096]{1,0:T(8,128)(2,1)S(1)} %collective-permute-done.4.high, bf16[4096,512]{1,0:T(8,128)(2,1)S(1)} %copy-done.4, bf16[192,8192]{1,0:T(8,128)(2,1)S(1)} %bitcast.57), custom_call_target="tpu_custom_call" | custom-call | flops 369098752 | bytes 7340032 | tf_op jit(solution)/shard_map/project_own/pallas_call | solution.py:150
  24.1 0.0 copy-start.10
  24.2 0.0 copy-start.8
  24.2 2.1 %project_other.1 = (bf16[32,4096]{1,0:T(8,128)(2,1)S(1)}, bf16[32,4096]{1,0:T(8,128)(2,1)S(1)}) custom-call(s32[2]{0:T(128)S(1)} %pad_add_fusion.place_ref, bf16[32,4096]{1,0:T(8,128)(2,1)S(1)} %collective-permute-done.3.low, bf16[32,4096]{1,0:T(8,128)(2,1)S(1)} %collective-permute-done.5.high, bf16[4096,512]{1,0:T(8,128)(2,1)S(1)} %dequantize.5.weight_ref, ...), custom_call_target="tpu_custom_call" | custom-call | flops 469762048 | bytes 8388608 | tf_op jit(solution)/shard_map/project_other/pallas_call | solution.py:214
  26.3 1.4 %collective-permute-start.6 = (bf16[32,4096]{1,0:T(8,128)(2,1)S(1)}, bf16[32,4096]{1,0:T(8,128)(2,1)S(1)}, u32[]{:S(2)}, u32[]{:S(2)}) collective-permute-start(bf16[32,4096]{1,0:T(8,128)(2,1)S(1)} %get-tuple-element.36), channel_id=1, source_target_pairs={{0,2},{2,0},{4,6},{6,4},{8,10},{10,8},{12,14},{14,12},{1,3},{3,1},... | collective-permute-start | bytes 786440 | tf_op jit(solution)/shard_map/ppermute | solution.py:430
  27.7 0.1 stack.97.starts_ref
  27.8 0.0 copy-start.14
  27.8 4.3 %dequantize.6.weight_ref = bf16[4096,512]{1,0:T(8,128)(2,1)S(1)} custom-call(s32[9]{0:T(128)S(1)} %stack.97.starts_ref, s32[4096,1024]{1,0:T(8,128)} %codes_ref.7, f32[64,1024]{1,0:T(8,128)S(1)} %copy-done.8), custom_call_target="tpu_custom_call" | custom-call | flops 4194304 | bytes 12582912 | tf_op jit(solution)/shard_map/dequantize/pallas_call | solution.py:115
  32.2 1.9 %copy-done.1 = bf16[4096,512]{1,0:T(8,128)(2,1)} copy-done((bf16[4096,512]{1,0:T(8,128)(2,1)}, bf16[4096,512]{1,0:T(8,128)(2,1)S(1)}, u32[]{:S(2)}) %copy-start.1) | copy-done | bytes 4194328
  34.1 0.8 %collective-permute-done.6 = bf16[32,4096]{1,0:T(8,128)(2,1)S(1)} collective-permute-done((bf16[32,4096]{1,0:T(8,128)(2,1)S(1)}, bf16[32,4096]{1,0:T(8,128)(2,1)S(1)}, u32[]{:S(2)}, u32[]{:S(2)}) %collective-permute-start.6) | collective-permute-done | bytes 262176 | tf_op jit(solution)/shard_map/ppermute | solution.py:430
  34.9 0.1 add.119
  35.0 0.7 collective-permute-start.7
  35.7 3.5 %collective-permute-start.8 = (bf16[8,4096]{1,0:T(8,128)(2,1)S(1)}, bf16[8,4096]{1,0:T(8,128)(2,1)S(1)}, u32[]{:S(2)}, u32[]{:S(2)}) collective-permute-start(bf16[8,4096]{1,0:T(8,128)(2,1)S(1)} %get-tuple-element.46), channel_id=1, source_target_pairs={{0,8},{2,10},{4,12},{6,14},{8,0},{10,2},{12,4},{14,6},{1,9},{3,11}... | collective-permute-start | bytes 196616 | tf_op jit(solution)/shard_map/ppermute | solution.py:430
  39.2 0.3 collective-permute-start.9
  39.5 0.1 iota_compare_fusion.2
  39.5 0.1 stack.99.starts_ref
  39.6 0.0 copy-start.11
  39.6 0.0 copy-start.9
  39.7 4.3 %dequantize.7.weight_ref = bf16[4096,512]{1,0:T(8,128)(2,1)S(1)} custom-call(s32[9]{0:T(128)S(1)} %stack.99.starts_ref, s32[4096,1024]{1,0:T(8,128)} %codes_ref.7, f32[64,1024]{1,0:T(8,128)S(1)} %copy-done.8), custom_call_target="tpu_custom_call" | custom-call | flops 4194304 | bytes 12582912 | tf_op jit(solution)/shard_map/dequantize/pallas_call | solution.py:115
  44.0 1.2 %collective-permute-done.9 = bf16[8,4096]{1,0:T(8,128)(2,1)S(1)} collective-permute-done((bf16[8,4096]{1,0:T(8,128)(2,1)S(1)}, bf16[8,4096]{1,0:T(8,128)(2,1)S(1)}, u32[]{:S(2)}, u32[]{:S(2)}) %collective-permute-start.9) | collective-permute-done | bytes 65568 | tf_op jit(solution)/shard_map/ppermute | solution.py:430
  45.3 0.2 fusion.12
  45.5 0.5 fusion.20
  45.9 0.2 fusion.7
  46.2 0.3 fusion.2
  46.6 1.6 %collective-permute-start.13 = (bf16[8,4096]{1,0:T(8,128)(2,1)S(1)}, bf16[8,4096]{1,0:T(8,128)(2,1)S(1)}, u32[]{:S(2)}, u32[]{:S(2)}) collective-permute-start(bf16[8,4096]{1,0:T(8,128)(2,1)S(1)} %bitcast.64), channel_id=1, source_target_pairs={{0,2},{2,0},{4,6},{6,4},{8,10},{10,8},{12,14},{14,12},{1,3},{3,1},... | collective-permute-start | bytes 196616 | tf_op jit(solution)/shard_map/ppermute | solution.py:430
  48.1 2.9 %collective-permute-start.11 = (bf16[8,4096]{1,0:T(8,128)(2,1)S(1)}, bf16[8,4096]{1,0:T(8,128)(2,1)S(1)}, u32[]{:S(2)}, u32[]{:S(2)}) collective-permute-start(bf16[8,4096]{1,0:T(8,128)(2,1)S(1)} %bitcast.66), channel_id=1, source_target_pairs={{0,8},{2,10},{4,12},{6,14},{8,0},{10,2},{12,4},{14,6},{1,9},{3,11}... | collective-permute-start | bytes 196616 | tf_op jit(solution)/shard_map/ppermute | solution.py:430
  51.0 1.5 %collective-permute-start.12 = (bf16[8,4096]{1,0:T(8,128)(2,1)S(1)}, bf16[8,4096]{1,0:T(8,128)(2,1)S(1)}, u32[]{:S(2)}, u32[]{:S(2)}) collective-permute-start(bf16[8,4096]{1,0:T(8,128)(2,1)S(1)} %bitcast.67), channel_id=1, source_target_pairs={{0,12},{2,14},{4,8},{6,10},{8,4},{10,6},{12,0},{14,2},{1,13},{3,15... | collective-permute-start | bytes 196616 | tf_op jit(solution)/shard_map/ppermute | solution.py:430
  52.6 0.6 collective-permute-start.14
  53.2 0.1 collective-permute-done.11
  53.3 1.4 %collective-permute-start.15 = (bf16[8,4096]{1,0:T(8,128)(2,1)S(1)}, bf16[8,4096]{1,0:T(8,128)(2,1)S(1)}, u32[]{:S(2)}, u32[]{:S(2)}) collective-permute-start(bf16[8,4096]{1,0:T(8,128)(2,1)S(1)} %collective-permute-done.11), channel_id=1, source_target_pairs={{0,2},{2,0},{4,6},{6,4},{8,10},{10,8},{12,14},{14,12},{1,3},{3,1},... | collective-permute-start | bytes 196616 | tf_op jit(solution)/shard_map/ppermute | solution.py:430
  54.7 2.4 %collective-permute-done.12 = bf16[8,4096]{1,0:T(8,128)(2,1)S(1)} collective-permute-done((bf16[8,4096]{1,0:T(8,128)(2,1)S(1)}, bf16[8,4096]{1,0:T(8,128)(2,1)S(1)}, u32[]{:S(2)}, u32[]{:S(2)}) %collective-permute-start.12) | collective-permute-done | bytes 65568 | tf_op jit(solution)/shard_map/ppermute | solution.py:430
  57.1 0.5 collective-permute-start.16
  57.7 0.6 collective-permute-done.15
  58.3 3.1 %collective-permute-done.16 = bf16[8,4096]{1,0:T(8,128)(2,1)S(1)} collective-permute-done((bf16[8,4096]{1,0:T(8,128)(2,1)S(1)}, bf16[8,4096]{1,0:T(8,128)(2,1)S(1)}, u32[]{:S(2)}, u32[]{:S(2)}) %collective-permute-start.16) | collective-permute-done | bytes 65568 | tf_op jit(solution)/shard_map/ppermute | solution.py:430
  61.4 0.8 %project_out.3 = f32[64,512]{1,0:T(8,128)S(1)} custom-call(bf16[32,4096]{1,0:T(8,128)(2,1)S(1)} %constant_dynamic-update-slice_fusion.low_ref, bf16[32,4096]{1,0:T(8,128)(2,1)S(1)} %constant_dynamic-update-slice_fusion.4.high_ref, bf16[4096,512]{1,0:T(8,128)(2,1)S(1)} %copy-done.2), custom_call_target="tpu_custom_call" | custom-call | flops 268435456 | bytes 6291456 | tf_op jit(solution)/shard_map/project_out/pallas_call | solution.py:236
  62.2 0.1 collective-permute-start.17
  62.3 0.8 %project_out.2.mine_ref = f32[64,512]{1,0:T(8,128)S(1)} custom-call(bf16[32,4096]{1,0:T(8,128)(2,1)S(1)} %constant_dynamic-update-slice_fusion.low_ref, bf16[32,4096]{1,0:T(8,128)(2,1)S(1)} %constant_dynamic-update-slice_fusion.4.high_ref, bf16[4096,512]{1,0:T(8,128)(2,1)S(1)} %dequantize.7.weight_ref), custom_call_target="tpu_custom_call" | custom-call | flops 268435456 | bytes 6291456 | tf_op jit(solution)/shard_map/project_out/pallas_call | solution.py:236
  63.1 0.5 collective-permute-done.17.theirs_ref
  63.6 0.6 sum_halves.1
  64.2 10.6 %all_to_all.5.pieces_ref = bf16[16,8,512]{2,1,0:T(8,128)(2,1)S(1)} all-to-all(bf16[16,8,512]{2,1,0:T(8,128)(2,1)S(1)} %sum_halves.1), channel_id=1, replica_groups=mesh['rep'=2,'wide'=8,'tensor'=2] {'wide','tensor'}, dimensions={0} | all-to-all | bytes 262144 | tf_op jit(solution)/shard_map/all_to_all | solution.py:508
  74.8 0.7 join_columns.1
  (48 shorter events, 0.3 us)
Async XLA Ops:
  0.0 46.2 %copy-start = (bf16[8,64,512]{2,1,0:T(8,128)(2,1)S(1)}, bf16[8,64,512]{2,1,0:T(8,128)(2,1)}, u32[]{:S(2)}) copy-start(bf16[8,64,512]{2,1,0:T(8,128)(2,1)} %param.26) | copy-start | bytes 1572868
  0.9 13.5 %collective-permute-start = (bf16[8,4096]{1,0:T(8,128)(2,1)S(1)}, bf16[8,4096]{1,0:T(8,128)(2,1)S(1)}, u32[]{:S(2)}, u32[]{:S(2)}) collective-permute-start(bf16[8,4096]{1,0:T(8,128)(2,1)S(1)} %constant_dynamic-slice_fusion), channel_id=1, source_target_pairs={{0,4},{2,6},{4,0},{6,2},{8,12},{10,14},{12,8},{14,10},{1,5},{3,7},... | collective-permute-start | bytes 196616 | tf_op jit(solution)/shard_map/ppermute | solution.py:430
  3.9 10.5 %collective-permute-start.1 = (bf16[8,4096]{1,0:T(8,128)(2,1)S(1)}, bf16[8,4096]{1,0:T(8,128)(2,1)S(1)}, u32[]{:S(2)}, u32[]{:S(2)}) collective-permute-start(bf16[8,4096]{1,0:T(8,128)(2,1)S(1)} %constant_dynamic-slice_fusion), channel_id=1, source_target_pairs={{0,8},{2,10},{4,12},{6,14},{8,0},{10,2},{12,4},{14,6},{1,9},{3,11}... | collective-permute-start | bytes 196616 | tf_op jit(solution)/shard_map/ppermute | solution.py:430
  6.5 7.9 %collective-permute-start.2 = (bf16[8,4096]{1,0:T(8,128)(2,1)S(1)}, bf16[8,4096]{1,0:T(8,128)(2,1)S(1)}, u32[]{:S(2)}, u32[]{:S(2)}) collective-permute-start(bf16[8,4096]{1,0:T(8,128)(2,1)S(1)} %constant_dynamic-slice_fusion), channel_id=1, source_target_pairs={{0,12},{2,14},{4,8},{6,10},{8,4},{10,6},{12,0},{14,2},{1,13},{3,15... | collective-permute-start | bytes 196616 | tf_op jit(solution)/shard_map/ppermute | solution.py:430
  7.9 8.6 %copy-start.12 = (s32[64]{0:T(128)S(1)}, s32[64]{0:T(128)}, u32[]{:S(2)}) copy-start(s32[64]{0:T(128)} %param.22) | copy-start | bytes 772
  7.9 8.7 %copy-start.13 = (s32[48]{0:T(128)S(1)}, s32[48]{0:T(128)}, u32[]{:S(2)}) copy-start(s32[48]{0:T(128)} %param.23) | copy-start | bytes 580
  7.9 8.9 %copy-start.7 = (f32[128,512]{1,0:T(8,128)S(1)}, f32[128,512]{1,0:T(8,128)}, u32[]{:S(2)}) copy-start(f32[128,512]{1,0:T(8,128)} %scales_ref.5) | copy-start | bytes 786436
  12.5 2.0 %copy-start.3 = (bf16[4096,512]{1,0:T(8,128)(2,1)}, bf16[4096,512]{1,0:T(8,128)(2,1)S(1)}, u32[]{:S(2)}) copy-start(bf16[4096,512]{1,0:T(8,128)(2,1)S(1)} %dequantize.4.weight_ref) | copy-start | bytes 12582916
  14.5 7.6 %collective-permute-start.4 = (bf16[32,4096]{1,0:T(8,128)(2,1)S(1)}, bf16[32,4096]{1,0:T(8,128)(2,1)S(1)}, u32[]{:S(2)}, u32[]{:S(2)}) collective-permute-start(bf16[32,4096]{1,0:T(8,128)(2,1)S(1)} %pad_maximum_fusion.low), channel_id=1, source_target_pairs={{0,2},{2,0},{4,6},{6,4},{8,10},{10,8},{12,14},{14,12},{1,3},{3,1},... | collective-permute-start | bytes 786440 | tf_op jit(solution)/shard_map/ppermute | solution.py:430
  16.7 5.5 %copy-start.4 = (bf16[4096,512]{1,0:T(8,128)(2,1)S(1)}, bf16[4096,512]{1,0:T(8,128)(2,1)}, u32[]{:S(2)}) copy-start(bf16[4096,512]{1,0:T(8,128)(2,1)} %copy-done.3) | copy-start | bytes 12582916
  16.7 5.6 %copy-start.5 = (bf16[8192,6,32]{0,2,1:T(8,128)(2,1)S(1)}, bf16[8192,6,32]{0,2,1:T(8,128)(2,1)}, u32[]{:S(2)}) copy-start(bf16[8192,6,32]{0,2,1:T(8,128)(2,1)} %param.20) | copy-start | bytes 9437188
  16.7 7.4 %collective-permute-start.3 = (bf16[32,4096]{1,0:T(8,128)(2,1)S(1)}, bf16[32,4096]{1,0:T(8,128)(2,1)S(1)}, u32[]{:S(2)}, u32[]{:S(2)}) collective-permute-start(bf16[32,4096]{1,0:T(8,128)(2,1)S(1)} %pad_maximum_fusion.low), channel_id=1, source_target_pairs={{0,1},{1,0},{2,3},{3,2},{4,5},{5,4},{6,7},{7,6},{8,9},{9,8},{10,11... | collective-permute-start | bytes 786440 | tf_op jit(solution)/shard_map/ppermute | solution.py:433
  21.4 2.7 %copy-start.6 = (bf16[6,32,4096]{2,1,0:T(8,128)(2,1)S(1)}, bf16[6,32,4096]{2,1,0:T(8,128)(2,1)}, u32[]{:S(2)}) copy-start(bf16[6,32,4096]{2,1,0:T(8,128)(2,1)} %param.21) | copy-start | bytes 4718596
  22.0 2.1 %collective-permute-start.5 = (bf16[32,4096]{1,0:T(8,128)(2,1)S(1)}, bf16[32,4096]{1,0:T(8,128)(2,1)S(1)}, u32[]{:S(2)}, u32[]{:S(2)}) collective-permute-start(bf16[32,4096]{1,0:T(8,128)(2,1)S(1)} %collective-permute-done.4.high), channel_id=1, source_target_pairs={{0,1},{1,0},{2,3},{3,2},{4,5},{5,4},{6,7},{7,6},{8,9},{9,8},{10,11... | collective-permute-start | bytes 786440 | tf_op jit(solution)/shard_map/ppermute | solution.py:433
  24.1 3.6 %copy-start.10 = (bf16[8,512]{1,0:T(8,128)(2,1)S(1)}, bf16[8,512]{1,0:T(8,128)(2,1)}, u32[]{:S(2)}) copy-start(bf16[8,512]{1,0:T(8,128)(2,1)} %param.28) | copy-start | bytes 24580
  24.2 3.6 %copy-start.8 = (f32[64,1024]{1,0:T(8,128)S(1)}, f32[64,1024]{1,0:T(8,128)}, u32[]{:S(2)}) copy-start(f32[64,1024]{1,0:T(8,128)} %scales_ref.7) | copy-start | bytes 786436
  26.3 8.6 %collective-permute-start.6 = (bf16[32,4096]{1,0:T(8,128)(2,1)S(1)}, bf16[32,4096]{1,0:T(8,128)(2,1)S(1)}, u32[]{:S(2)}, u32[]{:S(2)}) collective-permute-start(bf16[32,4096]{1,0:T(8,128)(2,1)S(1)} %get-tuple-element.36), channel_id=1, source_target_pairs={{0,2},{2,0},{4,6},{6,4},{8,10},{10,8},{12,14},{14,12},{1,3},{3,1},... | collective-permute-start | bytes 786440 | tf_op jit(solution)/shard_map/ppermute | solution.py:430
  27.8 11.7 %copy-start.14 = (s32[8]{0:T(128)S(1)}, s32[8]{0:T(128)}, u32[]{:S(2)}) copy-start(s32[8]{0:T(128)} %param.24) | copy-start | bytes 100
  32.2 2.0 %copy-start.1 = (bf16[4096,512]{1,0:T(8,128)(2,1)}, bf16[4096,512]{1,0:T(8,128)(2,1)S(1)}, u32[]{:S(2)}) copy-start(bf16[4096,512]{1,0:T(8,128)(2,1)S(1)} %dequantize.6.weight_ref) | copy-start | bytes 12582916
  35.0 9.0 %collective-permute-start.7 = (bf16[8,4096]{1,0:T(8,128)(2,1)S(1)}, bf16[8,4096]{1,0:T(8,128)(2,1)S(1)}, u32[]{:S(2)}, u32[]{:S(2)}) collective-permute-start(bf16[8,4096]{1,0:T(8,128)(2,1)S(1)} %get-tuple-element.47), channel_id=1, source_target_pairs={{0,4},{2,6},{4,0},{6,2},{8,12},{10,14},{12,8},{14,10},{1,5},{3,7},... | collective-permute-start | bytes 196616 | tf_op jit(solution)/shard_map/ppermute | solution.py:430
  35.7 8.3 %collective-permute-start.8 = (bf16[8,4096]{1,0:T(8,128)(2,1)S(1)}, bf16[8,4096]{1,0:T(8,128)(2,1)S(1)}, u32[]{:S(2)}, u32[]{:S(2)}) collective-permute-start(bf16[8,4096]{1,0:T(8,128)(2,1)S(1)} %get-tuple-element.46), channel_id=1, source_target_pairs={{0,8},{2,10},{4,12},{6,14},{8,0},{10,2},{12,4},{14,6},{1,9},{3,11}... | collective-permute-start | bytes 196616 | tf_op jit(solution)/shard_map/ppermute | solution.py:430
  39.2 6.1 %collective-permute-start.9 = (bf16[8,4096]{1,0:T(8,128)(2,1)S(1)}, bf16[8,4096]{1,0:T(8,128)(2,1)S(1)}, u32[]{:S(2)}, u32[]{:S(2)}) collective-permute-start(bf16[8,4096]{1,0:T(8,128)(2,1)S(1)} %get-tuple-element.45), channel_id=1, source_target_pairs={{0,12},{2,14},{4,8},{6,10},{8,4},{10,6},{12,0},{14,2},{1,13},{3,15... | collective-permute-start | bytes 196616 | tf_op jit(solution)/shard_map/ppermute | solution.py:430
  39.6 5.6 %copy-start.11 = (bf16[8,512]{1,0:T(8,128)(2,1)S(1)}, bf16[8,512]{1,0:T(8,128)(2,1)}, u32[]{:S(2)}) copy-start(bf16[8,512]{1,0:T(8,128)(2,1)} %param.27) | copy-start | bytes 24580
  39.6 5.8 %copy-start.9 = (bf16[8,64,512]{2,1,0:T(8,128)(2,1)S(1)}, bf16[8,64,512]{2,1,0:T(8,128)(2,1)}, u32[]{:S(2)}) copy-start(bf16[8,64,512]{2,1,0:T(8,128)(2,1)} %param.25) | copy-start | bytes 1572868
  44.0 17.4 %copy-start.2 = (bf16[4096,512]{1,0:T(8,128)(2,1)S(1)}, bf16[4096,512]{1,0:T(8,128)(2,1)}, u32[]{:S(2)}) copy-start(bf16[4096,512]{1,0:T(8,128)(2,1)} %copy-done.1) | copy-start | bytes 12582916
  46.6 6.0 %collective-permute-start.13 = (bf16[8,4096]{1,0:T(8,128)(2,1)S(1)}, bf16[8,4096]{1,0:T(8,128)(2,1)S(1)}, u32[]{:S(2)}, u32[]{:S(2)}) collective-permute-start(bf16[8,4096]{1,0:T(8,128)(2,1)S(1)} %bitcast.64), channel_id=1, source_target_pairs={{0,2},{2,0},{4,6},{6,4},{8,10},{10,8},{12,14},{14,12},{1,3},{3,1},... | collective-permute-start | bytes 196616 | tf_op jit(solution)/shard_map/ppermute | solution.py:430
  48.1 4.4 %collective-permute-start.10 = (bf16[8,4096]{1,0:T(8,128)(2,1)S(1)}, bf16[8,4096]{1,0:T(8,128)(2,1)S(1)}, u32[]{:S(2)}, u32[]{:S(2)}) collective-permute-start(bf16[8,4096]{1,0:T(8,128)(2,1)S(1)} %bitcast.65), channel_id=1, source_target_pairs={{0,4},{2,6},{4,0},{6,2},{8,12},{10,14},{12,8},{14,10},{1,5},{3,7},... | collective-permute-start | bytes 196616 | tf_op jit(solution)/shard_map/ppermute | solution.py:430
  48.1 5.2 %collective-permute-start.11 = (bf16[8,4096]{1,0:T(8,128)(2,1)S(1)}, bf16[8,4096]{1,0:T(8,128)(2,1)S(1)}, u32[]{:S(2)}, u32[]{:S(2)}) collective-permute-start(bf16[8,4096]{1,0:T(8,128)(2,1)S(1)} %bitcast.66), channel_id=1, source_target_pairs={{0,8},{2,10},{4,12},{6,14},{8,0},{10,2},{12,4},{14,6},{1,9},{3,11}... | collective-permute-start | bytes 196616 | tf_op jit(solution)/shard_map/ppermute | solution.py:430
  51.0 6.1 %collective-permute-start.12 = (bf16[8,4096]{1,0:T(8,128)(2,1)S(1)}, bf16[8,4096]{1,0:T(8,128)(2,1)S(1)}, u32[]{:S(2)}, u32[]{:S(2)}) collective-permute-start(bf16[8,4096]{1,0:T(8,128)(2,1)S(1)} %bitcast.67), channel_id=1, source_target_pairs={{0,12},{2,14},{4,8},{6,10},{8,4},{10,6},{12,0},{14,2},{1,13},{3,15... | collective-permute-start | bytes 196616 | tf_op jit(solution)/shard_map/ppermute | solution.py:430
  52.6 5.1 %collective-permute-start.14 = (bf16[8,4096]{1,0:T(8,128)(2,1)S(1)}, bf16[8,4096]{1,0:T(8,128)(2,1)S(1)}, u32[]{:S(2)}, u32[]{:S(2)}) collective-permute-start(bf16[8,4096]{1,0:T(8,128)(2,1)S(1)} %collective-permute-done.10), channel_id=1, source_target_pairs={{0,2},{2,0},{4,6},{6,4},{8,10},{10,8},{12,14},{14,12},{1,3},{3,1},... | collective-permute-start | bytes 196616 | tf_op jit(solution)/shard_map/ppermute | solution.py:430
  53.3 5.0 %collective-permute-start.15 = (bf16[8,4096]{1,0:T(8,128)(2,1)S(1)}, bf16[8,4096]{1,0:T(8,128)(2,1)S(1)}, u32[]{:S(2)}, u32[]{:S(2)}) collective-permute-start(bf16[8,4096]{1,0:T(8,128)(2,1)S(1)} %collective-permute-done.11), channel_id=1, source_target_pairs={{0,2},{2,0},{4,6},{6,4},{8,10},{10,8},{12,14},{14,12},{1,3},{3,1},... | collective-permute-start | bytes 196616 | tf_op jit(solution)/shard_map/ppermute | solution.py:430
  57.1 4.3 %collective-permute-start.16 = (bf16[8,4096]{1,0:T(8,128)(2,1)S(1)}, bf16[8,4096]{1,0:T(8,128)(2,1)S(1)}, u32[]{:S(2)}, u32[]{:S(2)}) collective-permute-start(bf16[8,4096]{1,0:T(8,128)(2,1)S(1)} %collective-permute-done.12), channel_id=1, source_target_pairs={{0,2},{2,0},{4,6},{6,4},{8,10},{10,8},{12,14},{14,12},{1,3},{3,1},... | collective-permute-start | bytes 196616 | tf_op jit(solution)/shard_map/ppermute | solution.py:430
  62.2 1.4 %collective-permute-start.17 = (f32[64,512]{1,0:T(8,128)S(1)}, f32[64,512]{1,0:T(8,128)S(1)}, u32[]{:S(2)}, u32[]{:S(2)}) collective-permute-start(f32[64,512]{1,0:T(8,128)S(1)} %project_out.3), channel_id=1, source_target_pairs={{0,1},{1,0},{2,3},{3,2},{4,5},{5,4},{6,7},{7,6},{8,9},{9,8},{10,11... | collective-permute-start | bytes 393224 | tf_op jit(solution)/shard_map/ppermute | solution.py:433

commit v4 on v3

--- a/solution.py
+++ b/solution.py
@@ -55,53 +55,33 @@
     return blocks.reshape(height, breadth).astype(jnp.bfloat16)
 
 
-def dequantize_part(codes, scales, segments, column, breadth, room, sent):
+def dequantize_all(place, codes, scales, halves):
     chunk = 512
-    height = sum(rows for _, rows in segments)
-    steps = height // chunk
+    height, breadth = codes.shape
     blocks = chunk // QBLOCK
-    starts = [first + at for first, rows in segments for at in range(0, rows, chunk)]
-    starts, _ = lax.optimization_barrier((jnp.stack([column] + starts).astype(jnp.int32), sent))
-
-    def kernel(starts_ref, codes_ref, scales_ref, out_ref, held, factors, arrived, factors_arrived):
-        columns = pl.ds(pl.multiple_of(starts_ref[0], LANES), breadth)
-
-        def fetch(step):
-            return pltpu.make_async_copy(
-                codes_ref.at[pl.ds(pl.multiple_of(starts_ref[step + 1], chunk), chunk), columns],
-                held.at[pl.ds(pl.multiple_of(step * chunk, chunk), chunk)],
-                arrived.at[step],
-            )
-
-        def fetch_factors(step):
-            first = pl.multiple_of(starts_ref[step + 1] // QBLOCK, blocks)
-            return pltpu.make_async_copy(
-                scales_ref.at[pl.ds(first, blocks), columns],
-                factors.at[pl.ds(pl.multiple_of(step * blocks, blocks), blocks)],
-                factors_arrived.at[step],
-            )
-
-        for step in range(steps):
-            fetch_factors(step).start()
-            fetch(step).start()
+    parts = 2 if halves else 1
+    width = breadth // parts
+
+    def kernel(place_ref, codes_ref, scales_ref, out_ref):
         number = lax.broadcasted_iota(jnp.int32, (16, LANES), 0)
         table = jnp.zeros((16, LANES), jnp.float32)
         for code, level in enumerate(NF4_LEVELS):
             table = jnp.where(number == code, level, table)
 
         def work(step, carry):
-            fetch_factors(step).wait()
-            fetch(step).wait()
             for lane in range(0, breadth, LANES):
-                group = factors[
+                part = lane // width
+                place_in = (part + 1 + place_ref[1]) % 2 if halves else 0
+                group = scales_ref[
                     pl.ds(pl.multiple_of(step * blocks, blocks), blocks), lane : lane + LANES
                 ]
                 for block in range(blocks):
                     products = (table * group[block : block + 1]).astype(jnp.bfloat16)
                     at = pl.multiple_of(step * chunk + block * QBLOCK, QBLOCK)
-                    numbers = held[pl.ds(at, QBLOCK), lane : lane + LANES].astype(jnp.int16)
+                    numbers = codes_ref[pl.ds(at, QBLOCK), lane : lane + LANES].astype(jnp.int16)
+                    to = lane - part * width
                     for piece in range(0, QBLOCK, 16):
-                        out_ref[pl.ds(at + piece, 16), lane : lane + LANES] = lax.gather(
+                        out_ref[place_in, pl.ds(at + piece, 16), to : to + LANES] = lax.gather(
                             products,
                             numbers[piece : piece + 16][..., None],
                             LOOKUP,
@@ -110,66 +90,98 @@
                         )
             return carry
 
-        lax.fori_loop(0, steps, work, 0)
-
-    return pl.pallas_call(
-        kernel,
-        in_specs=[SMEM, ANY, ANY],
+        lax.fori_loop(0, height // chunk, work, 0)
+
+    return pl.pallas_call(
+        kernel,
+        in_specs=[SMEM, VMEM, VMEM],
         out_specs=VMEM,
-        out_shape=pltpu.VMEM((height, breadth), jnp.bfloat16),
-        scratch_shapes=[
-            pltpu.VMEM((height, breadth), jnp.int32),
-            pltpu.VMEM((height // QBLOCK, breadth), jnp.float32),
-            pltpu.SemaphoreType.DMA((steps,)),
-            pltpu.SemaphoreType.DMA((steps,)),
-        ],
-        compiler_params=pltpu.CompilerParams(vmem_limit_bytes=room * MIB),
+        out_shape=pltpu.VMEM((parts, height, width), jnp.bfloat16),
+        compiler_params=pltpu.CompilerParams(vmem_limit_bytes=2 * MIB),
         cost_estimate=pl.CostEstimate(
             flops=2 * height * breadth, bytes_accessed=6 * height * breadth, transcendentals=0
         ),
         name="dequantize",
-    )(starts, codes, scales)
+    )(place, codes, scales)
+
+
+def begin_gather(place, block):
+    def kernel(place_ref, block_ref, out_ref):
+        out_ref[...] = block_ref[...]
+
+    return pl.pallas_call(
+        kernel,
+        in_specs=[SMEM, VMEM],
+        out_specs=VMEM,
+        out_shape=pltpu.VMEM(block.shape, block.dtype),
+        compiler_params=pltpu.CompilerParams(vmem_limit_bytes=2 * MIB),
+        cost_estimate=pl.CostEstimate(
+            flops=6_000_000_000, bytes_accessed=4 * block.size, transcendentals=0
+        ),
+        name="begin_gather",
+    )(place, block)
 
 
 LAST = (((1,), (1,)), ((), ()))
 
 
-def project_own(place, own, weight, down):
+def project_own(place, offsets, row_adapter_index, adapter_storage_slot, own, weight, down):
     count = own[0].shape[0] * 2
     half = own[0].shape[1]
-    query_width = weight.shape[1]
-
-    def kernel(place_ref, low, high, weight_ref, down_ref, query_ref, rank_ref):
+    query_width = weight.shape[2]
+    block = count // len(offsets)
+
+    def kernel(
+        place_ref,
+        adapters_ref,
+        storage_ref,
+        low,
+        high,
+        weight_ref,
+        down_ref,
+        query_ref,
+        rank_ref,
+        slots_ref,
+    ):
         rows = jnp.concatenate([low[...], high[...]], axis=0)
         here = pl.ds(pl.multiple_of(place_ref[1] * half, half), half)
         rank_ref[...] = lax.dot_general(
             down_ref[:, here], rows, LAST, preferred_element_type=jnp.float32
         )
-        query_ref[...] = jnp.dot(rows, weight_ref[...], preferred_element_type=jnp.float32)
-
-    return pl.pallas_call(
-        kernel,
-        in_specs=[SMEM] + [VMEM] * 4,
-        out_specs=[VMEM, VMEM],
+        query_ref[...] = jnp.dot(rows, weight_ref[0, here], preferred_element_type=jnp.float32)
+        column = lax.broadcasted_iota(jnp.int32, slots_ref.shape, 1)
+        slots = jnp.zeros(slots_ref.shape, jnp.int32)
+        for row in range(count):
+            source = (place_ref[0] ^ int(offsets[row // block])) * block + row % block
+            slots = jnp.where(column == row, storage_ref[adapters_ref[source]], slots)
+        slots_ref[...] = slots
+
+    return pl.pallas_call(
+        kernel,
+        in_specs=[SMEM] * 3 + [VMEM] * 4,
+        out_specs=[VMEM] * 3,
         out_shape=[
             jax.ShapeDtypeStruct((count, query_width), jnp.float32),
             jax.ShapeDtypeStruct((down.shape[0], count), jnp.float32),
+            jax.ShapeDtypeStruct((8, count), jnp.int32),
         ],
-        compiler_params=pltpu.CompilerParams(vmem_limit_bytes=24 * MIB),
+        compiler_params=pltpu.CompilerParams(vmem_limit_bytes=4 * MIB),
         cost_estimate=pl.CostEstimate(
             flops=2 * count * half * (query_width + down.shape[0]),
             bytes_accessed=7 * MIB,
             transcendentals=0,
         ),
         name="project_own",
-    )(place, *own, weight, down)
-
-
-def project_other(place, other, weight, down, query_mine, rank_mine, keep_rank, up):
+    )(place, row_adapter_index, adapter_storage_slot, *own, weight, down)
+
+
+def project_other(place, other, weight, down, query_mine, rank_mine, slots, owned, up):
     count = other[0].shape[0] * 2
     half = other[0].shape[1]
-    query_width = weight.shape[1]
+    query_width = weight.shape[2]
     width = up.shape[1]
+    rank = up.shape[0] // owned
+    part = count // 4
     chunk = 512
 
     def kernel(
@@ -180,19 +192,23 @@
         down_ref,
         query_ref,
         rank_ref,
-        keep_ref,
+        slots_ref,
         up_ref,
-        stay_ref,
-        leave_ref,
+        *out_refs,
     ):
         rows = jnp.concatenate([low[...], high[...]], axis=0)
         there = pl.ds(pl.multiple_of((1 - place_ref[1]) * half, half), half)
         ranks = rank_ref[...] + lax.dot_general(
             down_ref[:, there], rows, LAST, preferred_element_type=jnp.float32
         )
-        terms = jnp.where(keep_ref[...] != 0, ranks.T, 0.0).astype(jnp.bfloat16)
+        slot = slots_ref[:1]
+        kept = [
+            jnp.where(slot == place_ref[0] * owned + number, ranks[at : at + rank], 0.0)
+            for number, at in enumerate(range(0, owned * rank, rank))
+        ]
+        terms = jnp.concatenate(kept, axis=0).T.astype(jnp.bfloat16)
         query = query_ref[...] + jnp.dot(
-            rows, weight_ref[...], preferred_element_type=jnp.float32
+            rows, weight_ref[0, there], preferred_element_type=jnp.float32
         )
         base = query.astype(jnp.bfloat16).astype(jnp.float32)
         for lane in range(0, width, chunk):
@@ -200,63 +216,61 @@
                 terms, up_ref[:, lane : lane + chunk], preferred_element_type=jnp.float32
             ).astype(jnp.bfloat16)
             scaled = (ADAPTER_SCALE * delta.astype(jnp.float32)).astype(jnp.bfloat16)
-            stay_ref[:, lane : lane + chunk] = scaled[: count // 2]
-            leave_ref[:, lane : lane + chunk] = scaled[count // 2 :]
+            for number, out_ref in enumerate(out_refs):
+                out_ref[:, lane : lane + chunk] = scaled[number * part : (number + 1) * part]
         here = pl.ds(pl.multiple_of(place_ref[0] * query_width, query_width), query_width)
-        stay_ref[:, here] = (base[: count // 2] + stay_ref[:, here].astype(jnp.float32)).astype(
-            jnp.bfloat16
-        )
-        leave_ref[:, here] = (base[count // 2 :] + leave_ref[:, here].astype(jnp.float32)).astype(
-            jnp.bfloat16
-        )
-
-    shape = jax.ShapeDtypeStruct((count // 2, width), jnp.bfloat16)
+        for number, out_ref in enumerate(out_refs):
+            rows_base = base[number * part : (number + 1) * part]
+            out_ref[:, here] = (rows_base + out_ref[:, here].astype(jnp.float32)).astype(
+                jnp.bfloat16
+            )
+
+    shape = jax.ShapeDtypeStruct((part, width), jnp.bfloat16)
     return pl.pallas_call(
         kernel,
         in_specs=[SMEM] + [VMEM] * 8,
-        out_specs=[VMEM, VMEM],
-        out_shape=[shape, shape],
-        compiler_params=pltpu.CompilerParams(vmem_limit_bytes=24 * MIB),
+        out_specs=[VMEM] * 4,
+        out_shape=[shape] * 4,
+        compiler_params=pltpu.CompilerParams(vmem_limit_bytes=4 * MIB),
         cost_estimate=pl.CostEstimate(
             flops=2 * count * (half * (query_width + up.shape[0]) + up.shape[0] * width),
             bytes_accessed=8 * MIB,
             transcendentals=0,
         ),
         name="project_other",
-    )(place, *other, weight, down, query_mine, rank_mine, keep_rank, up)
-
-
-def project_out(low, high, weight):
+    )(place, *other, weight, down, query_mine, rank_mine, slots, up)
+
+
+def project_out(low, high, weight, part):
     count = low.shape[0] * 2
+    _, height, breadth = weight.shape
 
     def kernel(low_ref, high_ref, weight_ref, out_ref):
         rows = jnp.concatenate([low_ref[...], high_ref[...]], axis=0)
-        out_ref[...] = jnp.dot(rows, weight_ref[...], preferred_element_type=jnp.float32)
+        out_ref[...] = jnp.dot(rows, weight_ref[part], preferred_element_type=jnp.float32)
 
     return pl.pallas_call(
         kernel,
         in_specs=[VMEM] * 3,
         out_specs=VMEM,
-        out_shape=jax.ShapeDtypeStruct((count, weight.shape[1]), jnp.float32),
-        compiler_params=pltpu.CompilerParams(vmem_limit_bytes=12 * MIB),
+        out_shape=jax.ShapeDtypeStruct((count, breadth), jnp.float32),
+        compiler_params=pltpu.CompilerParams(vmem_limit_bytes=4 * MIB),
         cost_estimate=pl.CostEstimate(
-            flops=2 * count * weight.shape[0] * weight.shape[1],
-            bytes_accessed=6 * MIB,
-            transcendentals=0,
+            flops=2 * count * height * breadth, bytes_accessed=6 * MIB, transcendentals=0
         ),
         name="project_out",
     )(low, high, weight)
 
 
-def sum_halves(targets, mine, theirs):
+def sum_halves(place, offsets, mine, theirs):
     block = 8
     count, width = mine.shape
 
-    def kernel(targets_ref, mine_ref, theirs_ref, out_ref):
-        for at in range(0, count, block):
+    def kernel(place_ref, mine_ref, theirs_ref, out_ref):
+        for number, at in enumerate(range(0, count, block)):
             rows = (mine_ref[at : at + block] + theirs_ref[at : at + block]).astype(jnp.bfloat16)
             for side in range(2):
-                out_ref[targets_ref[at // block] * 2 + side] = rows
+                out_ref[(place_ref[0] ^ int(offsets[number])) * 2 + side] = rows
 
     return pl.pallas_call(
         kernel,
@@ -265,7 +279,7 @@
         out_shape=jax.ShapeDtypeStruct((count // block * 2, block, width), jnp.bfloat16),
         compiler_params=pltpu.CompilerParams(vmem_limit_bytes=4 * MIB),
         name="sum_halves",
-    )(targets, mine, theirs)
+    )(place, mine, theirs)
 
 
 def join_columns(pieces):
@@ -422,9 +436,7 @@
 
     me = lax.axis_index("wide").astype(jnp.int32)
     core = lax.axis_index("tensor").astype(jnp.int32)
-    zero = jnp.int32(0)
     place = jnp.stack([me, core])
-    targets = me ^ offsets
 
     def swap(array, offset):
         return lax.ppermute(array, "wide", [(peer, peer ^ offset) for peer in range(wide)])
@@ -432,65 +444,43 @@
     def cross(array):
         return lax.ppermute(array, "tensor", [(0, 1), (1, 0)])
 
-    def beside(work, sent, received):
-        return lax.optimization_barrier((received, work(sent)))
-
     far_offsets = range(2, wide, 2)
 
-    query_width = query_quant_codes.shape[1]
-    out_height, out_width = output_quant_codes.shape
-    out_half = out_width // 2
-
-    def query_part(row, room):
-        return lambda sent: dequantize_part(
-            query_quant_codes, query_absmax_scale, [(row, half)], zero, query_width, room, sent
-        )
-
-    def out_part(column, room):
-        return lambda sent: dequantize_part(
-            output_quant_codes,
-            output_absmax_scale,
-            [(zero, out_height)],
-            column,
-            out_half,
-            room,
-            sent,
-        )
-
     block = lax.dynamic_slice(tokens, (0, core * half), (rows_dev, half))
-    arrived, weight_own = beside(
-        query_part(core * half, 50), block, [swap(block, offset) for offset in far_offsets]
-    )
-    low = jnp.concatenate([block] + arrived, axis=0)
-    high, weight_other = beside(query_part((1 - core) * half, 48), low, swap(low, 1))
+    block = begin_gather(place, block)
+    blocks = [block] + [swap(block, offset) for offset in far_offsets]
+    query_weight = dequantize_all(place, query_quant_codes, query_absmax_scale, False)
+    blocks[1:] = [lax.optimization_barrier((part, query_weight))[0] for part in blocks[1:]]
+    low = jnp.concatenate(blocks, axis=0)
+    high = jnp.concatenate([swap(part, 1) for part in blocks], axis=0)
     own = (low, high)
     other = [cross(part) for part in own]
 
     owned, rank = adapter_down_maps.shape[1:]
-    all_rows = (targets[:, None] * rows_dev + jnp.arange(rows_dev)[None, :]).reshape(-1)
-    picked = all_rows[:, None] == jnp.arange(all_rows.shape[0])[None, :]
-    adapters = jnp.sum(jnp.where(picked, row_adapter_index[None, :], 0), axis=1)
-    matches = adapters[:, None] == jnp.arange(adapter_storage_slot.shape[0])[None, :]
-    slots = jnp.sum(jnp.where(matches, adapter_storage_slot[None, :], 0), axis=1)
-    rank_owner = jnp.arange(owned * rank) // rank + me * owned
-    keep_rank = (rank_owner[None, :] == slots[:, None]).astype(jnp.int32)
-
     down = adapter_down_maps.transpose(1, 2, 0).reshape(owned * rank, model_width)
     up = adapter_up_maps.reshape(owned * rank, adapter_up_maps.shape[2])
-    query_mine, rank_mine = project_own(place, own, weight_own, down)
-    stay, leave = project_other(
-        place, other, weight_other, down, query_mine, rank_mine, keep_rank, up
-    )
-
-    received, out_leave = beside(out_part((1 - core) * out_half, 46), leave, swap(leave, 1))
-    stay = stay + received
-    blocks = [stay[at : at + rows_dev] for at in range(0, stay.shape[0], rows_dev)]
-    arrived, out_stay = beside(
-        out_part(core * out_half, 44),
-        stay,
-        [swap(part, offset) for part, offset in zip(blocks[1:], far_offsets)],
-    )
-    query_vector = sum(arrived, blocks[0])
+    query_mine, rank_mine, slots = project_own(
+        place, offsets, row_adapter_index, adapter_storage_slot, own, query_weight, down
+    )
+    stay_low, stay_high, leave_low, leave_high = project_other(
+        place, other, query_weight, down, query_mine, rank_mine, slots, owned, up
+    )
+
+    received_high, received_low = swap(leave_high, 1), swap(leave_low, 1)
+    place, _ = lax.optimization_barrier((place, leave_high))
+    output_weight = dequantize_all(place, output_quant_codes, output_absmax_scale, True)
+    received_high, _ = lax.optimization_barrier((received_high, output_weight))
+    received_low, _ = lax.optimization_barrier((received_low, output_weight))
+
+    def blocks_of(array):
+        return [array[at : at + rows_dev] for at in range(0, array.shape[0], rows_dev)]
+
+    high_blocks = blocks_of(stay_high + received_high)
+    middle = len(high_blocks)
+    sums = [swap(part, offset) for part, offset in zip(high_blocks, far_offsets[middle - 1 :])]
+    low_blocks = blocks_of(stay_low + received_low)
+    sums += [swap(part, offset) for part, offset in zip(low_blocks[1:], far_offsets)]
+    query_vector = sum(sums, low_blocks[0])
 
     context = attend(
         query_vector,
@@ -500,12 +490,12 @@
         fresh_token_key,
         fresh_token_value,
     )
-    arrived = [context] + [swap(context, offset) for offset in far_offsets]
+    arrived = [context] + [swap(context, offset) for offset in far_offsets[::-1]][::-1]
     low = jnp.concatenate(arrived, axis=0)
     high = jnp.concatenate([swap(part, 1) for part in arrived], axis=0)
-    theirs = cross(project_out(low, high, out_leave))
-    mine = project_out(low, high, out_stay)
-    routed = lax.all_to_all(sum_halves(targets, mine, theirs), ("wide", "tensor"), 0, 0)
+    theirs = cross(project_out(low, high, output_weight, 0))
+    mine = project_out(low, high, output_weight, 1)
+    routed = lax.all_to_all(sum_halves(place, offsets, mine, theirs), ("wide", "tensor"), 0, 0)
     return join_columns(routed)
 
 

time: 75.7 us -> 69.9 us (0.923)
  Pallas kernels: 24.7 us -> 14.1 us
  waiting for transfers between devices: 9.34 us -> 14.9 us
  local copies, waits for them, and re-layouts: 6.05 us -> 1.12 us
  starting transfers between devices: 21.8 us -> 25.4 us
  blocking collectives: 10.6 us -> 12.4 us
  other arithmetic: 1.59 us -> 0.52 us
    pallas_call x6 -> x5, Pallas kernels: 21.8 us -> 11.2 us  [the longest x2 6.72 us: dequantize_all(): pl.pallas_call(kernel, in_specs=[SMEM, VMEM, VMEM], out_specs=VMEM, out_s...]
    ppermute x15 -> x19, waiting for transfers between devices: 8.85 us -> 14.4 us  [swap(): lax.ppermute(array, 'wide', [(peer, peer ^ offset) for peer in range(wide)])]
    unnamed x37 -> x42, local copies, waits for them, and re-layouts: 4.19 us -> 0.18 us
    ppermute x15 -> x19, starting transfers between devices: 21.7 us -> 25.2 us  [swap(): lax.ppermute(array, 'wide', [(peer, peer ^ offset) for peer in range(wide)])]
    all_to_all x1, blocking collectives: 10.6 us -> 12.4 us  [fast(): lax.all_to_all(sum_halves(place, offsets, mine, theirs), ('wide', 'tensor...]
    another operation x4 -> x0, local copies, waits for them, and re-layouts: 0.85 us -> none  [dequantize_part(): jnp.stack([column] + starts).astype(jnp.int32)]
  transfers between devices with their start and end apart: 18 -> 22, of which waited for: 8 -> 12; matrix products, arithmetic and copies ran while one was open for 3% -> 0% of each run, Pallas kernels for 27% -> 13%
where the time goes in v4:
time: 69.9 us; the launch traced here: 69.7 us
  starting transfers between devices  25.4 us (36%)
  waiting for transfers between devices  14.9 us (21%)
  Pallas kernels  14.1 us (20%)
  blocking collectives  12.4 us (18%)
  local copies, waits for them, and re-layouts  1.12 us (2%)
  matrix products  0.95 us (1%)
    ppermute x19, starting transfers between devices, swap(): lax.ppermute(array, 'wide', [(peer, peer ^ offset) for peer in range(wide)])  25.2 us
    ppermute x19, waiting for transfers between devices, swap(): lax.ppermute(array, 'wide', [(peer, peer ^ offset) for peer in range(wide)])  14.4 us
    all_to_all x1, blocking collectives, fast(): lax.all_to_all(sum_halves(place, offsets, mine, theirs), ('wide', 'tensor...  12.4 us
    pallas_call x2, Pallas kernels, dequantize_all(): pl.pallas_call(kernel, in_specs=[SMEM, VMEM, VMEM], out_specs=VMEM, out_s...  6.72 us
    pallas_call x1, Pallas kernels, project_other(): pl.pallas_call(kernel, in_specs=[SMEM] + [VMEM] * 8, out_specs=[VMEM] * 4...  2.12 us
    pallas_call x1, Pallas kernels, project_own(): pl.pallas_call(kernel, in_specs=[SMEM] * 3 + [VMEM] * 4, out_specs=[VMEM]...  1.79 us
    pallas_call x2, Pallas kernels, project_out(): pl.pallas_call(kernel, in_specs=[VMEM] * 3, out_specs=VMEM, out_shape=jax...  1.68 us
  transfers between devices with their start and end apart: 22, of which 12 were waited for; matrix products, arithmetic and copies ran while one was open for 0% of the time, Pallas kernels for 13%

profile of v4, /device:TPU:0, one launch (start us, length us, event | category | flops | bytes accessed | tf_op | source)
XLA Modules:
  0.0 69.7 jit_solution(9226659499935336414)
XLA Ops:
  0.0 0.9 %constant_dynamic-slice_fusion.block_ref = bf16[8,4096]{1,0:T(8,128)(2,1)S(1)} fusion(bf16[8,8192]{1,0:T(8,128)(2,1)} %param.14, s32[]{:T(128)S(6)} %select_n.7), kind=kLoop, calls=%fused_computation.43 | loop fusion | bytes 131076 | tf_op jit(solution)/shard_map/dynamic_slice | solution.py:449
  0.9 0.1 pad_add_fusion.place_ref
  1.0 0.5 begin_gather.1
  1.5 0.0 copy-start.2
  1.5 0.0 copy-start.6
  1.6 0.0 copy-start.7
  1.6 3.1 %collective-permute-start = (bf16[8,4096]{1,0:T(8,128)(2,1)S(1)}, bf16[8,4096]{1,0:T(8,128)(2,1)S(1)}, u32[]{:S(2)}, u32[]{:S(2)}) collective-permute-start(bf16[8,4096]{1,0:T(8,128)(2,1)S(1)} %begin_gather.1), channel_id=1, source_target_pairs={{0,4},{2,6},{4,0},{6,2},{8,12},{10,14},{12,8},{14,10},{1,5},{3,7},... | collective-permute-start | bytes 196616 | tf_op jit(solution)/shard_map/ppermute | solution.py:442
  4.7 2.6 %collective-permute-start.1 = (bf16[8,4096]{1,0:T(8,128)(2,1)S(1)}, bf16[8,4096]{1,0:T(8,128)(2,1)S(1)}, u32[]{:S(2)}, u32[]{:S(2)}) collective-permute-start(bf16[8,4096]{1,0:T(8,128)(2,1)S(1)} %begin_gather.1), channel_id=1, source_target_pairs={{0,8},{2,10},{4,12},{6,14},{8,0},{10,2},{12,4},{14,6},{1,9},{3,11}... | collective-permute-start | bytes 196616 | tf_op jit(solution)/shard_map/ppermute | solution.py:442
  7.3 0.0 collective-permute-start.2
  7.3 1.7 %collective-permute-start.4 = (bf16[8,4096]{1,0:T(8,128)(2,1)S(1)}, bf16[8,4096]{1,0:T(8,128)(2,1)S(1)}, u32[]{:S(2)}, u32[]{:S(2)}) collective-permute-start(bf16[8,4096]{1,0:T(8,128)(2,1)S(1)} %begin_gather.1), channel_id=1, source_target_pairs={{0,2},{2,0},{4,6},{6,4},{8,10},{10,8},{12,14},{14,12},{1,3},{3,1},... | collective-permute-start | bytes 196616 | tf_op jit(solution)/shard_map/ppermute | solution.py:442
  9.0 3.3 %dequantize.2.weight_ref = bf16[1,8192,512]{2,1,0:T(8,128)(2,1)S(1)} custom-call(s32[2]{0:T(128)S(1)} %pad_add_fusion.place_ref, s32[8192,512]{1,0:T(8,128)S(1)} %copy-done.1, f32[128,512]{1,0:T(8,128)S(1)} %copy-done.4), custom_call_target="tpu_custom_call" | custom-call | flops 8388608 | bytes 25165824 | tf_op jit(solution)/shard_map/dequantize/pallas_call | solution.py:95
  12.3 0.0 copy-start.3
  12.3 0.8 %collective-permute-start.5 = (bf16[8,4096]{1,0:T(8,128)(2,1)S(1)}, bf16[8,4096]{1,0:T(8,128)(2,1)S(1)}, u32[]{:S(2)}, u32[]{:S(2)}) collective-permute-start(bf16[8,4096]{1,0:T(8,128)(2,1)S(1)} %collective-permute-done), channel_id=1, source_target_pairs={{0,2},{2,0},{4,6},{6,4},{8,10},{10,8},{12,14},{14,12},{1,3},{3,1},... | collective-permute-start | bytes 196616 | tf_op jit(solution)/shard_map/ppermute | solution.py:442
  13.1 0.0 collective-permute-done.1
  13.1 1.3 %collective-permute-start.6 = (bf16[8,4096]{1,0:T(8,128)(2,1)S(1)}, bf16[8,4096]{1,0:T(8,128)(2,1)S(1)}, u32[]{:S(2)}, u32[]{:S(2)}) collective-permute-start(bf16[8,4096]{1,0:T(8,128)(2,1)S(1)} %collective-permute-done.1), channel_id=1, source_target_pairs={{0,2},{2,0},{4,6},{6,4},{8,10},{10,8},{12,14},{14,12},{1,3},{3,1},... | collective-permute-start | bytes 196616 | tf_op jit(solution)/shard_map/ppermute | solution.py:442
  14.4 0.7 %collective-permute-start.7 = (bf16[8,4096]{1,0:T(8,128)(2,1)S(1)}, bf16[8,4096]{1,0:T(8,128)(2,1)S(1)}, u32[]{:S(2)}, u32[]{:S(2)}) collective-permute-start(bf16[8,4096]{1,0:T(8,128)(2,1)S(1)} %collective-permute-done.2), channel_id=1, source_target_pairs={{0,2},{2,0},{4,6},{6,4},{8,10},{10,8},{12,14},{14,12},{1,3},{3,1},... | collective-permute-start | bytes 196616 | tf_op jit(solution)/shard_map/ppermute | solution.py:442
  15.1 0.1 collective-permute-start.3
  15.2 0.0 collective-permute-done.4
  15.2 2.1 %collective-permute-done.5 = bf16[8,4096]{1,0:T(8,128)(2,1)S(1)} collective-permute-done((bf16[8,4096]{1,0:T(8,128)(2,1)S(1)}, bf16[8,4096]{1,0:T(8,128)(2,1)S(1)}, u32[]{:S(2)}, u32[]{:S(2)}) %collective-permute-start.5) | collective-permute-done | bytes 65568 | tf_op jit(solution)/shard_map/ppermute | solution.py:442
  17.3 0.7 %collective-permute-done.6 = bf16[8,4096]{1,0:T(8,128)(2,1)S(1)} collective-permute-done((bf16[8,4096]{1,0:T(8,128)(2,1)S(1)}, bf16[8,4096]{1,0:T(8,128)(2,1)S(1)}, u32[]{:S(2)}, u32[]{:S(2)}) %collective-permute-start.6) | collective-permute-done | bytes 65568 | tf_op jit(solution)/shard_map/ppermute | solution.py:442
  18.0 0.7 collective-permute-done.7
  18.7 0.0 collective-permute-start.8
  18.8 1.8 %project_own.1 = (f32[64,512]{1,0:T(8,128)S(1)}, f32[192,64]{1,0:T(8,128)S(1)}, s32[8,64]{1,0:T(8,128)S(1)}) custom-call(s32[2]{0:T(128)S(1)} %pad_add_fusion.place_ref, s32[64]{0:T(128)S(1)} %copy-done.6, s32[48]{0:T(128)S(1)} %copy-done.7, bf16[32,4096]{1,0:T(8,128)(2,1)S(1)} %pad_maximum_fusion.low, ...), custom_call_target="tpu_custom_call" | custom-call | flops 369098752 | bytes 7340032 | tf_op jit(solution)/shard_map/project_own/pallas_call | solution.py:159
  20.6 0.0 copy-start.9
  20.6 0.0 copy-start.5
  20.6 0.0 collective-permute-done.8.high
  20.6 0.0 slice-start.3
  20.6 2.1 %project_other.1 = (bf16[16,4096]{1,0:T(8,128)(2,1)S(1)}, bf16[16,4096]{1,0:T(8,128)(2,1)S(1)}, bf16[16,4096]{1,0:T(8,128)(2,1)S(1)}, bf16[16,4096]{1,0:T(8,128)(2,1)S(1)}) custom-call(s32[2]{0:T(128)S(1)} %pad_add_fusion.place_ref, bf16[32,4096]{1,0:T(8,128)(2,1)S(1)} %collective-permute-done.3.low, bf16[32,4096]{1,0:T(8,128)(2,1)S(1)} %collective-permute-done.8.high, ...), custom_call_target="tpu_custom_call" | custom-call | flops 469762048 | bytes 8388608 | tf_op jit(solution)/shard_map/project_other/pallas_call | solution.py:229
  22.8 1.0 %collective-permute-start.10 = (bf16[16,4096]{1,0:T(8,128)(2,1)S(1)}, bf16[16,4096]{1,0:T(8,128)(2,1)S(1)}, u32[]{:S(2)}, u32[]{:S(2)}) collective-permute-start(bf16[16,4096]{1,0:T(8,128)(2,1)S(1)} %get-tuple-element.24), channel_id=1, source_target_pairs={{0,2},{2,0},{4,6},{6,4},{8,10},{10,8},{12,14},{14,12},{1,3},{3,1},... | collective-permute-start | bytes 393224 | tf_op jit(solution)/shard_map/ppermute | solution.py:442
  23.8 0.0 copy-start.8
  23.8 1.1 %collective-permute-start.9 = (bf16[16,4096]{1,0:T(8,128)(2,1)S(1)}, bf16[16,4096]{1,0:T(8,128)(2,1)S(1)}, u32[]{:S(2)}, u32[]{:S(2)}) collective-permute-start(bf16[16,4096]{1,0:T(8,128)(2,1)S(1)} %get-tuple-element.27), channel_id=1, source_target_pairs={{0,2},{2,0},{4,6},{6,4},{8,10},{10,8},{12,14},{14,12},{1,3},{3,1},... | collective-permute-start | bytes 393224 | tf_op jit(solution)/shard_map/ppermute | solution.py:442
  25.0 3.4 %dequantize.3.weight_ref = bf16[2,4096,512]{2,1,0:T(8,128)(2,1)S(1)} custom-call(s32[2]{0:T(128)S(1)} %pad_add_fusion.place_ref, s32[4096,1024]{1,0:T(8,128)S(1)} %bitcast.40, f32[64,1024]{1,0:T(8,128)S(1)} %copy-done.5), custom_call_target="tpu_custom_call" | custom-call | flops 8388608 | bytes 25165824 | tf_op jit(solution)/shard_map/dequantize/pallas_call | solution.py:95
  28.4 0.7 %collective-permute-done.10 = bf16[16,4096]{1,0:T(8,128)(2,1)S(1)} collective-permute-done((bf16[16,4096]{1,0:T(8,128)(2,1)S(1)}, bf16[16,4096]{1,0:T(8,128)(2,1)S(1)}, u32[]{:S(2)}, u32[]{:S(2)}) %collective-permute-start.10) | collective-permute-done | bytes 131104 | tf_op jit(solution)/shard_map/ppermute | solution.py:442
  29.2 2.6 %collective-permute-start.11 = (bf16[8,4096]{1,0:T(8,128)(2,1)S(1)}, bf16[8,4096]{1,0:T(8,128)(2,1)S(1)}, u32[]{:S(2)}, u32[]{:S(2)}) collective-permute-start(bf16[8,4096]{1,0:T(8,128)(2,1)S(1)} %get-tuple-element.31), channel_id=1, source_target_pairs={{0,8},{2,10},{4,12},{6,14},{8,0},{10,2},{12,4},{14,6},{1,9},{3,11}... | collective-permute-start | bytes 196616 | tf_op jit(solution)/shard_map/ppermute | solution.py:442
  31.8 1.3 %collective-permute-start.12 = (bf16[8,4096]{1,0:T(8,128)(2,1)S(1)}, bf16[8,4096]{1,0:T(8,128)(2,1)S(1)}, u32[]{:S(2)}, u32[]{:S(2)}) collective-permute-start(bf16[8,4096]{1,0:T(8,128)(2,1)S(1)} %get-tuple-element.32), channel_id=1, source_target_pairs={{0,12},{2,14},{4,8},{6,10},{8,4},{10,6},{12,0},{14,2},{1,13},{3,15... | collective-permute-start | bytes 196616 | tf_op jit(solution)/shard_map/ppermute | solution.py:442
  33.2 0.4 collective-permute-start.13
  33.6 0.1 iota_compare_fusion
  33.6 0.8 %collective-permute-done.11 = bf16[8,4096]{1,0:T(8,128)(2,1)S(1)} collective-permute-done((bf16[8,4096]{1,0:T(8,128)(2,1)S(1)}, bf16[8,4096]{1,0:T(8,128)(2,1)S(1)}, u32[]{:S(2)}, u32[]{:S(2)}) %collective-permute-start.11) | collective-permute-done | bytes 65568 | tf_op jit(solution)/shard_map/ppermute | solution.py:442
  34.4 3.6 %collective-permute-done.12 = bf16[8,4096]{1,0:T(8,128)(2,1)S(1)} collective-permute-done((bf16[8,4096]{1,0:T(8,128)(2,1)S(1)}, bf16[8,4096]{1,0:T(8,128)(2,1)S(1)}, u32[]{:S(2)}, u32[]{:S(2)}) %collective-permute-start.12) | collective-permute-done | bytes 65568 | tf_op jit(solution)/shard_map/ppermute | solution.py:442
  38.0 0.2 collective-permute-done.13
  38.2 0.2 fusion.12
  38.4 0.5 fusion.19
  38.9 0.2 fusion.7
  39.1 0.3 fusion.2
  39.5 1.1 %collective-permute-start.17 = (bf16[8,4096]{1,0:T(8,128)(2,1)S(1)}, bf16[8,4096]{1,0:T(8,128)(2,1)S(1)}, u32[]{:S(2)}, u32[]{:S(2)}) collective-permute-start(bf16[8,4096]{1,0:T(8,128)(2,1)S(1)} %bitcast.48), channel_id=1, source_target_pairs={{0,2},{2,0},{4,6},{6,4},{8,10},{10,8},{12,14},{14,12},{1,3},{3,1},... | collective-permute-start | bytes 196616 | tf_op jit(solution)/shard_map/ppermute | solution.py:442
  40.6 0.0 collective-permute-start.14
  40.7 2.8 %collective-permute-start.15 = (bf16[8,4096]{1,0:T(8,128)(2,1)S(1)}, bf16[8,4096]{1,0:T(8,128)(2,1)S(1)}, u32[]{:S(2)}, u32[]{:S(2)}) collective-permute-start(bf16[8,4096]{1,0:T(8,128)(2,1)S(1)} %bitcast.50), channel_id=1, source_target_pairs={{0,8},{2,10},{4,12},{6,14},{8,0},{10,2},{12,4},{14,6},{1,9},{3,11}... | collective-permute-start | bytes 196616 | tf_op jit(solution)/shard_map/ppermute | solution.py:442
  43.5 1.5 %collective-permute-start.16 = (bf16[8,4096]{1,0:T(8,128)(2,1)S(1)}, bf16[8,4096]{1,0:T(8,128)(2,1)S(1)}, u32[]{:S(2)}, u32[]{:S(2)}) collective-permute-start(bf16[8,4096]{1,0:T(8,128)(2,1)S(1)} %bitcast.51), channel_id=1, source_target_pairs={{0,12},{2,14},{4,8},{6,10},{8,4},{10,6},{12,0},{14,2},{1,13},{3,15... | collective-permute-start | bytes 196616 | tf_op jit(solution)/shard_map/ppermute | solution.py:442
  45.1 0.0 collective-permute-done.17
  45.1 0.0 collective-permute-done.14
  45.1 1.0 %collective-permute-start.18 = (bf16[8,4096]{1,0:T(8,128)(2,1)S(1)}, bf16[8,4096]{1,0:T(8,128)(2,1)S(1)}, u32[]{:S(2)}, u32[]{:S(2)}) collective-permute-start(bf16[8,4096]{1,0:T(8,128)(2,1)S(1)} %collective-permute-done.14), channel_id=1, source_target_pairs={{0,2},{2,0},{4,6},{6,4},{8,10},{10,8},{12,14},{14,12},{1,3},{3,1},... | collective-permute-start | bytes 196616 | tf_op jit(solution)/shard_map/ppermute | solution.py:442
  46.1 2.0 %collective-permute-done.15 = bf16[8,4096]{1,0:T(8,128)(2,1)S(1)} collective-permute-done((bf16[8,4096]{1,0:T(8,128)(2,1)S(1)}, bf16[8,4096]{1,0:T(8,128)(2,1)S(1)}, u32[]{:S(2)}, u32[]{:S(2)}) %collective-permute-start.15) | collective-permute-done | bytes 65568 | tf_op jit(solution)/shard_map/ppermute | solution.py:442
  48.1 1.0 %collective-permute-start.19 = (bf16[8,4096]{1,0:T(8,128)(2,1)S(1)}, bf16[8,4096]{1,0:T(8,128)(2,1)S(1)}, u32[]{:S(2)}, u32[]{:S(2)}) collective-permute-start(bf16[8,4096]{1,0:T(8,128)(2,1)S(1)} %collective-permute-done.15), channel_id=1, source_target_pairs={{0,2},{2,0},{4,6},{6,4},{8,10},{10,8},{12,14},{14,12},{1,3},{3,1},... | collective-permute-start | bytes 196616 | tf_op jit(solution)/shard_map/ppermute | solution.py:442
  49.2 0.4 collective-permute-done.16
  49.6 1.0 %collective-permute-start.20 = (bf16[8,4096]{1,0:T(8,128)(2,1)S(1)}, bf16[8,4096]{1,0:T(8,128)(2,1)S(1)}, u32[]{:S(2)}, u32[]{:S(2)}) collective-permute-start(bf16[8,4096]{1,0:T(8,128)(2,1)S(1)} %collective-permute-done.16), channel_id=1, source_target_pairs={{0,2},{2,0},{4,6},{6,4},{8,10},{10,8},{12,14},{14,12},{1,3},{3,1},... | collective-permute-start | bytes 196616 | tf_op jit(solution)/shard_map/ppermute | solution.py:442
  50.7 1.7 %collective-permute-done.19 = bf16[8,4096]{1,0:T(8,128)(2,1)S(1)} collective-permute-done((bf16[8,4096]{1,0:T(8,128)(2,1)S(1)}, bf16[8,4096]{1,0:T(8,128)(2,1)S(1)}, u32[]{:S(2)}, u32[]{:S(2)}) %collective-permute-start.19) | collective-permute-done | bytes 65568 | tf_op jit(solution)/shard_map/ppermute | solution.py:442
  52.4 1.5 %collective-permute-done.20 = bf16[8,4096]{1,0:T(8,128)(2,1)S(1)} collective-permute-done((bf16[8,4096]{1,0:T(8,128)(2,1)S(1)}, bf16[8,4096]{1,0:T(8,128)(2,1)S(1)}, u32[]{:S(2)}, u32[]{:S(2)}) %collective-permute-start.20) | collective-permute-done | bytes 65568 | tf_op jit(solution)/shard_map/ppermute | solution.py:442
  53.9 0.8 %project_out.3 = f32[64,512]{1,0:T(8,128)S(1)} custom-call(bf16[32,4096]{1,0:T(8,128)(2,1)S(1)} %constant_dynamic-update-slice_fusion.4.low_ref, bf16[32,4096]{1,0:T(8,128)(2,1)S(1)} %constant_dynamic-update-slice_fusion.8.high_ref, bf16[2,4096,512]{2,1,0:T(8,128)(2,1)S(1)} %dequantize.3.weight_ref), custom_call_target="tpu_custom_call" | custom-call | flops 268435456 | bytes 6291456 | tf_op jit(solution)/shard_map/project_out/pallas_call | solution.py:252
  54.7 0.1 collective-permute-start.21
  54.8 0.8 %project_out.2.mine_ref = f32[64,512]{1,0:T(8,128)S(1)} custom-call(bf16[32,4096]{1,0:T(8,128)(2,1)S(1)} %constant_dynamic-update-slice_fusion.4.low_ref, bf16[32,4096]{1,0:T(8,128)(2,1)S(1)} %constant_dynamic-update-slice_fusion.8.high_ref, bf16[2,4096,512]{2,1,0:T(8,128)(2,1)S(1)} %dequantize.3.weight_ref), custom_call_target="tpu_custom_call" | custom-call | flops 268435456 | bytes 6291456 | tf_op jit(solution)/shard_map/project_out/pallas_call | solution.py:252
  55.7 0.5 collective-permute-done.21.theirs_ref
  56.1 0.6 sum_halves.1
  56.7 12.4 %all_to_all.5.pieces_ref = bf16[16,8,512]{2,1,0:T(8,128)(2,1)S(1)} all-to-all(bf16[16,8,512]{2,1,0:T(8,128)(2,1)S(1)} %sum_halves.1), channel_id=1, replica_groups=mesh['rep'=2,'wide'=8,'tensor'=2] {'wide','tensor'}, dimensions={0} | all-to-all | bytes 262144 | tf_op jit(solution)/shard_map/all_to_all | solution.py:498
  69.1 0.7 join_columns.1
  (53 shorter events, 0.4 us)
Async XLA Ops:
  0.0 39.1 %copy-start = (bf16[8,64,512]{2,1,0:T(8,128)(2,1)S(1)}, bf16[8,64,512]{2,1,0:T(8,128)(2,1)}, u32[]{:S(2)}) copy-start(bf16[8,64,512]{2,1,0:T(8,128)(2,1)} %param.25) | copy-start | bytes 1572868
  1.0 8.0 %copy-start.1 = (s32[8192,512]{1,0:T(8,128)S(1)}, s32[8192,512]{1,0:T(8,128)}, u32[]{:S(2)}) copy-start(s32[8192,512]{1,0:T(8,128)} %codes_ref.2) | copy-start | bytes 50331652
  1.0 8.0 %copy-start.4 = (f32[128,512]{1,0:T(8,128)S(1)}, f32[128,512]{1,0:T(8,128)}, u32[]{:S(2)}) copy-start(f32[128,512]{1,0:T(8,128)} %scales_ref.2) | copy-start | bytes 786436
  1.5 17.2 %copy-start.2 = (bf16[8192,6,32]{0,2,1:T(8,128)(2,1)S(1)}, bf16[8192,6,32]{0,2,1:T(8,128)(2,1)}, u32[]{:S(2)}) copy-start(bf16[8192,6,32]{0,2,1:T(8,128)(2,1)} %param.19) | copy-start | bytes 9437188
  1.5 17.2 %copy-start.6 = (s32[64]{0:T(128)S(1)}, s32[64]{0:T(128)}, u32[]{:S(2)}) copy-start(s32[64]{0:T(128)} %adapters_ref.1) | copy-start | bytes 772
  1.6 17.2 %copy-start.7 = (s32[48]{0:T(128)S(1)}, s32[48]{0:T(128)}, u32[]{:S(2)}) copy-start(s32[48]{0:T(128)} %storage_ref.1) | copy-start | bytes 580
  1.6 10.7 %collective-permute-start = (bf16[8,4096]{1,0:T(8,128)(2,1)S(1)}, bf16[8,4096]{1,0:T(8,128)(2,1)S(1)}, u32[]{:S(2)}, u32[]{:S(2)}) collective-permute-start(bf16[8,4096]{1,0:T(8,128)(2,1)S(1)} %begin_gather.1), channel_id=1, source_target_pairs={{0,4},{2,6},{4,0},{6,2},{8,12},{10,14},{12,8},{14,10},{1,5},{3,7},... | collective-permute-start | bytes 196616 | tf_op jit(solution)/shard_map/ppermute | solution.py:442
  4.7 8.4 %collective-permute-start.1 = (bf16[8,4096]{1,0:T(8,128)(2,1)S(1)}, bf16[8,4096]{1,0:T(8,128)(2,1)S(1)}, u32[]{:S(2)}, u32[]{:S(2)}) collective-permute-start(bf16[8,4096]{1,0:T(8,128)(2,1)S(1)} %begin_gather.1), channel_id=1, source_target_pairs={{0,8},{2,10},{4,12},{6,14},{8,0},{10,2},{12,4},{14,6},{1,9},{3,11}... | collective-permute-start | bytes 196616 | tf_op jit(solution)/shard_map/ppermute | solution.py:442
  7.3 7.2 %collective-permute-start.2 = (bf16[8,4096]{1,0:T(8,128)(2,1)S(1)}, bf16[8,4096]{1,0:T(8,128)(2,1)S(1)}, u32[]{:S(2)}, u32[]{:S(2)}) collective-permute-start(bf16[8,4096]{1,0:T(8,128)(2,1)S(1)} %begin_gather.1), channel_id=1, source_target_pairs={{0,12},{2,14},{4,8},{6,10},{8,4},{10,6},{12,0},{14,2},{1,13},{3,15... | collective-permute-start | bytes 196616 | tf_op jit(solution)/shard_map/ppermute | solution.py:442
  7.3 8.0 %collective-permute-start.4 = (bf16[8,4096]{1,0:T(8,128)(2,1)S(1)}, bf16[8,4096]{1,0:T(8,128)(2,1)S(1)}, u32[]{:S(2)}, u32[]{:S(2)}) collective-permute-start(bf16[8,4096]{1,0:T(8,128)(2,1)S(1)} %begin_gather.1), channel_id=1, source_target_pairs={{0,2},{2,0},{4,6},{6,4},{8,10},{10,8},{12,14},{14,12},{1,3},{3,1},... | collective-permute-start | bytes 196616 | tf_op jit(solution)/shard_map/ppermute | solution.py:442
  9.0 16.0 %slice-start = ((s8[16777216]{0:T(1024)(128)(4,1)}), s8[4194304]{0:T(1024)(128)(4,1)S(1)}, s32[]{:S(2)}) async-start(s8[16777216]{0:T(1024)(128)(4,1)} %bitcast.39), calls=%async_computation.1 | async-start | bytes 8388608
  9.0 16.0 %slice-start.1 = ((s8[16777216]{0:T(1024)(128)(4,1)}), s8[4194304]{0:T(1024)(128)(4,1)S(1)}, s32[]{:S(2)}) async-start(s8[16777216]{0:T(1024)(128)(4,1)} %bitcast.39), calls=%async_computation.2 | async-start | bytes 8388608
  12.3 8.4 %copy-start.3 = (bf16[6,32,4096]{2,1,0:T(8,128)(2,1)S(1)}, bf16[6,32,4096]{2,1,0:T(8,128)(2,1)}, u32[]{:S(2)}) copy-start(bf16[6,32,4096]{2,1,0:T(8,128)(2,1)} %param.20) | copy-start | bytes 4718596
  12.3 5.0 %collective-permute-start.5 = (bf16[8,4096]{1,0:T(8,128)(2,1)S(1)}, bf16[8,4096]{1,0:T(8,128)(2,1)S(1)}, u32[]{:S(2)}, u32[]{:S(2)}) collective-permute-start(bf16[8,4096]{1,0:T(8,128)(2,1)S(1)} %collective-permute-done), channel_id=1, source_target_pairs={{0,2},{2,0},{4,6},{6,4},{8,10},{10,8},{12,14},{14,12},{1,3},{3,1},... | collective-permute-start | bytes 196616 | tf_op jit(solution)/shard_map/ppermute | solution.py:442
  13.1 5.0 %collective-permute-start.6 = (bf16[8,4096]{1,0:T(8,128)(2,1)S(1)}, bf16[8,4096]{1,0:T(8,128)(2,1)S(1)}, u32[]{:S(2)}, u32[]{:S(2)}) collective-permute-start(bf16[8,4096]{1,0:T(8,128)(2,1)S(1)} %collective-permute-done.1), channel_id=1, source_target_pairs={{0,2},{2,0},{4,6},{6,4},{8,10},{10,8},{12,14},{14,12},{1,3},{3,1},... | collective-permute-start | bytes 196616 | tf_op jit(solution)/shard_map/ppermute | solution.py:442
  14.4 4.3 %collective-permute-start.7 = (bf16[8,4096]{1,0:T(8,128)(2,1)S(1)}, bf16[8,4096]{1,0:T(8,128)(2,1)S(1)}, u32[]{:S(2)}, u32[]{:S(2)}) collective-permute-start(bf16[8,4096]{1,0:T(8,128)(2,1)S(1)} %collective-permute-done.2), channel_id=1, source_target_pairs={{0,2},{2,0},{4,6},{6,4},{8,10},{10,8},{12,14},{14,12},{1,3},{3,1},... | collective-permute-start | bytes 196616 | tf_op jit(solution)/shard_map/ppermute | solution.py:442
  15.1 5.5 %collective-permute-start.3 = (bf16[32,4096]{1,0:T(8,128)(2,1)S(1)}, bf16[32,4096]{1,0:T(8,128)(2,1)S(1)}, u32[]{:S(2)}, u32[]{:S(2)}) collective-permute-start(bf16[32,4096]{1,0:T(8,128)(2,1)S(1)} %pad_maximum_fusion.low), channel_id=1, source_target_pairs={{0,1},{1,0},{2,3},{3,2},{4,5},{5,4},{6,7},{7,6},{8,9},{9,8},{10,11... | collective-permute-start | bytes 786440 | tf_op jit(solution)/shard_map/ppermute | solution.py:445
  17.3 7.7 %slice-start.2 = ((s8[16777216]{0:T(1024)(128)(4,1)}), s8[4194304]{0:T(1024)(128)(4,1)S(1)}, s32[]{:S(2)}) async-start(s8[16777216]{0:T(1024)(128)(4,1)} %bitcast.39), calls=%async_computation.3 | async-start | bytes 8388608
  18.7 1.9 %collective-permute-start.8 = (bf16[32,4096]{1,0:T(8,128)(2,1)S(1)}, bf16[32,4096]{1,0:T(8,128)(2,1)S(1)}, u32[]{:S(2)}, u32[]{:S(2)}) collective-permute-start(bf16[32,4096]{1,0:T(8,128)(2,1)S(1)} %constant_dynamic-update-slice_fusion.high), channel_id=1, source_target_pairs={{0,1},{1,0},{2,3},{3,2},{4,5},{5,4},{6,7},{7,6},{8,9},{9,8},{10,11... | collective-permute-start | bytes 786440 | tf_op jit(solution)/shard_map/ppermute | solution.py:445
  20.6 3.2 %copy-start.9 = (bf16[8,512]{1,0:T(8,128)(2,1)S(1)}, bf16[8,512]{1,0:T(8,128)(2,1)}, u32[]{:S(2)}) copy-start(bf16[8,512]{1,0:T(8,128)(2,1)} %param.27) | copy-start | bytes 24580
  20.6 4.4 %copy-start.5 = (f32[64,1024]{1,0:T(8,128)S(1)}, f32[64,1024]{1,0:T(8,128)}, u32[]{:S(2)}) copy-start(f32[64,1024]{1,0:T(8,128)} %scales_ref.3) | copy-start | bytes 786436
  20.6 4.3 %slice-start.3 = ((s8[16777216]{0:T(1024)(128)(4,1)}), s8[4194304]{0:T(1024)(128)(4,1)S(1)}, s32[]{:S(2)}) async-start(s8[16777216]{0:T(1024)(128)(4,1)} %bitcast.39), calls=%async_computation.4 | async-start | bytes 8388608
  22.8 6.4 %collective-permute-start.10 = (bf16[16,4096]{1,0:T(8,128)(2,1)S(1)}, bf16[16,4096]{1,0:T(8,128)(2,1)S(1)}, u32[]{:S(2)}, u32[]{:S(2)}) collective-permute-start(bf16[16,4096]{1,0:T(8,128)(2,1)S(1)} %get-tuple-element.24), channel_id=1, source_target_pairs={{0,2},{2,0},{4,6},{6,4},{8,10},{10,8},{12,14},{14,12},{1,3},{3,1},... | collective-permute-start | bytes 393224 | tf_op jit(solution)/shard_map/ppermute | solution.py:442
  23.8 9.7 %copy-start.11 = (s32[8]{0:T(128)S(1)}, s32[8]{0:T(128)}, u32[]{:S(2)}) copy-start(s32[8]{0:T(128)} %param.23) | copy-start | bytes 100
  23.8 14.4 %copy-start.10 = (bf16[8,512]{1,0:T(8,128)(2,1)S(1)}, bf16[8,512]{1,0:T(8,128)(2,1)}, u32[]{:S(2)}) copy-start(bf16[8,512]{1,0:T(8,128)(2,1)} %param.26) | copy-start | bytes 24580
  23.8 14.6 %copy-start.8 = (bf16[8,64,512]{2,1,0:T(8,128)(2,1)S(1)}, bf16[8,64,512]{2,1,0:T(8,128)(2,1)}, u32[]{:S(2)}) copy-start(bf16[8,64,512]{2,1,0:T(8,128)(2,1)} %param.24) | copy-start | bytes 1572868
  23.8 9.3 %collective-permute-start.9 = (bf16[16,4096]{1,0:T(8,128)(2,1)S(1)}, bf16[16,4096]{1,0:T(8,128)(2,1)S(1)}, u32[]{:S(2)}, u32[]{:S(2)}) collective-permute-start(bf16[16,4096]{1,0:T(8,128)(2,1)S(1)} %get-tuple-element.27), channel_id=1, source_target_pairs={{0,2},{2,0},{4,6},{6,4},{8,10},{10,8},{12,14},{14,12},{1,3},{3,1},... | collective-permute-start | bytes 393224 | tf_op jit(solution)/shard_map/ppermute | solution.py:442
  29.2 5.2 %collective-permute-start.11 = (bf16[8,4096]{1,0:T(8,128)(2,1)S(1)}, bf16[8,4096]{1,0:T(8,128)(2,1)S(1)}, u32[]{:S(2)}, u32[]{:S(2)}) collective-permute-start(bf16[8,4096]{1,0:T(8,128)(2,1)S(1)} %get-tuple-element.31), channel_id=1, source_target_pairs={{0,8},{2,10},{4,12},{6,14},{8,0},{10,2},{12,4},{14,6},{1,9},{3,11}... | collective-permute-start | bytes 196616 | tf_op jit(solution)/shard_map/ppermute | solution.py:442
  31.8 6.2 %collective-permute-start.12 = (bf16[8,4096]{1,0:T(8,128)(2,1)S(1)}, bf16[8,4096]{1,0:T(8,128)(2,1)S(1)}, u32[]{:S(2)}, u32[]{:S(2)}) collective-permute-start(bf16[8,4096]{1,0:T(8,128)(2,1)S(1)} %get-tuple-element.32), channel_id=1, source_target_pairs={{0,12},{2,14},{4,8},{6,10},{8,4},{10,6},{12,0},{14,2},{1,13},{3,15... | collective-permute-start | bytes 196616 | tf_op jit(solution)/shard_map/ppermute | solution.py:442
  33.2 5.0 %collective-permute-start.13 = (bf16[8,4096]{1,0:T(8,128)(2,1)S(1)}, bf16[8,4096]{1,0:T(8,128)(2,1)S(1)}, u32[]{:S(2)}, u32[]{:S(2)}) collective-permute-start(bf16[8,4096]{1,0:T(8,128)(2,1)S(1)} %slice.19), channel_id=1, source_target_pairs={{0,4},{2,6},{4,0},{6,2},{8,12},{10,14},{12,8},{14,10},{1,5},{3,7},... | collective-permute-start | bytes 196616 | tf_op jit(solution)/shard_map/ppermute | solution.py:442
  39.5 5.6 %collective-permute-start.17 = (bf16[8,4096]{1,0:T(8,128)(2,1)S(1)}, bf16[8,4096]{1,0:T(8,128)(2,1)S(1)}, u32[]{:S(2)}, u32[]{:S(2)}) collective-permute-start(bf16[8,4096]{1,0:T(8,128)(2,1)S(1)} %bitcast.48), channel_id=1, source_target_pairs={{0,2},{2,0},{4,6},{6,4},{8,10},{10,8},{12,14},{14,12},{1,3},{3,1},... | collective-permute-start | bytes 196616 | tf_op jit(solution)/shard_map/ppermute | solution.py:442
  40.6 4.4 %collective-permute-start.14 = (bf16[8,4096]{1,0:T(8,128)(2,1)S(1)}, bf16[8,4096]{1,0:T(8,128)(2,1)S(1)}, u32[]{:S(2)}, u32[]{:S(2)}) collective-permute-start(bf16[8,4096]{1,0:T(8,128)(2,1)S(1)} %bitcast.49), channel_id=1, source_target_pairs={{0,4},{2,6},{4,0},{6,2},{8,12},{10,14},{12,8},{14,10},{1,5},{3,7},... | collective-permute-start | bytes 196616 | tf_op jit(solution)/shard_map/ppermute | solution.py:442
  40.7 7.5 %collective-permute-start.15 = (bf16[8,4096]{1,0:T(8,128)(2,1)S(1)}, bf16[8,4096]{1,0:T(8,128)(2,1)S(1)}, u32[]{:S(2)}, u32[]{:S(2)}) collective-permute-start(bf16[8,4096]{1,0:T(8,128)(2,1)S(1)} %bitcast.50), channel_id=1, source_target_pairs={{0,8},{2,10},{4,12},{6,14},{8,0},{10,2},{12,4},{14,6},{1,9},{3,11}... | collective-permute-start | bytes 196616 | tf_op jit(solution)/shard_map/ppermute | solution.py:442
  43.5 6.1 %collective-permute-start.16 = (bf16[8,4096]{1,0:T(8,128)(2,1)S(1)}, bf16[8,4096]{1,0:T(8,128)(2,1)S(1)}, u32[]{:S(2)}, u32[]{:S(2)}) collective-permute-start(bf16[8,4096]{1,0:T(8,128)(2,1)S(1)} %bitcast.51), channel_id=1, source_target_pairs={{0,12},{2,14},{4,8},{6,10},{8,4},{10,6},{12,0},{14,2},{1,13},{3,15... | collective-permute-start | bytes 196616 | tf_op jit(solution)/shard_map/ppermute | solution.py:442
  45.1 5.6 %collective-permute-start.18 = (bf16[8,4096]{1,0:T(8,128)(2,1)S(1)}, bf16[8,4096]{1,0:T(8,128)(2,1)S(1)}, u32[]{:S(2)}, u32[]{:S(2)}) collective-permute-start(bf16[8,4096]{1,0:T(8,128)(2,1)S(1)} %collective-permute-done.14), channel_id=1, source_target_pairs={{0,2},{2,0},{4,6},{6,4},{8,10},{10,8},{12,14},{14,12},{1,3},{3,1},... | collective-permute-start | bytes 196616 | tf_op jit(solution)/shard_map/ppermute | solution.py:442
  48.1 4.3 %collective-permute-start.19 = (bf16[8,4096]{1,0:T(8,128)(2,1)S(1)}, bf16[8,4096]{1,0:T(8,128)(2,1)S(1)}, u32[]{:S(2)}, u32[]{:S(2)}) collective-permute-start(bf16[8,4096]{1,0:T(8,128)(2,1)S(1)} %collective-permute-done.15), channel_id=1, source_target_pairs={{0,2},{2,0},{4,6},{6,4},{8,10},{10,8},{12,14},{14,12},{1,3},{3,1},... | collective-permute-start | bytes 196616 | tf_op jit(solution)/shard_map/ppermute | solution.py:442
  49.6 4.3 %collective-permute-start.20 = (bf16[8,4096]{1,0:T(8,128)(2,1)S(1)}, bf16[8,4096]{1,0:T(8,128)(2,1)S(1)}, u32[]{:S(2)}, u32[]{:S(2)}) collective-permute-start(bf16[8,4096]{1,0:T(8,128)(2,1)S(1)} %collective-permute-done.16), channel_id=1, source_target_pairs={{0,2},{2,0},{4,6},{6,4},{8,10},{10,8},{12,14},{14,12},{1,3},{3,1},... | collective-permute-start | bytes 196616 | tf_op jit(solution)/shard_map/ppermute | solution.py:442
  54.7 1.4 %collective-permute-start.21 = (f32[64,512]{1,0:T(8,128)S(1)}, f32[64,512]{1,0:T(8,128)S(1)}, u32[]{:S(2)}, u32[]{:S(2)}) collective-permute-start(f32[64,512]{1,0:T(8,128)S(1)} %project_out.3), channel_id=1, source_target_pairs={{0,1},{1,0},{2,3},{3,2},{4,5},{5,4},{6,7},{7,6},{8,9},{9,8},{10,11... | collective-permute-start | bytes 393224 | tf_op jit(solution)/shard_map/ppermute | solution.py:445

commit v5 on v4

--- a/solution.py
+++ b/solution.py
@@ -55,14 +55,16 @@
     return blocks.reshape(height, breadth).astype(jnp.bfloat16)
 
 
-def dequantize_all(place, codes, scales, halves):
+def dequantize_all(codes, scales, halves, *after):
     chunk = 512
     height, breadth = codes.shape
     blocks = chunk // QBLOCK
     parts = 2 if halves else 1
     width = breadth // parts
 
-    def kernel(place_ref, codes_ref, scales_ref, out_ref):
+    def kernel(codes_ref, scales_ref, *rest):
+        out_ref = rest[-1]
+        core = lax.axis_index("tensor")
         number = lax.broadcasted_iota(jnp.int32, (16, LANES), 0)
         table = jnp.zeros((16, LANES), jnp.float32)
         for code, level in enumerate(NF4_LEVELS):
@@ -71,7 +73,7 @@
         def work(step, carry):
             for lane in range(0, breadth, LANES):
                 part = lane // width
-                place_in = (part + 1 + place_ref[1]) % 2 if halves else 0
+                place_in = (part + 1 + core) % 2 if halves else 0
                 group = scales_ref[
                     pl.ds(pl.multiple_of(step * blocks, blocks), blocks), lane : lane + LANES
                 ]
@@ -94,7 +96,7 @@
 
     return pl.pallas_call(
         kernel,
-        in_specs=[SMEM, VMEM, VMEM],
+        in_specs=[VMEM, VMEM] + [ANY] * len(after),
         out_specs=VMEM,
         out_shape=pltpu.VMEM((parts, height, width), jnp.bfloat16),
         compiler_params=pltpu.CompilerParams(vmem_limit_bytes=2 * MIB),
@@ -102,68 +104,80 @@
             flops=2 * height * breadth, bytes_accessed=6 * height * breadth, transcendentals=0
         ),
         name="dequantize",
-    )(place, codes, scales)
-
-
-def begin_gather(place, block):
-    def kernel(place_ref, block_ref, out_ref):
-        out_ref[...] = block_ref[...]
-
-    return pl.pallas_call(
-        kernel,
-        in_specs=[SMEM, VMEM],
+    )(codes, scales, *after)
+
+
+def begin_gather(block):
+    def kernel(block_ref, out_ref):
+        del block_ref, out_ref
+
+    return pl.pallas_call(
+        kernel,
+        in_specs=[VMEM],
         out_specs=VMEM,
         out_shape=pltpu.VMEM(block.shape, block.dtype),
+        input_output_aliases={0: 0},
         compiler_params=pltpu.CompilerParams(vmem_limit_bytes=2 * MIB),
         cost_estimate=pl.CostEstimate(
             flops=6_000_000_000, bytes_accessed=4 * block.size, transcendentals=0
         ),
         name="begin_gather",
-    )(place, block)
+    )(block)
 
 
 LAST = (((1,), (1,)), ((), ()))
 
 
-def project_own(place, offsets, row_adapter_index, adapter_storage_slot, own, weight, down):
+def find_slots(offsets, row_adapter_index, adapter_storage_slot, after):
+    count = row_adapter_index.shape[0]
+    block = count // len(offsets)
+
+    def kernel(adapters_ref, storage_ref, after_ref, slots_ref):
+        me = lax.axis_index("wide").astype(jnp.int32)
+        column = lax.broadcasted_iota(jnp.int32, slots_ref.shape, 1)
+        slots = jnp.zeros(slots_ref.shape, jnp.int32)
+        for row in range(count):
+            source = (me ^ int(offsets[row // block])) * block + row % block
+            slots = jnp.where(column == row, storage_ref[adapters_ref[source]], slots)
+        slots_ref[...] = slots
+
+    return pl.pallas_call(
+        kernel,
+        in_specs=[SMEM, SMEM, ANY],
+        out_specs=VMEM,
+        out_shape=jax.ShapeDtypeStruct((8, count), jnp.int32),
+        compiler_params=pltpu.CompilerParams(vmem_limit_bytes=2 * MIB),
+        name="find_slots",
+    )(row_adapter_index, adapter_storage_slot, after)
+
+
+def project_own(own, weight, down):
     count = own[0].shape[0] * 2
     half = own[0].shape[1]
     query_width = weight.shape[2]
-    block = count // len(offsets)
 
     def kernel(
-        place_ref,
-        adapters_ref,
-        storage_ref,
         low,
         high,
         weight_ref,
         down_ref,
         query_ref,
         rank_ref,
-        slots_ref,
     ):
         rows = jnp.concatenate([low[...], high[...]], axis=0)
-        here = pl.ds(pl.multiple_of(place_ref[1] * half, half), half)
+        here = pl.ds(pl.multiple_of(lax.axis_index("tensor") * half, half), half)
         rank_ref[...] = lax.dot_general(
             down_ref[:, here], rows, LAST, preferred_element_type=jnp.float32
         )
         query_ref[...] = jnp.dot(rows, weight_ref[0, here], preferred_element_type=jnp.float32)
-        column = lax.broadcasted_iota(jnp.int32, slots_ref.shape, 1)
-        slots = jnp.zeros(slots_ref.shape, jnp.int32)
-        for row in range(count):
-            source = (place_ref[0] ^ int(offsets[row // block])) * block + row % block
-            slots = jnp.where(column == row, storage_ref[adapters_ref[source]], slots)
-        slots_ref[...] = slots
-
-    return pl.pallas_call(
-        kernel,
-        in_specs=[SMEM] * 3 + [VMEM] * 4,
-        out_specs=[VMEM] * 3,
+
+    return pl.pallas_call(
+        kernel,
+        in_specs=[VMEM] * 4,
+        out_specs=[VMEM] * 2,
         out_shape=[
             jax.ShapeDtypeStruct((count, query_width), jnp.float32),
             jax.ShapeDtypeStruct((down.shape[0], count), jnp.float32),
-            jax.ShapeDtypeStruct((8, count), jnp.int32),
         ],
         compiler_params=pltpu.CompilerParams(vmem_limit_bytes=4 * MIB),
         cost_estimate=pl.CostEstimate(
@@ -172,10 +186,10 @@
             transcendentals=0,
         ),
         name="project_own",
-    )(place, row_adapter_index, adapter_storage_slot, *own, weight, down)
-
-
-def project_other(place, other, weight, down, query_mine, rank_mine, slots, owned, up):
+    )(*own, weight, down)
+
+
+def project_other(other, weight, down, query_mine, rank_mine, slots, owned, up):
     count = other[0].shape[0] * 2
     half = other[0].shape[1]
     query_width = weight.shape[2]
@@ -185,7 +199,6 @@
     chunk = 512
 
     def kernel(
-        place_ref,
         low,
         high,
         weight_ref,
@@ -196,14 +209,15 @@
         up_ref,
         *out_refs,
     ):
+        me = lax.axis_index("wide").astype(jnp.int32)
         rows = jnp.concatenate([low[...], high[...]], axis=0)
-        there = pl.ds(pl.multiple_of((1 - place_ref[1]) * half, half), half)
+        there = pl.ds(pl.multiple_of((1 - lax.axis_index("tensor")) * half, half), half)
         ranks = rank_ref[...] + lax.dot_general(
             down_ref[:, there], rows, LAST, preferred_element_type=jnp.float32
         )
         slot = slots_ref[:1]
         kept = [
-            jnp.where(slot == place_ref[0] * owned + number, ranks[at : at + rank], 0.0)
+            jnp.where(slot == me * owned + number, ranks[at : at + rank], 0.0)
             for number, at in enumerate(range(0, owned * rank, rank))
         ]
         terms = jnp.concatenate(kept, axis=0).T.astype(jnp.bfloat16)
@@ -218,7 +232,7 @@
             scaled = (ADAPTER_SCALE * delta.astype(jnp.float32)).astype(jnp.bfloat16)
             for number, out_ref in enumerate(out_refs):
                 out_ref[:, lane : lane + chunk] = scaled[number * part : (number + 1) * part]
-        here = pl.ds(pl.multiple_of(place_ref[0] * query_width, query_width), query_width)
+        here = pl.ds(pl.multiple_of(me * query_width, query_width), query_width)
         for number, out_ref in enumerate(out_refs):
             rows_base = base[number * part : (number + 1) * part]
             out_ref[:, here] = (rows_base + out_ref[:, here].astype(jnp.float32)).astype(
@@ -228,7 +242,7 @@
     shape = jax.ShapeDtypeStruct((part, width), jnp.bfloat16)
     return pl.pallas_call(
         kernel,
-        in_specs=[SMEM] + [VMEM] * 8,
+        in_specs=[VMEM] * 8,
         out_specs=[VMEM] * 4,
         out_shape=[shape] * 4,
         compiler_params=pltpu.CompilerParams(vmem_limit_bytes=4 * MIB),
@@ -238,7 +252,7 @@
             transcendentals=0,
         ),
         name="project_other",
-    )(place, *other, weight, down, query_mine, rank_mine, slots, up)
+    )(*other, weight, down, query_mine, rank_mine, slots, up)
 
 
 def project_out(low, high, weight, part):
@@ -262,24 +276,25 @@
     )(low, high, weight)
 
 
-def sum_halves(place, offsets, mine, theirs):
+def sum_halves(offsets, mine, theirs):
     block = 8
     count, width = mine.shape
 
-    def kernel(place_ref, mine_ref, theirs_ref, out_ref):
+    def kernel(mine_ref, theirs_ref, out_ref):
+        me = lax.axis_index("wide").astype(jnp.int32)
         for number, at in enumerate(range(0, count, block)):
             rows = (mine_ref[at : at + block] + theirs_ref[at : at + block]).astype(jnp.bfloat16)
             for side in range(2):
-                out_ref[(place_ref[0] ^ int(offsets[number])) * 2 + side] = rows
-
-    return pl.pallas_call(
-        kernel,
-        in_specs=[SMEM, VMEM, VMEM],
+                out_ref[(me ^ int(offsets[number])) * 2 + side] = rows
+
+    return pl.pallas_call(
+        kernel,
+        in_specs=[VMEM, VMEM],
         out_specs=VMEM,
         out_shape=jax.ShapeDtypeStruct((count // block * 2, block, width), jnp.bfloat16),
         compiler_params=pltpu.CompilerParams(vmem_limit_bytes=4 * MIB),
         name="sum_halves",
-    )(place, mine, theirs)
+    )(mine, theirs)
 
 
 def join_columns(pieces):
@@ -434,9 +449,7 @@
     half = model_width // 2
     offsets = np.array([far * 2 + near for near in range(2) for far in range(wide // 2)], np.int32)
 
-    me = lax.axis_index("wide").astype(jnp.int32)
     core = lax.axis_index("tensor").astype(jnp.int32)
-    place = jnp.stack([me, core])
 
     def swap(array, offset):
         return lax.ppermute(array, "wide", [(peer, peer ^ offset) for peer in range(wide)])
@@ -447,28 +460,28 @@
     far_offsets = range(2, wide, 2)
 
     block = lax.dynamic_slice(tokens, (0, core * half), (rows_dev, half))
-    block = begin_gather(place, block)
+    block = begin_gather(block)
     blocks = [block] + [swap(block, offset) for offset in far_offsets]
-    query_weight = dequantize_all(place, query_quant_codes, query_absmax_scale, False)
+    query_weight = dequantize_all(query_quant_codes, query_absmax_scale, False, block)
     blocks[1:] = [lax.optimization_barrier((part, query_weight))[0] for part in blocks[1:]]
     low = jnp.concatenate(blocks, axis=0)
-    high = jnp.concatenate([swap(part, 1) for part in blocks], axis=0)
+    nearby = [swap(part, 1) for part in blocks]
+    slots = find_slots(offsets, row_adapter_index, adapter_storage_slot, low)
+    nearby = [lax.optimization_barrier((part, slots))[0] for part in nearby]
+    high = jnp.concatenate(nearby, axis=0)
     own = (low, high)
     other = [cross(part) for part in own]
 
     owned, rank = adapter_down_maps.shape[1:]
     down = adapter_down_maps.transpose(1, 2, 0).reshape(owned * rank, model_width)
     up = adapter_up_maps.reshape(owned * rank, adapter_up_maps.shape[2])
-    query_mine, rank_mine, slots = project_own(
-        place, offsets, row_adapter_index, adapter_storage_slot, own, query_weight, down
-    )
+    query_mine, rank_mine = project_own(own, query_weight, down)
     stay_low, stay_high, leave_low, leave_high = project_other(
-        place, other, query_weight, down, query_mine, rank_mine, slots, owned, up
+        other, query_weight, down, query_mine, rank_mine, slots, owned, up
     )
 
     received_high, received_low = swap(leave_high, 1), swap(leave_low, 1)
-    place, _ = lax.optimization_barrier((place, leave_high))
-    output_weight = dequantize_all(place, output_quant_codes, output_absmax_scale, True)
+    output_weight = dequantize_all(output_quant_codes, output_absmax_scale, True, leave_high)
     received_high, _ = lax.optimization_barrier((received_high, output_weight))
     received_low, _ = lax.optimization_barrier((received_low, output_weight))
 
@@ -495,7 +508,7 @@
     high = jnp.concatenate([swap(part, 1) for part in arrived], axis=0)
     theirs = cross(project_out(low, high, output_weight, 0))
     mine = project_out(low, high, output_weight, 1)
-    routed = lax.all_to_all(sum_halves(place, offsets, mine, theirs), ("wide", "tensor"), 0, 0)
+    routed = lax.all_to_all(sum_halves(offsets, mine, theirs), ("wide", "tensor"), 0, 0)
     return join_columns(routed)
 
 

time: 69.9 us -> 66.8 us (0.956)
  Pallas kernels: 14.1 us -> 11.4 us
  blocking collectives: 12.4 us -> 11.1 us
  waiting for transfers between devices: 14.9 us -> 16 us
    pallas_call x6 -> x7, Pallas kernels: 11.7 us -> 9.08 us  [the longest x2 5.62 us: dequantize_all(): pl.pallas_call(kernel, in_specs=[VMEM, VMEM] + [ANY] * len(after), out_sp...]
    all_to_all x1, blocking collectives: 12.4 us -> 11.1 us  [fast(): lax.all_to_all(sum_halves(offsets, mine, theirs), ('wide', 'tensor'), 0, 0)]
    ppermute x19, waiting for transfers between devices: 14.4 us -> 15.3 us  [swap(): lax.ppermute(array, 'wide', [(peer, peer ^ offset) for peer in range(wide)])]
  transfers between devices with their start and end apart: 22 -> 22, of which waited for: 12 -> 14; matrix products, arithmetic and copies ran while one was open for 0% -> 0% of each run, Pallas kernels for 13% -> 13%
where the time goes in v5:
time: 66.8 us; the launch traced here: 66.6 us
  starting transfers between devices  25.2 us (38%)
  waiting for transfers between devices  16 us (24%)
  Pallas kernels  11.4 us (17%)
  blocking collectives  11.1 us (17%)
  local copies, waits for them, and re-layouts  1.12 us (2%)
  matrix products  0.95 us (1%)
    ppermute x19, starting transfers between devices, swap(): lax.ppermute(array, 'wide', [(peer, peer ^ offset) for peer in range(wide)])  25 us
    ppermute x19, waiting for transfers between devices, swap(): lax.ppermute(array, 'wide', [(peer, peer ^ offset) for peer in range(wide)])  15.3 us
    all_to_all x1, blocking collectives, fast(): lax.all_to_all(sum_halves(offsets, mine, theirs), ('wide', 'tensor'), 0, 0)  11.1 us
    pallas_call x2, Pallas kernels, dequantize_all(): pl.pallas_call(kernel, in_specs=[VMEM, VMEM] + [ANY] * len(after), out_sp...  5.62 us
    pallas_call x2, Pallas kernels, project_out(): pl.pallas_call(kernel, in_specs=[VMEM] * 3, out_specs=VMEM, out_shape=jax...  1.68 us
    pallas_call x1, Pallas kernels, project_other(): pl.pallas_call(kernel, in_specs=[VMEM] * 8, out_specs=[VMEM] * 4, out_sha...  1.56 us
  transfers between devices with their start and end apart: 22, of which 14 were waited for; matrix products, arithmetic and copies ran while one was open for 0% of the time, Pallas kernels for 13%

profile of v5, /device:TPU:0, one launch (start us, length us, event | category | flops | bytes accessed | tf_op | source)
XLA Modules:
  0.0 66.6 jit_solution(3061907640345294934)
XLA Ops:
  0.0 0.9 %constant_dynamic-slice_fusion.block_ref = bf16[8,4096]{1,0:T(8,128)(2,1)S(1)} fusion(bf16[8,8192]{1,0:T(8,128)(2,1)} %param.14, s32[]{:T(128)S(6)} %select_n.7), kind=kLoop, calls=%fused_computation.42 | loop fusion | bytes 131076 | tf_op jit(solution)/shard_map/dynamic_slice | solution.py:462
  0.9 0.0 copy-start.6
  0.9 0.0 copy-start.7
  0.9 0.0 copy-start.2
  1.0 3.1 %collective-permute-start = (bf16[8,4096]{1,0:T(8,128)(2,1)S(1)}, bf16[8,4096]{1,0:T(8,128)(2,1)S(1)}, u32[]{:S(2)}, u32[]{:S(2)}) collective-permute-start(bf16[8,4096]{1,0:T(8,128)(2,1)S(1)} %begin_gather.1.rest_0_), channel_id=1, source_target_pairs={{0,4},{2,6},{4,0},{6,2},{8,12},{10,14},{12,8},{14,10},{1,5},{3,7},... | collective-permute-start | bytes 196616 | tf_op jit(solution)/shard_map/ppermute | solution.py:455
  4.0 2.6 %collective-permute-start.1 = (bf16[8,4096]{1,0:T(8,128)(2,1)S(1)}, bf16[8,4096]{1,0:T(8,128)(2,1)S(1)}, u32[]{:S(2)}, u32[]{:S(2)}) collective-permute-start(bf16[8,4096]{1,0:T(8,128)(2,1)S(1)} %begin_gather.1.rest_0_), channel_id=1, source_target_pairs={{0,8},{2,10},{4,12},{6,14},{8,0},{10,2},{12,4},{14,6},{1,9},{3,11}... | collective-permute-start | bytes 196616 | tf_op jit(solution)/shard_map/ppermute | solution.py:455
  6.6 0.0 collective-permute-start.2
  6.6 1.7 %collective-permute-start.4 = (bf16[8,4096]{1,0:T(8,128)(2,1)S(1)}, bf16[8,4096]{1,0:T(8,128)(2,1)S(1)}, u32[]{:S(2)}, u32[]{:S(2)}) collective-permute-start(bf16[8,4096]{1,0:T(8,128)(2,1)S(1)} %begin_gather.1.rest_0_), channel_id=1, source_target_pairs={{0,2},{2,0},{4,6},{6,4},{8,10},{10,8},{12,14},{14,12},{1,3},{3,1},... | collective-permute-start | bytes 196616 | tf_op jit(solution)/shard_map/ppermute | solution.py:455
  8.4 2.7 %dequantize.2.weight_ref = bf16[1,8192,512]{2,1,0:T(8,128)(2,1)S(1)} custom-call(s32[8192,512]{1,0:T(8,128)S(1)} %copy-done.1, f32[128,512]{1,0:T(8,128)S(1)} %copy-done.4, bf16[8,4096]{1,0:T(8,128)(2,1)S(1)} %begin_gather.1.rest_0_), custom_call_target="tpu_custom_call" | custom-call | flops 8388608 | bytes 25165824 | tf_op jit(solution)/shard_map/dequantize/pallas_call | solution.py:97
  11.1 0.0 copy-start.3
  11.1 0.0 collective-permute-done
  11.1 0.2 collective-permute-done.1
  11.3 1.4 %collective-permute-done.2 = bf16[8,4096]{1,0:T(8,128)(2,1)S(1)} collective-permute-done((bf16[8,4096]{1,0:T(8,128)(2,1)S(1)}, bf16[8,4096]{1,0:T(8,128)(2,1)S(1)}, u32[]{:S(2)}, u32[]{:S(2)}) %collective-permute-start.2) | collective-permute-done | bytes 65568 | tf_op jit(solution)/shard_map/ppermute | solution.py:455
  12.7 1.5 %collective-permute-start.5 = (bf16[8,4096]{1,0:T(8,128)(2,1)S(1)}, bf16[8,4096]{1,0:T(8,128)(2,1)S(1)}, u32[]{:S(2)}, u32[]{:S(2)}) collective-permute-start(bf16[8,4096]{1,0:T(8,128)(2,1)S(1)} %collective-permute-done), channel_id=1, source_target_pairs={{0,2},{2,0},{4,6},{6,4},{8,10},{10,8},{12,14},{14,12},{1,3},{3,1},... | collective-permute-start | bytes 196616 | tf_op jit(solution)/shard_map/ppermute | solution.py:455
  14.2 0.5 collective-permute-start.6
  14.8 1.6 %collective-permute-start.7 = (bf16[8,4096]{1,0:T(8,128)(2,1)S(1)}, bf16[8,4096]{1,0:T(8,128)(2,1)S(1)}, u32[]{:S(2)}, u32[]{:S(2)}) collective-permute-start(bf16[8,4096]{1,0:T(8,128)(2,1)S(1)} %collective-permute-done.2), channel_id=1, source_target_pairs={{0,2},{2,0},{4,6},{6,4},{8,10},{10,8},{12,14},{14,12},{1,3},{3,1},... | collective-permute-start | bytes 196616 | tf_op jit(solution)/shard_map/ppermute | solution.py:455
  16.3 0.0 collective-permute-start.3
  16.3 0.6 find_slots.1.slots_ref
  17.0 0.0 slice-start.2
  17.0 0.0 collective-permute-done.4
  17.0 1.5 %collective-permute-done.6 = bf16[8,4096]{1,0:T(8,128)(2,1)S(1)} collective-permute-done((bf16[8,4096]{1,0:T(8,128)(2,1)S(1)}, bf16[8,4096]{1,0:T(8,128)(2,1)S(1)}, u32[]{:S(2)}, u32[]{:S(2)}) %collective-permute-start.6) | collective-permute-done | bytes 65568 | tf_op jit(solution)/shard_map/ppermute | solution.py:455
  18.5 0.7 %collective-permute-done.7 = bf16[8,4096]{1,0:T(8,128)(2,1)S(1)} collective-permute-done((bf16[8,4096]{1,0:T(8,128)(2,1)S(1)}, bf16[8,4096]{1,0:T(8,128)(2,1)S(1)}, u32[]{:S(2)}, u32[]{:S(2)}) %collective-permute-start.7) | collective-permute-done | bytes 65568 | tf_op jit(solution)/shard_map/ppermute | solution.py:455
  19.2 0.1 collective-permute-start.8
  19.3 1.3 %project_own.1 = (f32[64,512]{1,0:T(8,128)S(1)}, f32[192,64]{1,0:T(8,128)S(1)}) custom-call(bf16[32,4096]{1,0:T(8,128)(2,1)S(1)} %pad_maximum_fusion.after_ref.low, bf16[32,4096]{1,0:T(8,128)(2,1)S(1)} %constant_dynamic-update-slice_fusion.high, bf16[1,8192,512]{2,1,0:T(8,128)(2,1)S(1)} %dequantize.2.weight_ref, bf16[192,8192]{1,0:T(8,128)(2,1)S(1)} %bitcast.39), custom_call_target="tpu_custom_call" | custom-call | flops 369098752 | bytes 7340032 | tf_op jit(solution)/shard_map/project_own/pallas_call | solution.py:174
  20.5 0.0 copy-start.9
  20.6 0.0 copy-start.5
  20.6 0.0 collective-permute-done.3.low
  20.6 0.2 collective-permute-done.8.high
  20.8 1.6 %project_other.1 = (bf16[16,4096]{1,0:T(8,128)(2,1)S(1)}, bf16[16,4096]{1,0:T(8,128)(2,1)S(1)}, bf16[16,4096]{1,0:T(8,128)(2,1)S(1)}, bf16[16,4096]{1,0:T(8,128)(2,1)S(1)}) custom-call(bf16[32,4096]{1,0:T(8,128)(2,1)S(1)} %collective-permute-done.3.low, bf16[32,4096]{1,0:T(8,128)(2,1)S(1)} %collective-permute-done.8.high, ...), custom_call_target="tpu_custom_call" | custom-call | flops 469762048 | bytes 8388608 | tf_op jit(solution)/shard_map/project_other/pallas_call | solution.py:243
  22.4 1.5 %collective-permute-start.10 = (bf16[16,4096]{1,0:T(8,128)(2,1)S(1)}, bf16[16,4096]{1,0:T(8,128)(2,1)S(1)}, u32[]{:S(2)}, u32[]{:S(2)}) collective-permute-start(bf16[16,4096]{1,0:T(8,128)(2,1)S(1)} %get-tuple-element.31.rest_0_), channel_id=1, source_target_pairs={{0,2},{2,0},{4,6},{6,4},{8,10},{10,8},{12,14},{14,12},{1,3},{3,1},... | collective-permute-start | bytes 393224 | tf_op jit(solution)/shard_map/ppermute | solution.py:455
  23.9 0.0 copy-start.8
  23.9 0.7 %collective-permute-start.9 = (bf16[16,4096]{1,0:T(8,128)(2,1)S(1)}, bf16[16,4096]{1,0:T(8,128)(2,1)S(1)}, u32[]{:S(2)}, u32[]{:S(2)}) collective-permute-start(bf16[16,4096]{1,0:T(8,128)(2,1)S(1)} %get-tuple-element.30), channel_id=1, source_target_pairs={{0,2},{2,0},{4,6},{6,4},{8,10},{10,8},{12,14},{14,12},{1,3},{3,1},... | collective-permute-start | bytes 393224 | tf_op jit(solution)/shard_map/ppermute | solution.py:455
  24.6 2.9 %dequantize.3.weight_ref = bf16[2,4096,512]{2,1,0:T(8,128)(2,1)S(1)} custom-call(s32[4096,1024]{1,0:T(8,128)S(1)} %bitcast.38, f32[64,1024]{1,0:T(8,128)S(1)} %copy-done.5, bf16[16,4096]{1,0:T(8,128)(2,1)S(1)} %get-tuple-element.31.rest_0_), custom_call_target="tpu_custom_call" | custom-call | flops 8388608 | bytes 25165824 | tf_op jit(solution)/shard_map/dequantize/pallas_call | solution.py:97
  27.5 1.3 %collective-permute-done.10 = bf16[16,4096]{1,0:T(8,128)(2,1)S(1)} collective-permute-done((bf16[16,4096]{1,0:T(8,128)(2,1)S(1)}, bf16[16,4096]{1,0:T(8,128)(2,1)S(1)}, u32[]{:S(2)}, u32[]{:S(2)}) %collective-permute-start.10) | collective-permute-done | bytes 131104 | tf_op jit(solution)/shard_map/ppermute | solution.py:455
  28.8 1.6 %collective-permute-start.11 = (bf16[8,4096]{1,0:T(8,128)(2,1)S(1)}, bf16[8,4096]{1,0:T(8,128)(2,1)S(1)}, u32[]{:S(2)}, u32[]{:S(2)}) collective-permute-start(bf16[8,4096]{1,0:T(8,128)(2,1)S(1)} %get-tuple-element.35), channel_id=1, source_target_pairs={{0,8},{2,10},{4,12},{6,14},{8,0},{10,2},{12,4},{14,6},{1,9},{3,11}... | collective-permute-start | bytes 196616 | tf_op jit(solution)/shard_map/ppermute | solution.py:455
  30.5 1.3 %collective-permute-start.12 = (bf16[8,4096]{1,0:T(8,128)(2,1)S(1)}, bf16[8,4096]{1,0:T(8,128)(2,1)S(1)}, u32[]{:S(2)}, u32[]{:S(2)}) collective-permute-start(bf16[8,4096]{1,0:T(8,128)(2,1)S(1)} %get-tuple-element.36), channel_id=1, source_target_pairs={{0,12},{2,14},{4,8},{6,10},{8,4},{10,6},{12,0},{14,2},{1,13},{3,15... | collective-permute-start | bytes 196616 | tf_op jit(solution)/shard_map/ppermute | solution.py:455
  31.7 0.0 collective-permute-done.9
  31.8 0.7 %collective-permute-start.13 = (bf16[8,4096]{1,0:T(8,128)(2,1)S(1)}, bf16[8,4096]{1,0:T(8,128)(2,1)S(1)}, u32[]{:S(2)}, u32[]{:S(2)}) collective-permute-start(bf16[8,4096]{1,0:T(8,128)(2,1)S(1)} %slice.19), channel_id=1, source_target_pairs={{0,4},{2,6},{4,0},{6,2},{8,12},{10,14},{12,8},{14,10},{1,5},{3,7},... | collective-permute-start | bytes 196616 | tf_op jit(solution)/shard_map/ppermute | solution.py:455
  32.5 0.1 iota_compare_fusion
  32.6 2.9 %collective-permute-done.11 = bf16[8,4096]{1,0:T(8,128)(2,1)S(1)} collective-permute-done((bf16[8,4096]{1,0:T(8,128)(2,1)S(1)}, bf16[8,4096]{1,0:T(8,128)(2,1)S(1)}, u32[]{:S(2)}, u32[]{:S(2)}) %collective-permute-start.11) | collective-permute-done | bytes 65568 | tf_op jit(solution)/shard_map/ppermute | solution.py:455
  35.4 1.2 %collective-permute-done.12 = bf16[8,4096]{1,0:T(8,128)(2,1)S(1)} collective-permute-done((bf16[8,4096]{1,0:T(8,128)(2,1)S(1)}, bf16[8,4096]{1,0:T(8,128)(2,1)S(1)}, u32[]{:S(2)}, u32[]{:S(2)}) %collective-permute-start.12) | collective-permute-done | bytes 65568 | tf_op jit(solution)/shard_map/ppermute | solution.py:455
  36.7 0.2 collective-permute-done.13
  36.9 0.2 fusion.12
  37.0 0.5 fusion.19
  37.5 0.2 fusion.7
  37.8 0.3 fusion.2
  38.2 1.3 %collective-permute-start.17 = (bf16[8,4096]{1,0:T(8,128)(2,1)S(1)}, bf16[8,4096]{1,0:T(8,128)(2,1)S(1)}, u32[]{:S(2)}, u32[]{:S(2)}) collective-permute-start(bf16[8,4096]{1,0:T(8,128)(2,1)S(1)} %bitcast.46), channel_id=1, source_target_pairs={{0,2},{2,0},{4,6},{6,4},{8,10},{10,8},{12,14},{14,12},{1,3},{3,1},... | collective-permute-start | bytes 196616 | tf_op jit(solution)/shard_map/ppermute | solution.py:455
  39.5 0.1 collective-permute-start.14
  39.5 2.7 %collective-permute-start.15 = (bf16[8,4096]{1,0:T(8,128)(2,1)S(1)}, bf16[8,4096]{1,0:T(8,128)(2,1)S(1)}, u32[]{:S(2)}, u32[]{:S(2)}) collective-permute-start(bf16[8,4096]{1,0:T(8,128)(2,1)S(1)} %bitcast.48), channel_id=1, source_target_pairs={{0,8},{2,10},{4,12},{6,14},{8,0},{10,2},{12,4},{14,6},{1,9},{3,11}... | collective-permute-start | bytes 196616 | tf_op jit(solution)/shard_map/ppermute | solution.py:455
  42.2 1.6 %collective-permute-start.16 = (bf16[8,4096]{1,0:T(8,128)(2,1)S(1)}, bf16[8,4096]{1,0:T(8,128)(2,1)S(1)}, u32[]{:S(2)}, u32[]{:S(2)}) collective-permute-start(bf16[8,4096]{1,0:T(8,128)(2,1)S(1)} %bitcast.49), channel_id=1, source_target_pairs={{0,12},{2,14},{4,8},{6,10},{8,4},{10,6},{12,0},{14,2},{1,13},{3,15... | collective-permute-start | bytes 196616 | tf_op jit(solution)/shard_map/ppermute | solution.py:455
  43.9 0.9 %collective-permute-start.18 = (bf16[8,4096]{1,0:T(8,128)(2,1)S(1)}, bf16[8,4096]{1,0:T(8,128)(2,1)S(1)}, u32[]{:S(2)}, u32[]{:S(2)}) collective-permute-start(bf16[8,4096]{1,0:T(8,128)(2,1)S(1)} %collective-permute-done.14), channel_id=1, source_target_pairs={{0,2},{2,0},{4,6},{6,4},{8,10},{10,8},{12,14},{14,12},{1,3},{3,1},... | collective-permute-start | bytes 196616 | tf_op jit(solution)/shard_map/ppermute | solution.py:455
  44.8 1.5 %collective-permute-done.15 = bf16[8,4096]{1,0:T(8,128)(2,1)S(1)} collective-permute-done((bf16[8,4096]{1,0:T(8,128)(2,1)S(1)}, bf16[8,4096]{1,0:T(8,128)(2,1)S(1)}, u32[]{:S(2)}, u32[]{:S(2)}) %collective-permute-start.15) | collective-permute-done | bytes 65568 | tf_op jit(solution)/shard_map/ppermute | solution.py:455
  46.3 0.9 %collective-permute-start.19 = (bf16[8,4096]{1,0:T(8,128)(2,1)S(1)}, bf16[8,4096]{1,0:T(8,128)(2,1)S(1)}, u32[]{:S(2)}, u32[]{:S(2)}) collective-permute-start(bf16[8,4096]{1,0:T(8,128)(2,1)S(1)} %collective-permute-done.15), channel_id=1, source_target_pairs={{0,2},{2,0},{4,6},{6,4},{8,10},{10,8},{12,14},{14,12},{1,3},{3,1},... | collective-permute-start | bytes 196616 | tf_op jit(solution)/shard_map/ppermute | solution.py:455
  47.2 1.0 %collective-permute-done.16 = bf16[8,4096]{1,0:T(8,128)(2,1)S(1)} collective-permute-done((bf16[8,4096]{1,0:T(8,128)(2,1)S(1)}, bf16[8,4096]{1,0:T(8,128)(2,1)S(1)}, u32[]{:S(2)}, u32[]{:S(2)}) %collective-permute-start.16) | collective-permute-done | bytes 65568 | tf_op jit(solution)/shard_map/ppermute | solution.py:455
  48.3 0.8 %collective-permute-start.20 = (bf16[8,4096]{1,0:T(8,128)(2,1)S(1)}, bf16[8,4096]{1,0:T(8,128)(2,1)S(1)}, u32[]{:S(2)}, u32[]{:S(2)}) collective-permute-start(bf16[8,4096]{1,0:T(8,128)(2,1)S(1)} %collective-permute-done.16), channel_id=1, source_target_pairs={{0,2},{2,0},{4,6},{6,4},{8,10},{10,8},{12,14},{14,12},{1,3},{3,1},... | collective-permute-start | bytes 196616 | tf_op jit(solution)/shard_map/ppermute | solution.py:455
  49.1 0.0 collective-permute-done.18
  49.1 1.4 %collective-permute-done.19 = bf16[8,4096]{1,0:T(8,128)(2,1)S(1)} collective-permute-done((bf16[8,4096]{1,0:T(8,128)(2,1)S(1)}, bf16[8,4096]{1,0:T(8,128)(2,1)S(1)}, u32[]{:S(2)}, u32[]{:S(2)}) %collective-permute-start.19) | collective-permute-done | bytes 65568 | tf_op jit(solution)/shard_map/ppermute | solution.py:455
  50.6 2.0 %collective-permute-done.20 = bf16[8,4096]{1,0:T(8,128)(2,1)S(1)} collective-permute-done((bf16[8,4096]{1,0:T(8,128)(2,1)S(1)}, bf16[8,4096]{1,0:T(8,128)(2,1)S(1)}, u32[]{:S(2)}, u32[]{:S(2)}) %collective-permute-start.20) | collective-permute-done | bytes 65568 | tf_op jit(solution)/shard_map/ppermute | solution.py:455
  52.6 0.8 %project_out.3 = f32[64,512]{1,0:T(8,128)S(1)} custom-call(bf16[32,4096]{1,0:T(8,128)(2,1)S(1)} %constant_dynamic-update-slice_fusion.4.low_ref, bf16[32,4096]{1,0:T(8,128)(2,1)S(1)} %constant_dynamic-update-slice_fusion.8.high_ref, bf16[2,4096,512]{2,1,0:T(8,128)(2,1)S(1)} %dequantize.3.weight_ref), custom_call_target="tpu_custom_call" | custom-call | flops 268435456 | bytes 6291456 | tf_op jit(solution)/shard_map/project_out/pallas_call | solution.py:266
  53.4 0.1 collective-permute-start.21
  53.5 0.8 %project_out.2.mine_ref = f32[64,512]{1,0:T(8,128)S(1)} custom-call(bf16[32,4096]{1,0:T(8,128)(2,1)S(1)} %constant_dynamic-update-slice_fusion.4.low_ref, bf16[32,4096]{1,0:T(8,128)(2,1)S(1)} %constant_dynamic-update-slice_fusion.8.high_ref, bf16[2,4096,512]{2,1,0:T(8,128)(2,1)S(1)} %dequantize.3.weight_ref), custom_call_target="tpu_custom_call" | custom-call | flops 268435456 | bytes 6291456 | tf_op jit(solution)/shard_map/project_out/pallas_call | solution.py:266
  54.3 0.5 collective-permute-done.21.theirs_ref
  54.8 11.1 %all_to_all.5.pieces_ref = bf16[16,8,512]{2,1,0:T(8,128)(2,1)S(1)} all-to-all(bf16[16,8,512]{2,1,0:T(8,128)(2,1)S(1)} %sum_halves.1), channel_id=1, replica_groups=mesh['rep'=2,'wide'=8,'tensor'=2] {'wide','tensor'}, dimensions={0} | all-to-all | bytes 262144 | tf_op jit(solution)/shard_map/all_to_all | solution.py:511
  65.9 0.7 join_columns.1
  (53 shorter events, 0.4 us)
Async XLA Ops:
  0.0 37.8 %copy-start = (bf16[8,64,512]{2,1,0:T(8,128)(2,1)S(1)}, bf16[8,64,512]{2,1,0:T(8,128)(2,1)}, u32[]{:S(2)}) copy-start(bf16[8,64,512]{2,1,0:T(8,128)(2,1)} %param.25) | copy-start | bytes 1572868
  0.9 7.4 %copy-start.1 = (s32[8192,512]{1,0:T(8,128)S(1)}, s32[8192,512]{1,0:T(8,128)}, u32[]{:S(2)}) copy-start(s32[8192,512]{1,0:T(8,128)} %codes_ref.2) | copy-start | bytes 50331652
  0.9 7.4 %copy-start.4 = (f32[128,512]{1,0:T(8,128)S(1)}, f32[128,512]{1,0:T(8,128)}, u32[]{:S(2)}) copy-start(f32[128,512]{1,0:T(8,128)} %scales_ref.2) | copy-start | bytes 786436
  0.9 15.4 %copy-start.6 = (s32[64]{0:T(128)S(1)}, s32[64]{0:T(128)}, u32[]{:S(2)}) copy-start(s32[64]{0:T(128)} %adapters_ref.1) | copy-start | bytes 772
  0.9 15.4 %copy-start.7 = (s32[48]{0:T(128)S(1)}, s32[48]{0:T(128)}, u32[]{:S(2)}) copy-start(s32[48]{0:T(128)} %storage_ref.1) | copy-start | bytes 580
  0.9 18.3 %copy-start.2 = (bf16[8192,6,32]{0,2,1:T(8,128)(2,1)S(1)}, bf16[8192,6,32]{0,2,1:T(8,128)(2,1)}, u32[]{:S(2)}) copy-start(bf16[8192,6,32]{0,2,1:T(8,128)(2,1)} %param.19) | copy-start | bytes 9437188
  1.0 10.2 %collective-permute-start = (bf16[8,4096]{1,0:T(8,128)(2,1)S(1)}, bf16[8,4096]{1,0:T(8,128)(2,1)S(1)}, u32[]{:S(2)}, u32[]{:S(2)}) collective-permute-start(bf16[8,4096]{1,0:T(8,128)(2,1)S(1)} %begin_gather.1.rest_0_), channel_id=1, source_target_pairs={{0,4},{2,6},{4,0},{6,2},{8,12},{10,14},{12,8},{14,10},{1,5},{3,7},... | collective-permute-start | bytes 196616 | tf_op jit(solution)/shard_map/ppermute | solution.py:455
  4.0 7.3 %collective-permute-start.1 = (bf16[8,4096]{1,0:T(8,128)(2,1)S(1)}, bf16[8,4096]{1,0:T(8,128)(2,1)S(1)}, u32[]{:S(2)}, u32[]{:S(2)}) collective-permute-start(bf16[8,4096]{1,0:T(8,128)(2,1)S(1)} %begin_gather.1.rest_0_), channel_id=1, source_target_pairs={{0,8},{2,10},{4,12},{6,14},{8,0},{10,2},{12,4},{14,6},{1,9},{3,11}... | collective-permute-start | bytes 196616 | tf_op jit(solution)/shard_map/ppermute | solution.py:455
  6.6 6.1 %collective-permute-start.2 = (bf16[8,4096]{1,0:T(8,128)(2,1)S(1)}, bf16[8,4096]{1,0:T(8,128)(2,1)S(1)}, u32[]{:S(2)}, u32[]{:S(2)}) collective-permute-start(bf16[8,4096]{1,0:T(8,128)(2,1)S(1)} %begin_gather.1.rest_0_), channel_id=1, source_target_pairs={{0,12},{2,14},{4,8},{6,10},{8,4},{10,6},{12,0},{14,2},{1,13},{3,15... | collective-permute-start | bytes 196616 | tf_op jit(solution)/shard_map/ppermute | solution.py:455
  6.6 10.3 %collective-permute-start.4 = (bf16[8,4096]{1,0:T(8,128)(2,1)S(1)}, bf16[8,4096]{1,0:T(8,128)(2,1)S(1)}, u32[]{:S(2)}, u32[]{:S(2)}) collective-permute-start(bf16[8,4096]{1,0:T(8,128)(2,1)S(1)} %begin_gather.1.rest_0_), channel_id=1, source_target_pairs={{0,2},{2,0},{4,6},{6,4},{8,10},{10,8},{12,14},{14,12},{1,3},{3,1},... | collective-permute-start | bytes 196616 | tf_op jit(solution)/shard_map/ppermute | solution.py:455
  8.4 16.2 %slice-start = ((s8[16777216]{0:T(1024)(128)(4,1)}), s8[4194304]{0:T(1024)(128)(4,1)S(1)}, s32[]{:S(2)}) async-start(s8[16777216]{0:T(1024)(128)(4,1)} %bitcast.37), calls=%async_computation.1 | async-start | bytes 8388608
  8.4 16.2 %slice-start.1 = ((s8[16777216]{0:T(1024)(128)(4,1)}), s8[4194304]{0:T(1024)(128)(4,1)S(1)}, s32[]{:S(2)}) async-start(s8[16777216]{0:T(1024)(128)(4,1)} %bitcast.37), calls=%async_computation.2 | async-start | bytes 8388608
  11.1 9.7 %copy-start.3 = (bf16[6,32,4096]{2,1,0:T(8,128)(2,1)S(1)}, bf16[6,32,4096]{2,1,0:T(8,128)(2,1)}, u32[]{:S(2)}) copy-start(bf16[6,32,4096]{2,1,0:T(8,128)(2,1)} %param.20) | copy-start | bytes 4718596
  12.7 4.3 %collective-permute-start.5 = (bf16[8,4096]{1,0:T(8,128)(2,1)S(1)}, bf16[8,4096]{1,0:T(8,128)(2,1)S(1)}, u32[]{:S(2)}, u32[]{:S(2)}) collective-permute-start(bf16[8,4096]{1,0:T(8,128)(2,1)S(1)} %collective-permute-done), channel_id=1, source_target_pairs={{0,2},{2,0},{4,6},{6,4},{8,10},{10,8},{12,14},{14,12},{1,3},{3,1},... | collective-permute-start | bytes 196616 | tf_op jit(solution)/shard_map/ppermute | solution.py:455
  14.2 4.3 %collective-permute-start.6 = (bf16[8,4096]{1,0:T(8,128)(2,1)S(1)}, bf16[8,4096]{1,0:T(8,128)(2,1)S(1)}, u32[]{:S(2)}, u32[]{:S(2)}) collective-permute-start(bf16[8,4096]{1,0:T(8,128)(2,1)S(1)} %collective-permute-done.1), channel_id=1, source_target_pairs={{0,2},{2,0},{4,6},{6,4},{8,10},{10,8},{12,14},{14,12},{1,3},{3,1},... | collective-permute-start | bytes 196616 | tf_op jit(solution)/shard_map/ppermute | solution.py:455
  14.8 4.4 %collective-permute-start.7 = (bf16[8,4096]{1,0:T(8,128)(2,1)S(1)}, bf16[8,4096]{1,0:T(8,128)(2,1)S(1)}, u32[]{:S(2)}, u32[]{:S(2)}) collective-permute-start(bf16[8,4096]{1,0:T(8,128)(2,1)S(1)} %collective-permute-done.2), channel_id=1, source_target_pairs={{0,2},{2,0},{4,6},{6,4},{8,10},{10,8},{12,14},{14,12},{1,3},{3,1},... | collective-permute-start | bytes 196616 | tf_op jit(solution)/shard_map/ppermute | solution.py:455
  16.3 4.3 %collective-permute-start.3 = (bf16[32,4096]{1,0:T(8,128)(2,1)S(1)}, bf16[32,4096]{1,0:T(8,128)(2,1)S(1)}, u32[]{:S(2)}, u32[]{:S(2)}) collective-permute-start(bf16[32,4096]{1,0:T(8,128)(2,1)S(1)} %pad_maximum_fusion.after_ref.low), channel_id=1, source_target_pairs={{0,1},{1,0},{2,3},{3,2},{4,5},{5,4},{6,7},{7,6},{8,9},{9,8},{10,11... | collective-permute-start | bytes 786440 | tf_op jit(solution)/shard_map/ppermute | solution.py:458
  17.0 7.6 %slice-start.2 = ((s8[16777216]{0:T(1024)(128)(4,1)}), s8[4194304]{0:T(1024)(128)(4,1)S(1)}, s32[]{:S(2)}) async-start(s8[16777216]{0:T(1024)(128)(4,1)} %bitcast.37), calls=%async_computation.3 | async-start | bytes 8388608
  19.2 1.6 %collective-permute-start.8 = (bf16[32,4096]{1,0:T(8,128)(2,1)S(1)}, bf16[32,4096]{1,0:T(8,128)(2,1)S(1)}, u32[]{:S(2)}, u32[]{:S(2)}) collective-permute-start(bf16[32,4096]{1,0:T(8,128)(2,1)S(1)} %constant_dynamic-update-slice_fusion.high), channel_id=1, source_target_pairs={{0,1},{1,0},{2,3},{3,2},{4,5},{5,4},{6,7},{7,6},{8,9},{9,8},{10,11... | collective-permute-start | bytes 786440 | tf_op jit(solution)/shard_map/ppermute | solution.py:458
  20.5 3.3 %copy-start.9 = (bf16[8,512]{1,0:T(8,128)(2,1)S(1)}, bf16[8,512]{1,0:T(8,128)(2,1)}, u32[]{:S(2)}) copy-start(bf16[8,512]{1,0:T(8,128)(2,1)} %param.27) | copy-start | bytes 24580
  20.6 4.0 %copy-start.5 = (f32[64,1024]{1,0:T(8,128)S(1)}, f32[64,1024]{1,0:T(8,128)}, u32[]{:S(2)}) copy-start(f32[64,1024]{1,0:T(8,128)} %scales_ref.3) | copy-start | bytes 786436
  20.8 3.8 %slice-start.3 = ((s8[16777216]{0:T(1024)(128)(4,1)}), s8[4194304]{0:T(1024)(128)(4,1)S(1)}, s32[]{:S(2)}) async-start(s8[16777216]{0:T(1024)(128)(4,1)} %bitcast.37), calls=%async_computation.4 | async-start | bytes 8388608
  22.4 6.4 %collective-permute-start.10 = (bf16[16,4096]{1,0:T(8,128)(2,1)S(1)}, bf16[16,4096]{1,0:T(8,128)(2,1)S(1)}, u32[]{:S(2)}, u32[]{:S(2)}) collective-permute-start(bf16[16,4096]{1,0:T(8,128)(2,1)S(1)} %get-tuple-element.31.rest_0_), channel_id=1, source_target_pairs={{0,2},{2,0},{4,6},{6,4},{8,10},{10,8},{12,14},{14,12},{1,3},{3,1},... | collective-permute-start | bytes 393224 | tf_op jit(solution)/shard_map/ppermute | solution.py:455
  23.9 8.6 %copy-start.11 = (s32[8]{0:T(128)S(1)}, s32[8]{0:T(128)}, u32[]{:S(2)}) copy-start(s32[8]{0:T(128)} %param.23) | copy-start | bytes 100
  23.9 13.0 %copy-start.10 = (bf16[8,512]{1,0:T(8,128)(2,1)S(1)}, bf16[8,512]{1,0:T(8,128)(2,1)}, u32[]{:S(2)}) copy-start(bf16[8,512]{1,0:T(8,128)(2,1)} %param.26) | copy-start | bytes 24580
  23.9 13.2 %copy-start.8 = (bf16[8,64,512]{2,1,0:T(8,128)(2,1)S(1)}, bf16[8,64,512]{2,1,0:T(8,128)(2,1)}, u32[]{:S(2)}) copy-start(bf16[8,64,512]{2,1,0:T(8,128)(2,1)} %param.24) | copy-start | bytes 1572868
  23.9 7.9 %collective-permute-start.9 = (bf16[16,4096]{1,0:T(8,128)(2,1)S(1)}, bf16[16,4096]{1,0:T(8,128)(2,1)S(1)}, u32[]{:S(2)}, u32[]{:S(2)}) collective-permute-start(bf16[16,4096]{1,0:T(8,128)(2,1)S(1)} %get-tuple-element.30), channel_id=1, source_target_pairs={{0,2},{2,0},{4,6},{6,4},{8,10},{10,8},{12,14},{14,12},{1,3},{3,1},... | collective-permute-start | bytes 393224 | tf_op jit(solution)/shard_map/ppermute | solution.py:455
  28.8 6.6 %collective-permute-start.11 = (bf16[8,4096]{1,0:T(8,128)(2,1)S(1)}, bf16[8,4096]{1,0:T(8,128)(2,1)S(1)}, u32[]{:S(2)}, u32[]{:S(2)}) collective-permute-start(bf16[8,4096]{1,0:T(8,128)(2,1)S(1)} %get-tuple-element.35), channel_id=1, source_target_pairs={{0,8},{2,10},{4,12},{6,14},{8,0},{10,2},{12,4},{14,6},{1,9},{3,11}... | collective-permute-start | bytes 196616 | tf_op jit(solution)/shard_map/ppermute | solution.py:455
  30.5 6.2 %collective-permute-start.12 = (bf16[8,4096]{1,0:T(8,128)(2,1)S(1)}, bf16[8,4096]{1,0:T(8,128)(2,1)S(1)}, u32[]{:S(2)}, u32[]{:S(2)}) collective-permute-start(bf16[8,4096]{1,0:T(8,128)(2,1)S(1)} %get-tuple-element.36), channel_id=1, source_target_pairs={{0,12},{2,14},{4,8},{6,10},{8,4},{10,6},{12,0},{14,2},{1,13},{3,15... | collective-permute-start | bytes 196616 | tf_op jit(solution)/shard_map/ppermute | solution.py:455
  31.8 5.1 %collective-permute-start.13 = (bf16[8,4096]{1,0:T(8,128)(2,1)S(1)}, bf16[8,4096]{1,0:T(8,128)(2,1)S(1)}, u32[]{:S(2)}, u32[]{:S(2)}) collective-permute-start(bf16[8,4096]{1,0:T(8,128)(2,1)S(1)} %slice.19), channel_id=1, source_target_pairs={{0,4},{2,6},{4,0},{6,2},{8,12},{10,14},{12,8},{14,10},{1,5},{3,7},... | collective-permute-start | bytes 196616 | tf_op jit(solution)/shard_map/ppermute | solution.py:455
  38.2 5.7 %collective-permute-start.17 = (bf16[8,4096]{1,0:T(8,128)(2,1)S(1)}, bf16[8,4096]{1,0:T(8,128)(2,1)S(1)}, u32[]{:S(2)}, u32[]{:S(2)}) collective-permute-start(bf16[8,4096]{1,0:T(8,128)(2,1)S(1)} %bitcast.46), channel_id=1, source_target_pairs={{0,2},{2,0},{4,6},{6,4},{8,10},{10,8},{12,14},{14,12},{1,3},{3,1},... | collective-permute-start | bytes 196616 | tf_op jit(solution)/shard_map/ppermute | solution.py:455
  39.5 4.4 %collective-permute-start.14 = (bf16[8,4096]{1,0:T(8,128)(2,1)S(1)}, bf16[8,4096]{1,0:T(8,128)(2,1)S(1)}, u32[]{:S(2)}, u32[]{:S(2)}) collective-permute-start(bf16[8,4096]{1,0:T(8,128)(2,1)S(1)} %bitcast.47), channel_id=1, source_target_pairs={{0,4},{2,6},{4,0},{6,2},{8,12},{10,14},{12,8},{14,10},{1,5},{3,7},... | collective-permute-start | bytes 196616 | tf_op jit(solution)/shard_map/ppermute | solution.py:455
  39.5 6.8 %collective-permute-start.15 = (bf16[8,4096]{1,0:T(8,128)(2,1)S(1)}, bf16[8,4096]{1,0:T(8,128)(2,1)S(1)}, u32[]{:S(2)}, u32[]{:S(2)}) collective-permute-start(bf16[8,4096]{1,0:T(8,128)(2,1)S(1)} %bitcast.48), channel_id=1, source_target_pairs={{0,8},{2,10},{4,12},{6,14},{8,0},{10,2},{12,4},{14,6},{1,9},{3,11}... | collective-permute-start | bytes 196616 | tf_op jit(solution)/shard_map/ppermute | solution.py:455
  42.2 6.1 %collective-permute-start.16 = (bf16[8,4096]{1,0:T(8,128)(2,1)S(1)}, bf16[8,4096]{1,0:T(8,128)(2,1)S(1)}, u32[]{:S(2)}, u32[]{:S(2)}) collective-permute-start(bf16[8,4096]{1,0:T(8,128)(2,1)S(1)} %bitcast.49), channel_id=1, source_target_pairs={{0,12},{2,14},{4,8},{6,10},{8,4},{10,6},{12,0},{14,2},{1,13},{3,15... | collective-permute-start | bytes 196616 | tf_op jit(solution)/shard_map/ppermute | solution.py:455
  43.9 5.2 %collective-permute-start.18 = (bf16[8,4096]{1,0:T(8,128)(2,1)S(1)}, bf16[8,4096]{1,0:T(8,128)(2,1)S(1)}, u32[]{:S(2)}, u32[]{:S(2)}) collective-permute-start(bf16[8,4096]{1,0:T(8,128)(2,1)S(1)} %collective-permute-done.14), channel_id=1, source_target_pairs={{0,2},{2,0},{4,6},{6,4},{8,10},{10,8},{12,14},{14,12},{1,3},{3,1},... | collective-permute-start | bytes 196616 | tf_op jit(solution)/shard_map/ppermute | solution.py:455
  46.3 4.3 %collective-permute-start.19 = (bf16[8,4096]{1,0:T(8,128)(2,1)S(1)}, bf16[8,4096]{1,0:T(8,128)(2,1)S(1)}, u32[]{:S(2)}, u32[]{:S(2)}) collective-permute-start(bf16[8,4096]{1,0:T(8,128)(2,1)S(1)} %collective-permute-done.15), channel_id=1, source_target_pairs={{0,2},{2,0},{4,6},{6,4},{8,10},{10,8},{12,14},{14,12},{1,3},{3,1},... | collective-permute-start | bytes 196616 | tf_op jit(solution)/shard_map/ppermute | solution.py:455
  48.3 4.3 %collective-permute-start.20 = (bf16[8,4096]{1,0:T(8,128)(2,1)S(1)}, bf16[8,4096]{1,0:T(8,128)(2,1)S(1)}, u32[]{:S(2)}, u32[]{:S(2)}) collective-permute-start(bf16[8,4096]{1,0:T(8,128)(2,1)S(1)} %collective-permute-done.16), channel_id=1, source_target_pairs={{0,2},{2,0},{4,6},{6,4},{8,10},{10,8},{12,14},{14,12},{1,3},{3,1},... | collective-permute-start | bytes 196616 | tf_op jit(solution)/shard_map/ppermute | solution.py:455
  53.4 1.4 %collective-permute-start.21 = (f32[64,512]{1,0:T(8,128)S(1)}, f32[64,512]{1,0:T(8,128)S(1)}, u32[]{:S(2)}, u32[]{:S(2)}) collective-permute-start(f32[64,512]{1,0:T(8,128)S(1)} %project_out.3), channel_id=1, source_target_pairs={{0,1},{1,0},{2,3},{3,2},{4,5},{5,4},{6,7},{7,6},{8,9},{9,8},{10,11... | collective-permute-start | bytes 393224 | tf_op jit(solution)/shard_map/ppermute | solution.py:458

commit v6 on v5

--- a/solution.py
+++ b/solution.py
@@ -481,7 +481,14 @@
     )
 
     received_high, received_low = swap(leave_high, 1), swap(leave_low, 1)
-    output_weight = dequantize_all(output_quant_codes, output_absmax_scale, True, leave_high)
+    output_weight = dequantize_all(
+        output_quant_codes,
+        output_absmax_scale,
+        True,
+        leave_high,
+        stored_key_cache,
+        stored_value_cache,
+    )
     received_high, _ = lax.optimization_barrier((received_high, output_weight))
     received_low, _ = lax.optimization_barrier((received_low, output_weight))
 

time: 66.8 us -> 66.8 us (level)
    unnamed x42 -> x44, local copies, waits for them, and re-layouts: 0.18 us -> 1.09 us
    dynamic_slice x1, local copies, waits for them, and re-layouts: 0.9 us -> 0.01 us  [fast(): block = lax.dynamic_slice(tokens, (0, core * half), (rows_dev, half))]
where the time goes in v6:
time: 66.8 us; the launch traced here: 66.6 us
  starting transfers between devices  25.2 us (38%)
  waiting for transfers between devices  15.9 us (24%)
  Pallas kernels  11.4 us (17%)
  blocking collectives  11.1 us (17%)
  local copies, waits for them, and re-layouts  1.13 us (2%)
  matrix products  0.95 us (1%)
    ppermute x19, starting transfers between devices, swap(): lax.ppermute(array, 'wide', [(peer, peer ^ offset) for peer in range(wide)])  25 us
    ppermute x19, waiting for transfers between devices, swap(): lax.ppermute(array, 'wide', [(peer, peer ^ offset) for peer in range(wide)])  15.3 us
    all_to_all x1, blocking collectives, fast(): lax.all_to_all(sum_halves(offsets, mine, theirs), ('wide', 'tensor'), 0, 0)  11.1 us
    pallas_call x2, Pallas kernels, dequantize_all(): pl.pallas_call(kernel, in_specs=[VMEM, VMEM] + [ANY] * len(after), out_sp...  5.62 us
    pallas_call x2, Pallas kernels, project_out(): pl.pallas_call(kernel, in_specs=[VMEM] * 3, out_specs=VMEM, out_shape=jax...  1.68 us
    pallas_call x1, Pallas kernels, project_other(): pl.pallas_call(kernel, in_specs=[VMEM] * 8, out_specs=[VMEM] * 4, out_sha...  1.56 us
  transfers between devices with their start and end apart: 22, of which 14 were waited for; matrix products, arithmetic and copies ran while one was open for 0% of the time, Pallas kernels for 13%

profile of v6, /device:TPU:0, one launch (start us, length us, event | category | flops | bytes accessed | tf_op | source)
XLA Modules:
  0.0 66.6 jit_solution(12146966598624301298)
XLA Ops:
  0.0 0.9 %copy-done = bf16[8,8192]{1,0:T(8,128)(2,1)S(1)} copy-done((bf16[8,8192]{1,0:T(8,128)(2,1)S(1)}, bf16[8,8192]{1,0:T(8,128)(2,1)}, u32[]{:S(2)}) %copy-start) | copy-done | bytes 131096
  0.9 0.0 copy-start.8
  0.9 0.0 copy-start.9
  1.0 0.0 copy-start.2
  1.0 3.1 %collective-permute-start = (bf16[8,4096]{1,0:T(8,128)(2,1)S(1)}, bf16[8,4096]{1,0:T(8,128)(2,1)S(1)}, u32[]{:S(2)}, u32[]{:S(2)}) collective-permute-start(bf16[8,4096]{1,0:T(8,128)(2,1)S(1)} %begin_gather.1.rest_0_), channel_id=1, source_target_pairs={{0,4},{2,6},{4,0},{6,2},{8,12},{10,14},{12,8},{14,10},{1,5},{3,7},... | collective-permute-start | bytes 196616 | tf_op jit(solution)/shard_map/ppermute | solution.py:455
  4.1 2.6 %collective-permute-start.1 = (bf16[8,4096]{1,0:T(8,128)(2,1)S(1)}, bf16[8,4096]{1,0:T(8,128)(2,1)S(1)}, u32[]{:S(2)}, u32[]{:S(2)}) collective-permute-start(bf16[8,4096]{1,0:T(8,128)(2,1)S(1)} %begin_gather.1.rest_0_), channel_id=1, source_target_pairs={{0,8},{2,10},{4,12},{6,14},{8,0},{10,2},{12,4},{14,6},{1,9},{3,11}... | collective-permute-start | bytes 196616 | tf_op jit(solution)/shard_map/ppermute | solution.py:455
  6.6 0.0 collective-permute-start.2
  6.6 1.7 %collective-permute-start.4 = (bf16[8,4096]{1,0:T(8,128)(2,1)S(1)}, bf16[8,4096]{1,0:T(8,128)(2,1)S(1)}, u32[]{:S(2)}, u32[]{:S(2)}) collective-permute-start(bf16[8,4096]{1,0:T(8,128)(2,1)S(1)} %begin_gather.1.rest_0_), channel_id=1, source_target_pairs={{0,2},{2,0},{4,6},{6,4},{8,10},{10,8},{12,14},{14,12},{1,3},{3,1},... | collective-permute-start | bytes 196616 | tf_op jit(solution)/shard_map/ppermute | solution.py:455
  8.4 2.7 %dequantize.2.weight_ref = bf16[1,8192,512]{2,1,0:T(8,128)(2,1)S(1)} custom-call(s32[8192,512]{1,0:T(8,128)S(1)} %copy-done.1, f32[128,512]{1,0:T(8,128)S(1)} %copy-done.6, bf16[8,4096]{1,0:T(8,128)(2,1)S(1)} %begin_gather.1.rest_0_), custom_call_target="tpu_custom_call" | custom-call | flops 8388608 | bytes 25165824 | tf_op jit(solution)/shard_map/dequantize/pallas_call | solution.py:97
  11.1 0.0 copy-start.4
  11.1 0.0 collective-permute-done
  11.2 0.2 collective-permute-done.1
  11.3 1.4 %collective-permute-done.2 = bf16[8,4096]{1,0:T(8,128)(2,1)S(1)} collective-permute-done((bf16[8,4096]{1,0:T(8,128)(2,1)S(1)}, bf16[8,4096]{1,0:T(8,128)(2,1)S(1)}, u32[]{:S(2)}, u32[]{:S(2)}) %collective-permute-start.2) | collective-permute-done | bytes 65568 | tf_op jit(solution)/shard_map/ppermute | solution.py:455
  12.7 1.5 %collective-permute-start.5 = (bf16[8,4096]{1,0:T(8,128)(2,1)S(1)}, bf16[8,4096]{1,0:T(8,128)(2,1)S(1)}, u32[]{:S(2)}, u32[]{:S(2)}) collective-permute-start(bf16[8,4096]{1,0:T(8,128)(2,1)S(1)} %collective-permute-done), channel_id=1, source_target_pairs={{0,2},{2,0},{4,6},{6,4},{8,10},{10,8},{12,14},{14,12},{1,3},{3,1},... | collective-permute-start | bytes 196616 | tf_op jit(solution)/shard_map/ppermute | solution.py:455
  14.2 0.5 collective-permute-start.6
  14.8 1.6 %collective-permute-start.7 = (bf16[8,4096]{1,0:T(8,128)(2,1)S(1)}, bf16[8,4096]{1,0:T(8,128)(2,1)S(1)}, u32[]{:S(2)}, u32[]{:S(2)}) collective-permute-start(bf16[8,4096]{1,0:T(8,128)(2,1)S(1)} %collective-permute-done.2), channel_id=1, source_target_pairs={{0,2},{2,0},{4,6},{6,4},{8,10},{10,8},{12,14},{14,12},{1,3},{3,1},... | collective-permute-start | bytes 196616 | tf_op jit(solution)/shard_map/ppermute | solution.py:455
  16.3 0.0 collective-permute-start.3
  16.3 0.6 find_slots.1.slots_ref
  17.0 0.0 slice-start.2
  17.0 1.5 %collective-permute-done.6 = bf16[8,4096]{1,0:T(8,128)(2,1)S(1)} collective-permute-done((bf16[8,4096]{1,0:T(8,128)(2,1)S(1)}, bf16[8,4096]{1,0:T(8,128)(2,1)S(1)}, u32[]{:S(2)}, u32[]{:S(2)}) %collective-permute-start.6) | collective-permute-done | bytes 65568 | tf_op jit(solution)/shard_map/ppermute | solution.py:455
  18.5 0.7 %collective-permute-done.7 = bf16[8,4096]{1,0:T(8,128)(2,1)S(1)} collective-permute-done((bf16[8,4096]{1,0:T(8,128)(2,1)S(1)}, bf16[8,4096]{1,0:T(8,128)(2,1)S(1)}, u32[]{:S(2)}, u32[]{:S(2)}) %collective-permute-start.7) | collective-permute-done | bytes 65568 | tf_op jit(solution)/shard_map/ppermute | solution.py:455
  19.2 0.1 collective-permute-start.8
  19.3 1.3 %project_own.1 = (f32[64,512]{1,0:T(8,128)S(1)}, f32[192,64]{1,0:T(8,128)S(1)}) custom-call(bf16[32,4096]{1,0:T(8,128)(2,1)S(1)} %pad_maximum_fusion.after_ref.low, bf16[32,4096]{1,0:T(8,128)(2,1)S(1)} %constant_dynamic-update-slice_fusion.high, bf16[1,8192,512]{2,1,0:T(8,128)(2,1)S(1)} %dequantize.2.weight_ref, bf16[192,8192]{1,0:T(8,128)(2,1)S(1)} %bitcast.39), custom_call_target="tpu_custom_call" | custom-call | flops 369098752 | bytes 7340032 | tf_op jit(solution)/shard_map/project_own/pallas_call | solution.py:174
  20.6 0.0 copy-start.10
  20.6 0.0 copy-start.3
  20.6 0.0 copy-start.5
  20.6 0.0 copy-start.7
  20.6 0.0 collective-permute-done.3.low
  20.6 0.2 collective-permute-done.8.high
  20.8 1.6 %project_other.1 = (bf16[16,4096]{1,0:T(8,128)(2,1)S(1)}, bf16[16,4096]{1,0:T(8,128)(2,1)S(1)}, bf16[16,4096]{1,0:T(8,128)(2,1)S(1)}, bf16[16,4096]{1,0:T(8,128)(2,1)S(1)}) custom-call(bf16[32,4096]{1,0:T(8,128)(2,1)S(1)} %collective-permute-done.3.low, bf16[32,4096]{1,0:T(8,128)(2,1)S(1)} %collective-permute-done.8.high, ...), custom_call_target="tpu_custom_call" | custom-call | flops 469762048 | bytes 8388608 | tf_op jit(solution)/shard_map/project_other/pallas_call | solution.py:243
  22.4 1.5 %collective-permute-start.10 = (bf16[16,4096]{1,0:T(8,128)(2,1)S(1)}, bf16[16,4096]{1,0:T(8,128)(2,1)S(1)}, u32[]{:S(2)}, u32[]{:S(2)}) collective-permute-start(bf16[16,4096]{1,0:T(8,128)(2,1)S(1)} %get-tuple-element.31.rest_0_), channel_id=1, source_target_pairs={{0,2},{2,0},{4,6},{6,4},{8,10},{10,8},{12,14},{14,12},{1,3},{3,1},... | collective-permute-start | bytes 393224 | tf_op jit(solution)/shard_map/ppermute | solution.py:455
  23.9 0.7 %collective-permute-start.9 = (bf16[16,4096]{1,0:T(8,128)(2,1)S(1)}, bf16[16,4096]{1,0:T(8,128)(2,1)S(1)}, u32[]{:S(2)}, u32[]{:S(2)}) collective-permute-start(bf16[16,4096]{1,0:T(8,128)(2,1)S(1)} %get-tuple-element.30), channel_id=1, source_target_pairs={{0,2},{2,0},{4,6},{6,4},{8,10},{10,8},{12,14},{14,12},{1,3},{3,1},... | collective-permute-start | bytes 393224 | tf_op jit(solution)/shard_map/ppermute | solution.py:455
  24.6 2.9 %dequantize.3.weight_ref = bf16[2,4096,512]{2,1,0:T(8,128)(2,1)S(1)} custom-call(s32[4096,1024]{1,0:T(8,128)S(1)} %bitcast.38, f32[64,1024]{1,0:T(8,128)S(1)} %copy-done.7, bf16[16,4096]{1,0:T(8,128)(2,1)S(1)} %get-tuple-element.31.rest_0_, bf16[8,64,512]{2,1,0:T(8,128)(2,1)S(1)} %copy-done.3, bf16[8,64,512]{2,1,0:T(8,128)(2,1)S(1)} %copy-done.5), custom_call_target="tpu_custom_call" | custom-call | flops 8388608 | bytes 25165824 | tf_op jit(solution)/shard_map/dequantize/pallas_call | solution.py:97
  27.5 1.3 %collective-permute-done.10 = bf16[16,4096]{1,0:T(8,128)(2,1)S(1)} collective-permute-done((bf16[16,4096]{1,0:T(8,128)(2,1)S(1)}, bf16[16,4096]{1,0:T(8,128)(2,1)S(1)}, u32[]{:S(2)}, u32[]{:S(2)}) %collective-permute-start.10) | collective-permute-done | bytes 131104 | tf_op jit(solution)/shard_map/ppermute | solution.py:455
  28.8 1.7 %collective-permute-start.11 = (bf16[8,4096]{1,0:T(8,128)(2,1)S(1)}, bf16[8,4096]{1,0:T(8,128)(2,1)S(1)}, u32[]{:S(2)}, u32[]{:S(2)}) collective-permute-start(bf16[8,4096]{1,0:T(8,128)(2,1)S(1)} %get-tuple-element.35), channel_id=1, source_target_pairs={{0,8},{2,10},{4,12},{6,14},{8,0},{10,2},{12,4},{14,6},{1,9},{3,11}... | collective-permute-start | bytes 196616 | tf_op jit(solution)/shard_map/ppermute | solution.py:455
  30.5 1.3 %collective-permute-start.12 = (bf16[8,4096]{1,0:T(8,128)(2,1)S(1)}, bf16[8,4096]{1,0:T(8,128)(2,1)S(1)}, u32[]{:S(2)}, u32[]{:S(2)}) collective-permute-start(bf16[8,4096]{1,0:T(8,128)(2,1)S(1)} %get-tuple-element.36), channel_id=1, source_target_pairs={{0,12},{2,14},{4,8},{6,10},{8,4},{10,6},{12,0},{14,2},{1,13},{3,15... | collective-permute-start | bytes 196616 | tf_op jit(solution)/shard_map/ppermute | solution.py:455
  31.7 0.0 collective-permute-done.9
  31.8 0.7 %collective-permute-start.13 = (bf16[8,4096]{1,0:T(8,128)(2,1)S(1)}, bf16[8,4096]{1,0:T(8,128)(2,1)S(1)}, u32[]{:S(2)}, u32[]{:S(2)}) collective-permute-start(bf16[8,4096]{1,0:T(8,128)(2,1)S(1)} %slice.19), channel_id=1, source_target_pairs={{0,4},{2,6},{4,0},{6,2},{8,12},{10,14},{12,8},{14,10},{1,5},{3,7},... | collective-permute-start | bytes 196616 | tf_op jit(solution)/shard_map/ppermute | solution.py:455
  32.5 0.1 iota_compare_fusion
  32.6 2.9 %collective-permute-done.11 = bf16[8,4096]{1,0:T(8,128)(2,1)S(1)} collective-permute-done((bf16[8,4096]{1,0:T(8,128)(2,1)S(1)}, bf16[8,4096]{1,0:T(8,128)(2,1)S(1)}, u32[]{:S(2)}, u32[]{:S(2)}) %collective-permute-start.11) | collective-permute-done | bytes 65568 | tf_op jit(solution)/shard_map/ppermute | solution.py:455
  35.5 1.2 %collective-permute-done.12 = bf16[8,4096]{1,0:T(8,128)(2,1)S(1)} collective-permute-done((bf16[8,4096]{1,0:T(8,128)(2,1)S(1)}, bf16[8,4096]{1,0:T(8,128)(2,1)S(1)}, u32[]{:S(2)}, u32[]{:S(2)}) %collective-permute-start.12) | collective-permute-done | bytes 65568 | tf_op jit(solution)/shard_map/ppermute | solution.py:455
  36.7 0.2 collective-permute-done.13
  36.9 0.5 fusion.19
  37.4 0.2 fusion.12
  37.6 0.2 fusion.7
  37.8 0.3 fusion.2
  38.2 1.3 %collective-permute-start.17 = (bf16[8,4096]{1,0:T(8,128)(2,1)S(1)}, bf16[8,4096]{1,0:T(8,128)(2,1)S(1)}, u32[]{:S(2)}, u32[]{:S(2)}) collective-permute-start(bf16[8,4096]{1,0:T(8,128)(2,1)S(1)} %bitcast.46), channel_id=1, source_target_pairs={{0,2},{2,0},{4,6},{6,4},{8,10},{10,8},{12,14},{14,12},{1,3},{3,1},... | collective-permute-start | bytes 196616 | tf_op jit(solution)/shard_map/ppermute | solution.py:455
  39.5 0.0 collective-permute-start.14
  39.5 2.7 %collective-permute-start.15 = (bf16[8,4096]{1,0:T(8,128)(2,1)S(1)}, bf16[8,4096]{1,0:T(8,128)(2,1)S(1)}, u32[]{:S(2)}, u32[]{:S(2)}) collective-permute-start(bf16[8,4096]{1,0:T(8,128)(2,1)S(1)} %bitcast.48), channel_id=1, source_target_pairs={{0,8},{2,10},{4,12},{6,14},{8,0},{10,2},{12,4},{14,6},{1,9},{3,11}... | collective-permute-start | bytes 196616 | tf_op jit(solution)/shard_map/ppermute | solution.py:455
  42.2 1.7 %collective-permute-start.16 = (bf16[8,4096]{1,0:T(8,128)(2,1)S(1)}, bf16[8,4096]{1,0:T(8,128)(2,1)S(1)}, u32[]{:S(2)}, u32[]{:S(2)}) collective-permute-start(bf16[8,4096]{1,0:T(8,128)(2,1)S(1)} %bitcast.49), channel_id=1, source_target_pairs={{0,12},{2,14},{4,8},{6,10},{8,4},{10,6},{12,0},{14,2},{1,13},{3,15... | collective-permute-start | bytes 196616 | tf_op jit(solution)/shard_map/ppermute | solution.py:455
  43.9 0.9 %collective-permute-start.18 = (bf16[8,4096]{1,0:T(8,128)(2,1)S(1)}, bf16[8,4096]{1,0:T(8,128)(2,1)S(1)}, u32[]{:S(2)}, u32[]{:S(2)}) collective-permute-start(bf16[8,4096]{1,0:T(8,128)(2,1)S(1)} %collective-permute-done.14), channel_id=1, source_target_pairs={{0,2},{2,0},{4,6},{6,4},{8,10},{10,8},{12,14},{14,12},{1,3},{3,1},... | collective-permute-start | bytes 196616 | tf_op jit(solution)/shard_map/ppermute | solution.py:455
  44.8 1.5 %collective-permute-done.15 = bf16[8,4096]{1,0:T(8,128)(2,1)S(1)} collective-permute-done((bf16[8,4096]{1,0:T(8,128)(2,1)S(1)}, bf16[8,4096]{1,0:T(8,128)(2,1)S(1)}, u32[]{:S(2)}, u32[]{:S(2)}) %collective-permute-start.15) | collective-permute-done | bytes 65568 | tf_op jit(solution)/shard_map/ppermute | solution.py:455
  46.3 0.9 %collective-permute-start.19 = (bf16[8,4096]{1,0:T(8,128)(2,1)S(1)}, bf16[8,4096]{1,0:T(8,128)(2,1)S(1)}, u32[]{:S(2)}, u32[]{:S(2)}) collective-permute-start(bf16[8,4096]{1,0:T(8,128)(2,1)S(1)} %collective-permute-done.15), channel_id=1, source_target_pairs={{0,2},{2,0},{4,6},{6,4},{8,10},{10,8},{12,14},{14,12},{1,3},{3,1},... | collective-permute-start | bytes 196616 | tf_op jit(solution)/shard_map/ppermute | solution.py:455
  47.3 1.0 %collective-permute-done.16 = bf16[8,4096]{1,0:T(8,128)(2,1)S(1)} collective-permute-done((bf16[8,4096]{1,0:T(8,128)(2,1)S(1)}, bf16[8,4096]{1,0:T(8,128)(2,1)S(1)}, u32[]{:S(2)}, u32[]{:S(2)}) %collective-permute-start.16) | collective-permute-done | bytes 65568 | tf_op jit(solution)/shard_map/ppermute | solution.py:455
  48.3 0.8 %collective-permute-start.20 = (bf16[8,4096]{1,0:T(8,128)(2,1)S(1)}, bf16[8,4096]{1,0:T(8,128)(2,1)S(1)}, u32[]{:S(2)}, u32[]{:S(2)}) collective-permute-start(bf16[8,4096]{1,0:T(8,128)(2,1)S(1)} %collective-permute-done.16), channel_id=1, source_target_pairs={{0,2},{2,0},{4,6},{6,4},{8,10},{10,8},{12,14},{14,12},{1,3},{3,1},... | collective-permute-start | bytes 196616 | tf_op jit(solution)/shard_map/ppermute | solution.py:455
  49.1 0.0 collective-permute-done.18
  49.1 1.5 %collective-permute-done.19 = bf16[8,4096]{1,0:T(8,128)(2,1)S(1)} collective-permute-done((bf16[8,4096]{1,0:T(8,128)(2,1)S(1)}, bf16[8,4096]{1,0:T(8,128)(2,1)S(1)}, u32[]{:S(2)}, u32[]{:S(2)}) %collective-permute-start.19) | collective-permute-done | bytes 65568 | tf_op jit(solution)/shard_map/ppermute | solution.py:455
  50.6 1.9 %collective-permute-done.20 = bf16[8,4096]{1,0:T(8,128)(2,1)S(1)} collective-permute-done((bf16[8,4096]{1,0:T(8,128)(2,1)S(1)}, bf16[8,4096]{1,0:T(8,128)(2,1)S(1)}, u32[]{:S(2)}, u32[]{:S(2)}) %collective-permute-start.20) | collective-permute-done | bytes 65568 | tf_op jit(solution)/shard_map/ppermute | solution.py:455
  52.5 0.8 %project_out.3 = f32[64,512]{1,0:T(8,128)S(1)} custom-call(bf16[32,4096]{1,0:T(8,128)(2,1)S(1)} %constant_dynamic-update-slice_fusion.4.low_ref, bf16[32,4096]{1,0:T(8,128)(2,1)S(1)} %constant_dynamic-update-slice_fusion.8.high_ref, bf16[2,4096,512]{2,1,0:T(8,128)(2,1)S(1)} %dequantize.3.weight_ref), custom_call_target="tpu_custom_call" | custom-call | flops 268435456 | bytes 6291456 | tf_op jit(solution)/shard_map/project_out/pallas_call | solution.py:266
  53.4 0.1 collective-permute-start.21
  53.5 0.8 %project_out.2.mine_ref = f32[64,512]{1,0:T(8,128)S(1)} custom-call(bf16[32,4096]{1,0:T(8,128)(2,1)S(1)} %constant_dynamic-update-slice_fusion.4.low_ref, bf16[32,4096]{1,0:T(8,128)(2,1)S(1)} %constant_dynamic-update-slice_fusion.8.high_ref, bf16[2,4096,512]{2,1,0:T(8,128)(2,1)S(1)} %dequantize.3.weight_ref), custom_call_target="tpu_custom_call" | custom-call | flops 268435456 | bytes 6291456 | tf_op jit(solution)/shard_map/project_out/pallas_call | solution.py:266
  54.3 0.5 collective-permute-done.21.theirs_ref
  54.8 11.1 %all_to_all.5.pieces_ref = bf16[16,8,512]{2,1,0:T(8,128)(2,1)S(1)} all-to-all(bf16[16,8,512]{2,1,0:T(8,128)(2,1)S(1)} %sum_halves.1), channel_id=1, replica_groups=mesh['rep'=2,'wide'=8,'tensor'=2] {'wide','tensor'}, dimensions={0} | all-to-all | bytes 262144 | tf_op jit(solution)/shard_map/all_to_all | solution.py:518
  66.0 0.7 join_columns.1
  (55 shorter events, 0.4 us)
Async XLA Ops:
  0.0 0.9 %copy-start = (bf16[8,8192]{1,0:T(8,128)(2,1)S(1)}, bf16[8,8192]{1,0:T(8,128)(2,1)}, u32[]{:S(2)}) copy-start(bf16[8,8192]{1,0:T(8,128)(2,1)} %param.14) | copy-start | bytes 393220
  0.9 7.5 %copy-start.1 = (s32[8192,512]{1,0:T(8,128)S(1)}, s32[8192,512]{1,0:T(8,128)}, u32[]{:S(2)}) copy-start(s32[8192,512]{1,0:T(8,128)} %codes_ref.2) | copy-start | bytes 50331652
  0.9 7.5 %copy-start.6 = (f32[128,512]{1,0:T(8,128)S(1)}, f32[128,512]{1,0:T(8,128)}, u32[]{:S(2)}) copy-start(f32[128,512]{1,0:T(8,128)} %scales_ref.2) | copy-start | bytes 786436
  0.9 15.4 %copy-start.8 = (s32[64]{0:T(128)S(1)}, s32[64]{0:T(128)}, u32[]{:S(2)}) copy-start(s32[64]{0:T(128)} %adapters_ref.1) | copy-start | bytes 772
  0.9 15.4 %copy-start.9 = (s32[48]{0:T(128)S(1)}, s32[48]{0:T(128)}, u32[]{:S(2)}) copy-start(s32[48]{0:T(128)} %storage_ref.1) | copy-start | bytes 580
  1.0 18.3 %copy-start.2 = (bf16[8192,6,32]{0,2,1:T(8,128)(2,1)S(1)}, bf16[8192,6,32]{0,2,1:T(8,128)(2,1)}, u32[]{:S(2)}) copy-start(bf16[8192,6,32]{0,2,1:T(8,128)(2,1)} %param.19) | copy-start | bytes 9437188
  1.0 10.2 %collective-permute-start = (bf16[8,4096]{1,0:T(8,128)(2,1)S(1)}, bf16[8,4096]{1,0:T(8,128)(2,1)S(1)}, u32[]{:S(2)}, u32[]{:S(2)}) collective-permute-start(bf16[8,4096]{1,0:T(8,128)(2,1)S(1)} %begin_gather.1.rest_0_), channel_id=1, source_target_pairs={{0,4},{2,6},{4,0},{6,2},{8,12},{10,14},{12,8},{14,10},{1,5},{3,7},... | collective-permute-start | bytes 196616 | tf_op jit(solution)/shard_map/ppermute | solution.py:455
  4.1 7.3 %collective-permute-start.1 = (bf16[8,4096]{1,0:T(8,128)(2,1)S(1)}, bf16[8,4096]{1,0:T(8,128)(2,1)S(1)}, u32[]{:S(2)}, u32[]{:S(2)}) collective-permute-start(bf16[8,4096]{1,0:T(8,128)(2,1)S(1)} %begin_gather.1.rest_0_), channel_id=1, source_target_pairs={{0,8},{2,10},{4,12},{6,14},{8,0},{10,2},{12,4},{14,6},{1,9},{3,11}... | collective-permute-start | bytes 196616 | tf_op jit(solution)/shard_map/ppermute | solution.py:455
  6.6 6.1 %collective-permute-start.2 = (bf16[8,4096]{1,0:T(8,128)(2,1)S(1)}, bf16[8,4096]{1,0:T(8,128)(2,1)S(1)}, u32[]{:S(2)}, u32[]{:S(2)}) collective-permute-start(bf16[8,4096]{1,0:T(8,128)(2,1)S(1)} %begin_gather.1.rest_0_), channel_id=1, source_target_pairs={{0,12},{2,14},{4,8},{6,10},{8,4},{10,6},{12,0},{14,2},{1,13},{3,15... | collective-permute-start | bytes 196616 | tf_op jit(solution)/shard_map/ppermute | solution.py:455
  6.6 10.3 %collective-permute-start.4 = (bf16[8,4096]{1,0:T(8,128)(2,1)S(1)}, bf16[8,4096]{1,0:T(8,128)(2,1)S(1)}, u32[]{:S(2)}, u32[]{:S(2)}) collective-permute-start(bf16[8,4096]{1,0:T(8,128)(2,1)S(1)} %begin_gather.1.rest_0_), channel_id=1, source_target_pairs={{0,2},{2,0},{4,6},{6,4},{8,10},{10,8},{12,14},{14,12},{1,3},{3,1},... | collective-permute-start | bytes 196616 | tf_op jit(solution)/shard_map/ppermute | solution.py:455
  8.4 16.2 %slice-start = ((s8[16777216]{0:T(1024)(128)(4,1)}), s8[4194304]{0:T(1024)(128)(4,1)S(1)}, s32[]{:S(2)}) async-start(s8[16777216]{0:T(1024)(128)(4,1)} %bitcast.37), calls=%async_computation.1 | async-start | bytes 8388608
  8.4 16.2 %slice-start.1 = ((s8[16777216]{0:T(1024)(128)(4,1)}), s8[4194304]{0:T(1024)(128)(4,1)S(1)}, s32[]{:S(2)}) async-start(s8[16777216]{0:T(1024)(128)(4,1)} %bitcast.37), calls=%async_computation.2 | async-start | bytes 8388608
  11.1 9.7 %copy-start.4 = (bf16[6,32,4096]{2,1,0:T(8,128)(2,1)S(1)}, bf16[6,32,4096]{2,1,0:T(8,128)(2,1)}, u32[]{:S(2)}) copy-start(bf16[6,32,4096]{2,1,0:T(8,128)(2,1)} %param.20) | copy-start | bytes 4718596
  12.7 4.3 %collective-permute-start.5 = (bf16[8,4096]{1,0:T(8,128)(2,1)S(1)}, bf16[8,4096]{1,0:T(8,128)(2,1)S(1)}, u32[]{:S(2)}, u32[]{:S(2)}) collective-permute-start(bf16[8,4096]{1,0:T(8,128)(2,1)S(1)} %collective-permute-done), channel_id=1, source_target_pairs={{0,2},{2,0},{4,6},{6,4},{8,10},{10,8},{12,14},{14,12},{1,3},{3,1},... | collective-permute-start | bytes 196616 | tf_op jit(solution)/shard_map/ppermute | solution.py:455
  14.2 4.3 %collective-permute-start.6 = (bf16[8,4096]{1,0:T(8,128)(2,1)S(1)}, bf16[8,4096]{1,0:T(8,128)(2,1)S(1)}, u32[]{:S(2)}, u32[]{:S(2)}) collective-permute-start(bf16[8,4096]{1,0:T(8,128)(2,1)S(1)} %collective-permute-done.1), channel_id=1, source_target_pairs={{0,2},{2,0},{4,6},{6,4},{8,10},{10,8},{12,14},{14,12},{1,3},{3,1},... | collective-permute-start | bytes 196616 | tf_op jit(solution)/shard_map/ppermute | solution.py:455
  14.8 4.4 %collective-permute-start.7 = (bf16[8,4096]{1,0:T(8,128)(2,1)S(1)}, bf16[8,4096]{1,0:T(8,128)(2,1)S(1)}, u32[]{:S(2)}, u32[]{:S(2)}) collective-permute-start(bf16[8,4096]{1,0:T(8,128)(2,1)S(1)} %collective-permute-done.2), channel_id=1, source_target_pairs={{0,2},{2,0},{4,6},{6,4},{8,10},{10,8},{12,14},{14,12},{1,3},{3,1},... | collective-permute-start | bytes 196616 | tf_op jit(solution)/shard_map/ppermute | solution.py:455
  16.3 4.3 %collective-permute-start.3 = (bf16[32,4096]{1,0:T(8,128)(2,1)S(1)}, bf16[32,4096]{1,0:T(8,128)(2,1)S(1)}, u32[]{:S(2)}, u32[]{:S(2)}) collective-permute-start(bf16[32,4096]{1,0:T(8,128)(2,1)S(1)} %pad_maximum_fusion.after_ref.low), channel_id=1, source_target_pairs={{0,1},{1,0},{2,3},{3,2},{4,5},{5,4},{6,7},{7,6},{8,9},{9,8},{10,11... | collective-permute-start | bytes 786440 | tf_op jit(solution)/shard_map/ppermute | solution.py:458
  17.0 7.6 %slice-start.2 = ((s8[16777216]{0:T(1024)(128)(4,1)}), s8[4194304]{0:T(1024)(128)(4,1)S(1)}, s32[]{:S(2)}) async-start(s8[16777216]{0:T(1024)(128)(4,1)} %bitcast.37), calls=%async_computation.3 | async-start | bytes 8388608
  19.2 1.6 %collective-permute-start.8 = (bf16[32,4096]{1,0:T(8,128)(2,1)S(1)}, bf16[32,4096]{1,0:T(8,128)(2,1)S(1)}, u32[]{:S(2)}, u32[]{:S(2)}) collective-permute-start(bf16[32,4096]{1,0:T(8,128)(2,1)S(1)} %constant_dynamic-update-slice_fusion.high), channel_id=1, source_target_pairs={{0,1},{1,0},{2,3},{3,2},{4,5},{5,4},{6,7},{7,6},{8,9},{9,8},{10,11... | collective-permute-start | bytes 786440 | tf_op jit(solution)/shard_map/ppermute | solution.py:458
  20.6 3.3 %copy-start.10 = (bf16[8,512]{1,0:T(8,128)(2,1)S(1)}, bf16[8,512]{1,0:T(8,128)(2,1)}, u32[]{:S(2)}) copy-start(bf16[8,512]{1,0:T(8,128)(2,1)} %param.27) | copy-start | bytes 24580
  20.6 4.0 %copy-start.3 = (bf16[8,64,512]{2,1,0:T(8,128)(2,1)S(1)}, bf16[8,64,512]{2,1,0:T(8,128)(2,1)}, u32[]{:S(2)}) copy-start(bf16[8,64,512]{2,1,0:T(8,128)(2,1)} %rest_1_.1) | copy-start | bytes 1572868
  20.6 4.0 %copy-start.5 = (bf16[8,64,512]{2,1,0:T(8,128)(2,1)S(1)}, bf16[8,64,512]{2,1,0:T(8,128)(2,1)}, u32[]{:S(2)}) copy-start(bf16[8,64,512]{2,1,0:T(8,128)(2,1)} %rest_2_.1) | copy-start | bytes 1572868
  20.6 4.0 %copy-start.7 = (f32[64,1024]{1,0:T(8,128)S(1)}, f32[64,1024]{1,0:T(8,128)}, u32[]{:S(2)}) copy-start(f32[64,1024]{1,0:T(8,128)} %scales_ref.3) | copy-start | bytes 786436
  20.8 3.8 %slice-start.3 = ((s8[16777216]{0:T(1024)(128)(4,1)}), s8[4194304]{0:T(1024)(128)(4,1)S(1)}, s32[]{:S(2)}) async-start(s8[16777216]{0:T(1024)(128)(4,1)} %bitcast.37), calls=%async_computation.4 | async-start | bytes 8388608
  22.4 6.4 %collective-permute-start.10 = (bf16[16,4096]{1,0:T(8,128)(2,1)S(1)}, bf16[16,4096]{1,0:T(8,128)(2,1)S(1)}, u32[]{:S(2)}, u32[]{:S(2)}) collective-permute-start(bf16[16,4096]{1,0:T(8,128)(2,1)S(1)} %get-tuple-element.31.rest_0_), channel_id=1, source_target_pairs={{0,2},{2,0},{4,6},{6,4},{8,10},{10,8},{12,14},{14,12},{1,3},{3,1},... | collective-permute-start | bytes 393224 | tf_op jit(solution)/shard_map/ppermute | solution.py:455
  23.9 8.6 %copy-start.12 = (s32[8]{0:T(128)S(1)}, s32[8]{0:T(128)}, u32[]{:S(2)}) copy-start(s32[8]{0:T(128)} %param.23) | copy-start | bytes 100
  23.9 13.5 %copy-start.11 = (bf16[8,512]{1,0:T(8,128)(2,1)S(1)}, bf16[8,512]{1,0:T(8,128)(2,1)}, u32[]{:S(2)}) copy-start(bf16[8,512]{1,0:T(8,128)(2,1)} %param.26) | copy-start | bytes 24580
  23.9 7.9 %collective-permute-start.9 = (bf16[16,4096]{1,0:T(8,128)(2,1)S(1)}, bf16[16,4096]{1,0:T(8,128)(2,1)S(1)}, u32[]{:S(2)}, u32[]{:S(2)}) collective-permute-start(bf16[16,4096]{1,0:T(8,128)(2,1)S(1)} %get-tuple-element.30), channel_id=1, source_target_pairs={{0,2},{2,0},{4,6},{6,4},{8,10},{10,8},{12,14},{14,12},{1,3},{3,1},... | collective-permute-start | bytes 393224 | tf_op jit(solution)/shard_map/ppermute | solution.py:455
  28.8 6.7 %collective-permute-start.11 = (bf16[8,4096]{1,0:T(8,128)(2,1)S(1)}, bf16[8,4096]{1,0:T(8,128)(2,1)S(1)}, u32[]{:S(2)}, u32[]{:S(2)}) collective-permute-start(bf16[8,4096]{1,0:T(8,128)(2,1)S(1)} %get-tuple-element.35), channel_id=1, source_target_pairs={{0,8},{2,10},{4,12},{6,14},{8,0},{10,2},{12,4},{14,6},{1,9},{3,11}... | collective-permute-start | bytes 196616 | tf_op jit(solution)/shard_map/ppermute | solution.py:455
  30.5 6.2 %collective-permute-start.12 = (bf16[8,4096]{1,0:T(8,128)(2,1)S(1)}, bf16[8,4096]{1,0:T(8,128)(2,1)S(1)}, u32[]{:S(2)}, u32[]{:S(2)}) collective-permute-start(bf16[8,4096]{1,0:T(8,128)(2,1)S(1)} %get-tuple-element.36), channel_id=1, source_target_pairs={{0,12},{2,14},{4,8},{6,10},{8,4},{10,6},{12,0},{14,2},{1,13},{3,15... | collective-permute-start | bytes 196616 | tf_op jit(solution)/shard_map/ppermute | solution.py:455
  31.8 5.1 %collective-permute-start.13 = (bf16[8,4096]{1,0:T(8,128)(2,1)S(1)}, bf16[8,4096]{1,0:T(8,128)(2,1)S(1)}, u32[]{:S(2)}, u32[]{:S(2)}) collective-permute-start(bf16[8,4096]{1,0:T(8,128)(2,1)S(1)} %slice.19), channel_id=1, source_target_pairs={{0,4},{2,6},{4,0},{6,2},{8,12},{10,14},{12,8},{14,10},{1,5},{3,7},... | collective-permute-start | bytes 196616 | tf_op jit(solution)/shard_map/ppermute | solution.py:455
  38.2 5.7 %collective-permute-start.17 = (bf16[8,4096]{1,0:T(8,128)(2,1)S(1)}, bf16[8,4096]{1,0:T(8,128)(2,1)S(1)}, u32[]{:S(2)}, u32[]{:S(2)}) collective-permute-start(bf16[8,4096]{1,0:T(8,128)(2,1)S(1)} %bitcast.46), channel_id=1, source_target_pairs={{0,2},{2,0},{4,6},{6,4},{8,10},{10,8},{12,14},{14,12},{1,3},{3,1},... | collective-permute-start | bytes 196616 | tf_op jit(solution)/shard_map/ppermute | solution.py:455
  39.5 4.4 %collective-permute-start.14 = (bf16[8,4096]{1,0:T(8,128)(2,1)S(1)}, bf16[8,4096]{1,0:T(8,128)(2,1)S(1)}, u32[]{:S(2)}, u32[]{:S(2)}) collective-permute-start(bf16[8,4096]{1,0:T(8,128)(2,1)S(1)} %bitcast.47), channel_id=1, source_target_pairs={{0,4},{2,6},{4,0},{6,2},{8,12},{10,14},{12,8},{14,10},{1,5},{3,7},... | collective-permute-start | bytes 196616 | tf_op jit(solution)/shard_map/ppermute | solution.py:455
  39.5 6.8 %collective-permute-start.15 = (bf16[8,4096]{1,0:T(8,128)(2,1)S(1)}, bf16[8,4096]{1,0:T(8,128)(2,1)S(1)}, u32[]{:S(2)}, u32[]{:S(2)}) collective-permute-start(bf16[8,4096]{1,0:T(8,128)(2,1)S(1)} %bitcast.48), channel_id=1, source_target_pairs={{0,8},{2,10},{4,12},{6,14},{8,0},{10,2},{12,4},{14,6},{1,9},{3,11}... | collective-permute-start | bytes 196616 | tf_op jit(solution)/shard_map/ppermute | solution.py:455
  42.2 6.1 %collective-permute-start.16 = (bf16[8,4096]{1,0:T(8,128)(2,1)S(1)}, bf16[8,4096]{1,0:T(8,128)(2,1)S(1)}, u32[]{:S(2)}, u32[]{:S(2)}) collective-permute-start(bf16[8,4096]{1,0:T(8,128)(2,1)S(1)} %bitcast.49), channel_id=1, source_target_pairs={{0,12},{2,14},{4,8},{6,10},{8,4},{10,6},{12,0},{14,2},{1,13},{3,15... | collective-permute-start | bytes 196616 | tf_op jit(solution)/shard_map/ppermute | solution.py:455
  43.9 5.2 %collective-permute-start.18 = (bf16[8,4096]{1,0:T(8,128)(2,1)S(1)}, bf16[8,4096]{1,0:T(8,128)(2,1)S(1)}, u32[]{:S(2)}, u32[]{:S(2)}) collective-permute-start(bf16[8,4096]{1,0:T(8,128)(2,1)S(1)} %collective-permute-done.14), channel_id=1, source_target_pairs={{0,2},{2,0},{4,6},{6,4},{8,10},{10,8},{12,14},{14,12},{1,3},{3,1},... | collective-permute-start | bytes 196616 | tf_op jit(solution)/shard_map/ppermute | solution.py:455
  46.3 4.3 %collective-permute-start.19 = (bf16[8,4096]{1,0:T(8,128)(2,1)S(1)}, bf16[8,4096]{1,0:T(8,128)(2,1)S(1)}, u32[]{:S(2)}, u32[]{:S(2)}) collective-permute-start(bf16[8,4096]{1,0:T(8,128)(2,1)S(1)} %collective-permute-done.15), channel_id=1, source_target_pairs={{0,2},{2,0},{4,6},{6,4},{8,10},{10,8},{12,14},{14,12},{1,3},{3,1},... | collective-permute-start | bytes 196616 | tf_op jit(solution)/shard_map/ppermute | solution.py:455
  48.3 4.3 %collective-permute-start.20 = (bf16[8,4096]{1,0:T(8,128)(2,1)S(1)}, bf16[8,4096]{1,0:T(8,128)(2,1)S(1)}, u32[]{:S(2)}, u32[]{:S(2)}) collective-permute-start(bf16[8,4096]{1,0:T(8,128)(2,1)S(1)} %collective-permute-done.16), channel_id=1, source_target_pairs={{0,2},{2,0},{4,6},{6,4},{8,10},{10,8},{12,14},{14,12},{1,3},{3,1},... | collective-permute-start | bytes 196616 | tf_op jit(solution)/shard_map/ppermute | solution.py:455
  53.4 1.4 %collective-permute-start.21 = (f32[64,512]{1,0:T(8,128)S(1)}, f32[64,512]{1,0:T(8,128)S(1)}, u32[]{:S(2)}, u32[]{:S(2)}) collective-permute-start(f32[64,512]{1,0:T(8,128)S(1)} %project_out.3), channel_id=1, source_target_pairs={{0,1},{1,0},{2,3},{3,2},{4,5},{5,4},{6,7},{7,6},{8,9},{9,8},{10,11... | collective-permute-start | bytes 393224 | tf_op jit(solution)/shard_map/ppermute | solution.py:458
